TPU v7x, 32 devices: a whole 2x2x4 slice. The times are simulated.
32 devices in a mesh: lon: 4 (over y, x), lat: 8 (over z, core).
Axes of the slice: x: 2, y: 2, z: 4, core: 2. Of those that a mesh axis runs over, the one named last changes fastest.
Arguments:
- tracer: float32 [16, 512, 5760], P(None, 'lat', 'lon'), may hold values from -6 to 6
- zonal_wind: float32 [16, 512, 5760], P(None, 'lat', 'lon'), may hold values from -1 to 1
- meridional_wind: float32 [16, 512, 5760], P(None, 'lat', 'lon'), may hold values from -1 to 1
- cutoff_wave: int32 [512], P('lat'), may hold values from 1 to 127, as said below
- polar_mask: int32 [512], P('lat'), may hold values from 0 to 1, as said below
Outputs:
- advanced: float32 [16, 512, 5760], P(None, 'lat', 'lon')
Inputs may be any that keep to these rules, and one draw needn't show every extreme that they name: `polar_mask`: the rows with value 1 form one contiguous cap at each end of the latitude rows, each cap 512 // 6 rows or somewhat more. `cutoff_wave`: the value is 1 on the first and the last latitude row.
All inputs are finite; a program needn't handle non-finite values.
Results may differ from a plain program's by a relative error of at most 0.0001.
Values sent between devices are 32-bit elements; how exact they have to be, the bound alone decides.
No kernel may reach another device: no remote copies, remote signals or barrier semaphores. Data moves between devices by JAX's collectives and lax.ppermute only.
A program may use at most 192 MiB of HBM per device.

v0:
```python
import functools

import jax
import jax.numpy as jnp
import ml_dtypes
import numpy as np
from jax import lax
from jax.experimental import pallas as pl
from jax.experimental.pallas import tpu as pltpu
from jax.sharding import PartitionSpec as P

KMAX = 128
HALF = KMAX // 2
DIFFUSION = 0.1
GROUP = 4
SUB = 8
VMEM_MIB = 48
LIMITS = (48, 68, 92, 128)
F32 = jnp.float32
BF16 = jnp.bfloat16
MIB = 1024 * 1024


def wide(cells):
    return -(-(cells + 2) // 128) * 128


def split_np(values):
    high = values.astype(ml_dtypes.bfloat16)
    low = (values - high.astype(np.float64)).astype(ml_dtypes.bfloat16)
    return high, low


@functools.lru_cache(maxsize=None)
def wave_tables(cells, ways):
    total = cells * ways
    width = wide(cells)
    lane = np.arange(width)
    start = np.arange(ways)[:, None] * cells
    place = np.where(lane == width - 1, -1, lane)[None, :] + start
    used = (lane <= cells) | (lane == width - 1)
    column = np.arange(2 * KMAX)
    wave = column // KMAX * HALF + column % HALF
    sine = column % KMAX // HALF
    angle = (place[:, :, None] * wave[None, None, :] % total) * (2.0 * np.pi / total)
    table = np.where(sine == 1, np.sin(angle), np.cos(angle))
    project = split_np(np.where(used[None, :, None], table, 0.0))
    inside = np.where((lane < cells)[None, :, None], table, 0.0).transpose(0, 2, 1)
    rebuild = split_np(inside)
    return np.concatenate(project, axis=2), np.concatenate(rebuild, axis=1)


def split(x):
    high = x.astype(BF16)
    return high, (x - high.astype(F32)).astype(BF16)


def project(x, table):
    high, low = split(x)
    both = jnp.dot(high, table, preferred_element_type=F32)
    cross = jnp.dot(low, table[:, : 2 * KMAX], preferred_element_type=F32)
    return both[:, : 2 * KMAX] + both[:, 2 * KMAX :] + cross


def rebuild(coefficients, table):
    high, low = split(coefficients)
    both = jnp.dot(jnp.concatenate([high, high], axis=1), table, preferred_element_type=F32)
    return both + jnp.dot(low, table[: 2 * KMAX], preferred_element_type=F32)


def padded(x, width):
    return jnp.concatenate([x, jnp.zeros((x.shape[0], width - x.shape[1]), F32)], axis=1)


def along_lon(s, u):
    width = s.shape[1]
    spread = DIFFUSION * s
    carry = (0.5 * u) * s
    return (
        (1.0 - 4.0 * DIFFUSION) * s
        + pltpu.roll(spread - carry, width - 1, 1)
        + pltpu.roll(spread + carry, 1, 1)
    )


def moved_rows(s, u, v):
    rows = s.shape[0]
    spread = DIFFUSION * s
    carry = (0.5 * v) * s
    row = lax.broadcasted_iota(jnp.int32, s.shape, 0)
    from_next = jnp.where(row == rows - 1, 0.0, pltpu.roll(spread - carry, rows - 1, 0))
    from_last = jnp.where(row == 0, 0.0, pltpu.roll(spread + carry, 1, 0))
    return along_lon(s, u) + from_next + from_last


def put_halves(ref, at, value):
    for half in range(2):
        ref[half, at, :] = value[:, half * KMAX : (half + 1) * KMAX]


def both_halves(ref, at):
    return jnp.concatenate([ref[0, at, :], ref[1, at, :]], axis=1)


def southward(s, v):
    return DIFFUSION * s + (0.5 * v) * s


def northward(s, v):
    return DIFFUSION * s - (0.5 * v) * s


def filtered_column(cut_row_ref):
    rows = cut_row_ref.shape[1]
    shape_ = (rows, rows)
    diagonal = lax.broadcasted_iota(jnp.int32, shape_, 0) == lax.broadcasted_iota(jnp.int32, shape_, 1)
    spread = jnp.broadcast_to(cut_row_ref[...].astype(F32), shape_)
    return jnp.sum(jnp.where(diagonal, spread, 0.0), axis=1, keepdims=True) >= 0.0


def edge_kernel(
    info_ref, cutoff_ref, mask_ref, s0_ref, u0_ref, v0_ref, s1_ref, u1_ref, v1_ref, ring0_ref, ring1_ref, own_ref,
):
    levels, width = own_ref.shape[1:]
    rows = cutoff_ref.shape[0]
    near = info_ref[0] < info_ref[1] // 2
    last = s1_ref.shape[1] - 1
    sides = []
    for refs, at, beyond, flow, row in (
        ((s0_ref, u0_ref, v0_ref), 0, 1, northward, 0),
        ((s1_ref, u1_ref, v1_ref), last, last - 1, southward, rows - 1),
    ):
        cut = jnp.where(mask_ref[row] == 1, cutoff_ref[row], -1)
        s, u, v = (ref[:, at, :] for ref in refs)
        tail = jnp.full((levels, width - s.shape[1]), cut.astype(F32))
        parts = [padded(u, width), padded(v, width), padded(flow(refs[0][:, beyond, :], refs[2][:, beyond, :]), width)]
        sides.append([jnp.concatenate([s, tail], axis=1), *parts])
    own_ref[0] = padded(northward(s0_ref[:, 0, :], v0_ref[:, 0, :]), width)
    own_ref[1] = padded(southward(s1_ref[:, last, :], v1_ref[:, last, :]), width)
    for i in range(4):
        ring0_ref[i] = jnp.where(near, sides[1][i], sides[0][i])
        ring1_ref[i] = jnp.where(near, sides[0][i], sides[1][i])


def group_copies(hbm_refs, buffers, sem, first, i):
    return [
        pltpu.make_async_copy(h.at[pl.ds(first + i * GROUP, GROUP)], b.at[pl.ds(i * GROUP, GROUP)], sem.at[q, i])
        for q, (h, b) in enumerate(zip(hbm_refs, buffers))
    ]


def group_stores(buffer, hbm_ref, sem, first, i):
    return pltpu.make_async_copy(
        buffer.at[pl.ds(i * GROUP, GROUP)], hbm_ref.at[pl.ds(first + i * GROUP, GROUP)], sem.at[i]
    )


def outflow(x, cells):
    tile = jnp.transpose(x[:, x.shape[1] - 128 :])
    at = cells - (x.shape[1] - 128)
    return jnp.concatenate([tile[at : at + 1, :], tile[127:128, :]], axis=1)


def pack_rows(cut_ref, source_ref, first, out_ref):
    rows = cut_ref.shape[0]

    def body(r, unit):
        cut = cut_ref[r]
        for half in range(2):
            out_ref[unit + half] = source_ref[half, pl.ds(r, SUB, stride=rows), :]
        return unit + (cut >= 0).astype(jnp.int32) + (cut >= HALF).astype(jnp.int32)

    lax.fori_loop(0, rows, body, first, unroll=8)


def scaled(x, half, cut, total):
    lane = lax.broadcasted_iota(jnp.int32, (SUB, KMAX), 1)
    wave = half * HALF + lane % HALF
    scale = jnp.where(wave == 0, 1.0 / total, 2.0 / total)
    return jnp.where(wave <= cut, x * scale, 0.0)


def unpack_rows(cut_ref, a_ref, b_ref, first, total, out_ref):
    rows = cut_ref.shape[0]
    last = a_ref.shape[0] - 1

    def body(r, unit):
        cut = cut_ref[r]
        for half in range(2):
            at = jnp.minimum(unit + half, last)
            out_ref[half, pl.ds(r, SUB, stride=rows), :] = scaled(a_ref[at] + b_ref[at], half, cut, total)
        return unit + (cut >= 0).astype(jnp.int32) + (cut >= HALF).astype(jnp.int32)

    lax.fori_loop(0, rows, body, first, unroll=8)


def put_slots(out_ref, first, ways, lon, value):
    for i in range(ways):
        out_ref[first + i] = jnp.zeros(value.shape, F32)
    out_ref[first + lon] = value


def inflow(a_ref, b_ref, first, ways, lon, rows, place):
    west, east = first + lax.rem(lon + ways - 1, ways), first + lax.rem(lon + 1, ways)
    place[0:SUB, :] = a_ref[west] + b_ref[west]
    west_columns = jnp.transpose(place[...])[:rows, :]
    place[0:SUB, :] = a_ref[east] + b_ref[east]
    east_columns = jnp.transpose(place[...])[rows : 2 * rows, :]
    return west_columns, east_columns


def first_body(first, cells, hbm_refs, buffers, sem, moved_ref, hbm_moved_ref, out_sem, coef_ref, edge_ref, table_ref, ready):
    levels, rows, width = moved_ref.shape
    for i in range(levels // GROUP):
        for copy in group_copies(hbm_refs, buffers, sem, first, i):
            copy.wait()
        for g in range(GROUP):
            level = i * GROUP + g
            x = moved_rows(*[padded(b[level], width) for b in buffers])
            moved_ref[level] = x
            edge_ref[level : level + 1, :] = outflow(x, cells)
        group_stores(moved_ref, hbm_moved_ref, out_sem, 0, i).start()
        if i == 0:
            ready.wait()
        x = moved_ref[i * GROUP : (i + 1) * GROUP].reshape(GROUP * rows, width)
        put_halves(coef_ref, slice(i * GROUP * rows, (i + 1) * GROUP * rows), project(x, table_ref[...]))


def first_kernel(
    first, cells, info_ref, s_ref, u_ref, v_ref, tables_ref, hbm_moved_ref, coef_ref, edge_ref,
    s_buf, u_buf, v_buf, moved_ref, table_ref, sem, out_sem, table_sem,
):
    hbm_refs, buffers = (s_ref, u_ref, v_ref), (s_buf, u_buf, v_buf)
    steps = moved_ref.shape[0] // GROUP
    ready = pltpu.make_async_copy(tables_ref.at[info_ref[0]], table_ref, table_sem)
    for i in range(steps):
        for copy in group_copies(hbm_refs, buffers, sem, first, i):
            copy.start()
        if i == 0:
            ready.start()
    first_body(first, cells, hbm_refs, buffers, sem, moved_ref, hbm_moved_ref, out_sem, coef_ref, edge_ref, table_ref, ready)
    for i in range(steps):
        group_stores(moved_ref, hbm_moved_ref, out_sem, 0, i).wait()


def join_flows(first, cells, info_ref, own_ref, ring0_ref, ring1_ref, flow_ref, edge_v_ref, edge_cut_ref):
    levels, width = flow_ref.shape[1:]
    at = slice(first, first + levels)
    near = info_ref[0] < info_ref[1] // 2
    lane = lax.broadcasted_iota(jnp.int32, (levels, width), 1)
    for side in range(2):
        got = [jnp.where(near == (side == 0), ring0_ref[i, at, :], ring1_ref[i, at, :]) for i in range(4)]
        edge_cut_ref[side] = jnp.broadcast_to(got[0][:, cells : cells + 1], (levels, KMAX))
        s = jnp.where(lane < cells, got[0], 0.0)
        pole = info_ref[2] == (0 if side == 0 else info_ref[3] - 1)
        v = jnp.where(pole, -got[2], got[2])
        edge_v_ref[side] = v
        flow_ref[side] = southward(s, v) if side == 0 else northward(s, v)
        flow_ref[2 + side] = along_lon(s, got[1]) + got[3] + own_ref[side, at, :]


def join_body(cells, info_ref, cut_ref, ways, coef_ref, edge_ref, flow_ref, table_ref, out_ref):
    rows = cut_ref.shape[0]
    levels, width = flow_ref.shape[1:]
    lon = info_ref[0]
    extra = project(flow_ref[...].reshape(4 * levels, width), table_ref[...])
    first = pl.ds(0, SUB, stride=rows)
    last = pl.ds(rows - 1, SUB, stride=rows)
    for half in range(2):
        part = extra[:, half * KMAX : (half + 1) * KMAX]
        coef_ref[half, first, :] = coef_ref[half, first, :] + part[:levels]
        coef_ref[half, last, :] = coef_ref[half, last, :] + part[levels : 2 * levels]
        out_ref[half] = part[2 * levels : 3 * levels]
        out_ref[2 + half] = part[3 * levels :]
    put_slots(out_ref, 4, ways, lon, edge_ref[...])
    lane = lax.broadcasted_iota(jnp.int32, (SUB, KMAX), 1)
    unit = jnp.zeros((SUB, KMAX), F32)
    for side in range(2):
        for way, at in enumerate((cells, width - 1)):
            unit = jnp.where(lane == 4 * lon + 2 * side + way, flow_ref[2 + side][:, at : at + 1], unit)
    out_ref[4 + ways] = unit
    pack_rows(cut_ref, coef_ref, 5 + ways, out_ref)


def join_kernel(
    first, cells, ways,
    info_ref, cut_ref, coef_in_ref, edge_ref, own_ref, ring0_ref, ring1_ref, tables_ref,
    flow_ref, edge_v_ref, edge_cut_ref, out_ref, coef_ref, table_ref, table_sem,
):
    ready = pltpu.make_async_copy(tables_ref.at[info_ref[0]], table_ref, table_sem)
    ready.start()
    coef_ref[...] = coef_in_ref[...]
    join_flows(first, cells, info_ref, own_ref, ring0_ref, ring1_ref, flow_ref, edge_v_ref, edge_cut_ref)
    ready.wait()
    join_body(cells, info_ref, cut_ref, ways, coef_ref, edge_ref, flow_ref, table_ref, out_ref)


def first_join_kernel(
    first, cells, ways,
    info_ref, cut_ref, s_ref, u_ref, v_ref, own_ref, ring0_ref, ring1_ref, tables_ref,
    hbm_moved_ref, flow_ref, edge_v_ref, edge_cut_ref, out_ref,
    s_buf, u_buf, v_buf, moved_ref, table_ref, coef_ref, edge_ref, sem, out_sem, table_sem,
):
    hbm_refs, buffers = (s_ref, u_ref, v_ref), (s_buf, u_buf, v_buf)
    steps = moved_ref.shape[0] // GROUP
    ready = pltpu.make_async_copy(tables_ref.at[info_ref[0]], table_ref, table_sem)
    for i in range(steps):
        for copy in group_copies(hbm_refs, buffers, sem, first, i):
            copy.start()
        if i == 0:
            ready.start()
    join_flows(first, cells, info_ref, own_ref, ring0_ref, ring1_ref, flow_ref, edge_v_ref, edge_cut_ref)
    first_body(first, cells, hbm_refs, buffers, sem, moved_ref, hbm_moved_ref, out_sem, coef_ref, edge_ref, table_ref, ready)
    join_body(cells, info_ref, cut_ref, ways, coef_ref, edge_ref, flow_ref, table_ref, out_ref)
    for i in range(steps):
        group_stores(moved_ref, hbm_moved_ref, out_sem, 0, i).wait()


def closed(x, west, east, cells):
    end = x.shape[1] - 128
    lane = lax.broadcasted_iota(jnp.int32, (x.shape[0], 128), 1)
    head = x[:, :128] + jnp.where(lane == 0, west, 0.0)
    tail = x[:, end:] + jnp.where(lane == cells - 1 - end, east, 0.0)
    return jnp.concatenate([head, x[:, 128:end], jnp.where(lane < cells - end, tail, 0.0)], axis=1)


def second_kernel(
    first, total, cells, ways,
    info_ref, cut_ref, cut_row_ref, a_ref, b_ref, flow_ref, edge_v_ref, edge_cut_ref,
    hbm_in_ref, tables_ref, backs_ref, u_ref, v_ref,
    hbm_out_ref, pay_ref,
    moved_buf, out_ref, coef_ref, sum_ref, step_ref, edge_ref, place_ref, u_buf, v_buf, table_ref, back_ref,
    sem, in_sem, out_sem, table_sem,
):
    rows = cut_ref.shape[0]
    levels, _, width = out_ref.shape
    steps = levels // GROUP
    lon = info_ref[0]
    loads = [
        pltpu.make_async_copy(backs_ref.at[lon], back_ref, table_sem.at[0]),
        pltpu.make_async_copy(tables_ref.at[lon], table_ref, table_sem.at[1]),
    ]
    loads[0].start()
    for i in range(steps):
        for copy in group_copies((hbm_in_ref,), (moved_buf,), in_sem, 0, i):
            copy.start()
        for copy in group_copies((u_ref, v_ref), (u_buf, v_buf), sem, first, i):
            copy.start()
        if i == 0:
            loads[1].start()
    place_ref[...] = jnp.zeros_like(place_ref)
    unpack_rows(cut_ref, a_ref, b_ref, 5 + ways, total, coef_ref)
    for side in range(2):
        for half in range(2):
            at = 2 * side + half
            cut = edge_cut_ref[side].astype(jnp.int32)
            edge_ref[side * levels : (side + 1) * levels, half * KMAX : (half + 1) * KMAX] = scaled(
                a_ref[at] + b_ref[at], half, cut, total
            )
    west, east = inflow(a_ref, b_ref, 4, ways, lon, rows, place_ref)
    unit = a_ref[4 + ways] + b_ref[4 + ways]
    lane = lax.broadcasted_iota(jnp.int32, (SUB, KMAX), 1)
    loads[0].wait()
    smooth = rebuild(edge_ref[...], back_ref[...])
    for side in range(2):
        came = [
            jnp.sum(jnp.where(lane == 4 * lax.rem(lon + ways + step, ways) + 2 * side + way, unit, 0.0), axis=1, keepdims=True)
            for way, step in enumerate((-1, 1))
        ]
        plain = closed(flow_ref[2 + side], came[0], came[1], cells)
        filtered = edge_cut_ref[side][:, 0:1] >= 0.0
        s = jnp.where(filtered, smooth[side * levels : (side + 1) * levels], plain)
        step_ref[side] = (southward if side == 0 else northward)(s, edge_v_ref[side])
    filtered = filtered_column(cut_row_ref)
    for i in range(steps):
        smooth = rebuild(both_halves(coef_ref, slice(i * GROUP * rows, (i + 1) * GROUP * rows)), back_ref[...])
        for copy in group_copies((u_ref, v_ref), (u_buf, v_buf), sem, first, i):
            copy.wait()
        group_copies((hbm_in_ref,), (moved_buf,), in_sem, 0, i)[0].wait()
        for g in range(GROUP):
            level = i * GROUP + g
            row = slice(level, level + 1)
            moved_buf[level, 0:1, :] = moved_buf[level, 0:1, :] + flow_ref[0, row, :]
            moved_buf[level, rows - 1 : rows, :] = moved_buf[level, rows - 1 : rows, :] + flow_ref[1, row, :]
            plain = closed(moved_buf[level], west[:, row], east[:, row], cells)
            s = jnp.where(filtered, smooth[g * rows : (g + 1) * rows], plain)
            out_ref[level] = moved_rows(s, padded(u_buf[level], width), padded(v_buf[level], width))
            out_ref[level, 0:1, :] = out_ref[level, 0:1, :] + step_ref[0, row, :]
            out_ref[level, rows - 1 : rows, :] = out_ref[level, rows - 1 : rows, :] + step_ref[1, row, :]
            place_ref[row, :] = outflow(out_ref[level], cells)
        group_stores(out_ref, hbm_out_ref, out_sem, 0, i).start()
        if i == 0:
            loads[1].wait()
        x = out_ref[i * GROUP : (i + 1) * GROUP].reshape(GROUP * rows, width)
        put_halves(sum_ref, slice(i * GROUP * rows, (i + 1) * GROUP * rows), project(x, table_ref[...]))
    put_slots(pay_ref, 0, ways, lon, place_ref[0:SUB, :])
    pack_rows(cut_ref, sum_ref, ways, pay_ref)
    for i in range(steps):
        group_stores(out_ref, hbm_out_ref, out_sem, 0, i).wait()


def third_kernel(
    first, total, cells, ways, info_ref, cut_ref, cut_row_ref, a_ref, b_ref, hbm_in_ref, backs_ref, *refs
):
    out_ref, coef_ref, place_ref, moved_buf, buffer, back_ref, in_sem, out_sem, table_sem = refs[-9:]
    rows = cut_ref.shape[0]
    levels = moved_buf.shape[0]
    steps = levels // GROUP
    lon = info_ref[0]
    ready = pltpu.make_async_copy(backs_ref.at[lon], back_ref, table_sem)
    ready.start()
    for i in range(steps):
        group_copies((hbm_in_ref,), (moved_buf,), in_sem, 0, i)[0].start()
    place_ref[...] = jnp.zeros_like(place_ref)
    unpack_rows(cut_ref, a_ref, b_ref, ways, total, coef_ref)
    west, east = inflow(a_ref, b_ref, 0, ways, lon, rows, place_ref)
    filtered = filtered_column(cut_row_ref)
    ready.wait()
    for i in range(steps):
        smooth = rebuild(both_halves(coef_ref, slice(i * GROUP * rows, (i + 1) * GROUP * rows)), back_ref[...])
        group_copies((hbm_in_ref,), (moved_buf,), in_sem, 0, i)[0].wait()
        for g in range(GROUP):
            level = i * GROUP + g
            row = slice(level, level + 1)
            plain = closed(moved_buf[level], west[:, row], east[:, row], cells)
            buffer[level] = jnp.where(filtered, smooth[g * rows : (g + 1) * rows], plain)[:, :cells]
        group_stores(buffer, out_ref, out_sem, first, i).start()
    for i in range(steps):
        group_stores(buffer, out_ref, out_sem, first, i).wait()


SMEM = pl.BlockSpec(memory_space=pltpu.SMEM)
VMEM = pl.BlockSpec(memory_space=pltpu.VMEM)
HBM = pl.BlockSpec(memory_space=pltpu.HBM)


def shape(*dims, dtype=F32):
    return jax.ShapeDtypeStruct(dims, dtype)


def call(kernel, inputs, outputs, scratch, mib, aliases=None):
    return pl.pallas_call(
        kernel,
        in_specs=[spec for _, spec in inputs],
        out_specs=[spec for _, spec in outputs],
        out_shape=[what for what, _ in outputs],
        scratch_shapes=scratch,
        input_output_aliases=aliases or {},
        compiler_params=pltpu.CompilerParams(vmem_limit_bytes=mib * MIB),
    )(*[array for array, _ in inputs])


def swap(x, bit):
    count = lax.axis_size("lon")
    return lax.ppermute(x, "lon", [(i, i ^ (1 << bit)) for i in range(count)])


def sum_over_lon(x, upward):
    bits = lax.axis_size("lon").bit_length() - 1
    for i in range(bits):
        got = swap(x, i if upward else bits - 1 - i)
        if i == bits - 1:
            return x, got
        x = x + got


def lat_ring(bands, ways, turn):
    pairs = []
    for band in range(bands):
        for l in range(ways):
            east = l < ways // 2
            other = (l + ways // 2) % ways
            step = 1 if east == (turn == 0) else -1
            to = (band + step, l) if 0 <= band + step < bands else (band, other)
            pairs.append((l * bands + band, to[1] * bands + to[0]))
    return pairs


def on_device(tracer, zonal, meridional, cutoff_wave, polar_mask):
    levels, rows, cells = tracer.shape
    ways, bands = lax.axis_size("lon"), lax.axis_size("lat")
    width = wide(cells)
    total = cells * ways
    tables, backs = (jnp.asarray(x) for x in wave_tables(cells, ways))
    lon, band = lax.axis_index("lon"), lax.axis_index("lat")
    info = jnp.stack([lon, jnp.int32(ways), band, jnp.int32(bands)]).astype(jnp.int32)
    parts = levels // SUB
    steps = SUB // GROUP
    winds = (tracer, zonal, meridional)

    top = pl.BlockSpec((levels, SUB, cells), lambda i: (0, 0, 0))
    bottom = pl.BlockSpec((levels, SUB, cells), lambda i: (0, rows // SUB - 1, 0))
    full = pl.BlockSpec((4, levels, width), lambda i: (0, 0, 0))
    ring0, ring1, own = pl.pallas_call(
        edge_kernel,
        grid=(1,),
        in_specs=[SMEM, SMEM, SMEM, top, top, top, bottom, bottom, bottom],
        out_specs=[full, full, pl.BlockSpec((2, levels, width), lambda i: (0, 0, 0))],
        out_shape=[shape(4, levels, width), shape(4, levels, width), shape(2, levels, width)],
        compiler_params=pltpu.CompilerParams(vmem_limit_bytes=VMEM_MIB * MIB),
    )(info, cutoff_wave, polar_mask, *winds, *winds)
    ring = ("lon", "lat")
    got0 = lax.ppermute(ring0, ring, lat_ring(bands, ways, 0))
    got1 = lax.ppermute(ring1, ring, lat_ring(bands, ways, 1))
    cut = jnp.where(polar_mask == 1, cutoff_wave, -1)
    kept = jnp.sum((cut >= 0).astype(jnp.int32) + (cut >= HALF).astype(jnp.int32))
    cut_row = cut[None, :]

    grid = shape(SUB, rows, width)
    coef = shape(2, SUB * rows, KMAX)
    edge = shape(SUB, KMAX)
    flows = [(shape(4, SUB, width), VMEM), (shape(2, SUB, width), VMEM), (shape(2, SUB, KMAX), VMEM)]
    head = 5 + ways

    def room(what):
        return pltpu.VMEM(what.shape, what.dtype)

    buffer = pltpu.VMEM((SUB, rows, cells), F32)
    table, back = room(shape(*tables.shape[1:], dtype=BF16)), room(shape(*backs.shape[1:], dtype=BF16))
    sems = pltpu.SemaphoreType.DMA
    first_scratch = [buffer, buffer, buffer, room(grid), table]
    moved_a, coef_a, edge_a = call(
        functools.partial(first_kernel, 0, cells),
        [(info, SMEM), *[(x, HBM) for x in winds], (tables, HBM)],
        [(grid, HBM), (coef, VMEM), (edge, VMEM)],
        [*first_scratch, sems((3, steps)), sems((steps,)), sems(())],
        VMEM_MIB,
    )

    def rest(limit, info, cut, cut_row, tracer, zonal, meridional, own, got0, got1, moved_a, coef_a, edge_a):
        pay = (shape(limit + head + 2, SUB, KMAX), VMEM)
        around = [(x, VMEM) for x in (own, got0, got1)]
        scalars = [(info, SMEM), (cut, SMEM)]
        joined = [(moved_a, *call(
            functools.partial(join_kernel, 0, cells, ways),
            [*scalars, (coef_a, VMEM), (edge_a, VMEM), *around, (tables, HBM)],
            [*flows, pay],
            [room(coef), table, sems(())],
            VMEM_MIB,
        ))]
        sums = [sum_over_lon(joined[0][4], True)]
        for part in range(1, parts):
            joined.append(call(
                functools.partial(first_join_kernel, part * SUB, cells, ways),
                [*scalars, *[(x, HBM) for x in (tracer, zonal, meridional)], *around, (tables, HBM)],
                [(grid, HBM), *flows, pay],
                [*first_scratch, room(coef), room(edge), sems((3, steps)), sems((steps,)), sems(())],
                VMEM_MIB,
            ))
            sums.append(sum_over_lon(joined[part][4], part % 2 == 0))
        seconds = []
        for part in range(parts):
            moved, flow, edge_v, edge_cut, _ = joined[part]
            seconds.append(call(
                functools.partial(second_kernel, part * SUB, total, cells, ways),
                [*scalars, *[(x, VMEM) for x in (cut_row, *sums[part], flow, edge_v, edge_cut)],
                 *[(x, HBM) for x in (moved, tables, backs, zonal, meridional)]],
                [(grid, HBM), (shape(limit + ways + 2, SUB, KMAX), VMEM)],
                [room(grid), room(grid), room(coef), room(coef), pltpu.VMEM((2, SUB, width), F32),
                 pltpu.VMEM((2 * SUB, 2 * KMAX), F32), pltpu.VMEM((KMAX, KMAX), F32), buffer, buffer, table, back,
                 sems((2, steps)), sems((1, steps)), sems((steps,)), sems((2,))],
                VMEM_MIB,
            ))
        sums = [sum_over_lon(x[1], part % 2 == 0) for part, x in enumerate(seconds)]
        out = []
        for part in range(parts):
            out = call(
                functools.partial(third_kernel, part * SUB, total, cells, ways),
                [*scalars, *[(x, VMEM) for x in (cut_row, *sums[part])],
                 *[(x, HBM) for x in (seconds[part][0], backs, *out)]],
                [(shape(levels, rows, cells), HBM)],
                [room(coef), pltpu.VMEM((KMAX, KMAX), F32), room(grid), buffer, back,
                 sems((1, steps)), sems((steps,)), sems(())],
                VMEM_MIB,
                {7: 0} if part else None,
            )
        return out[0]

    limits = sorted({min(-(-x * rows // 64), 2 * rows) for x in LIMITS})
    choice = sum((kept > x).astype(jnp.int32) for x in limits[:-1])
    return lax.switch(
        choice, [functools.partial(rest, x) for x in limits],
        info, cut, cut_row, tracer, zonal, meridional, own, got0, got1, moved_a, coef_a, edge_a,
    )


def solution(mesh):
    placed = (
        P(None, "lat", "lon"),
        P(None, "lat", "lon"),
        P(None, "lat", "lon"),
        P("lat"),
        P("lat"),
    )
    return jax.shard_map(
        on_device, mesh=mesh, in_specs=placed, out_specs=P(None, "lat", "lon"), check_vma=False
    )
```

profile of v0, /device:TPU:0, one launch (start us, length us, event | category | flops | bytes accessed | tf_op | source)
XLA Modules:
  0.0 126.7 jit_solution(17784402030046478439)
XLA Ops:
  0.0 0.1 pad_add_fusion.info_ref
  0.1 0.7 copy-done.4
  0.7 0.7 copy-done.5
  1.4 2.7 %shard_map.81 = (f32[4,16,1536]{2,1,0:T(8,128)S(1)}, f32[4,16,1536]{2,1,0:T(8,128)S(1)}, f32[2,16,1536]{2,1,0:T(8,128)S(1)}) custom-call(s32[4]{0:T(128)S(1)} %pad_add_fusion.info_ref, s32[64]{0:T(128)S(1)} %copy-done.4, s32[64]{0:T(128)S(1)} %copy-done.5, f32[16,64,1440]{2,1,0:T(8,128)} %s_ref.1, f32[16,64,1440]{2,1,0:T(8,128)} %u_ref.1, ...), custom_call_target="tpu_custom_call" | custom-call | tf_op jit(solution)/shard_map/pallas_call | solution.py:494
  4.1 0.5 collective-permute-start.32
  4.6 2.6 %collective-permute-start.33 = (f32[4,16,1536]{2,1,0:T(8,128)S(1)}, f32[4,16,1536]{2,1,0:T(8,128)S(1)}, u32[]{:S(2)}, u32[]{:S(2)}) collective-permute-start(f32[4,16,1536]{2,1,0:T(8,128)S(1)} %get-tuple-element.238), channel_id=1, source_target_pairs={{0,16},{8,24},{16,17},{24,25},{1,0},{9,8},{17,18},{25,26},{2,1},{1... | collective-permute-start | bytes 1179656 | tf_op jit(solution)/shard_map/ppermute | solution.py:504
  7.2 0.6 fusion.1
  9.8 8.5 %shard_map.82 = (f32[8,64,1536]{2,1,0:T(8,128)}, f32[2,512,128]{2,1,0:T(8,128)S(1)}, f32[8,128]{1,0:T(8,128)S(1)}) custom-call(s32[4]{0:T(128)S(1)} %pad_add_fusion.info_ref, f32[16,64,1440]{2,1,0:T(8,128)} %s_ref.1, f32[16,64,1440]{2,1,0:T(8,128)} %u_ref.1, f32[16,64,1440]{2,1,0:T(8,128)} %v_ref.1, bf16[4,1536,512]{2,1,0:T(8,128)(2,1)} %constant.33.clone.tables_ref), custom_call_target="tpu_custom_call" | custom-call | tf_op jit(solution)/shard_map/pallas_call | solution.py:442
  18.3 0.0 collective-permute-done.32
  18.3 107.0 %conditional.1 = (f32[16,64,1440]{2,1,0:T(8,128)}) conditional(s32[]{:T(128)} %clamp.3, (s32[4]{0:T(128)S(1)}, s32[64]{0:T(128)S(1)}, f32[16,64,1440]{2,1,0:T(8,128)}, f32[16,64,1440]{2,1,0:T(8,128)}, f32[16,64,1440]{2,1,0:T(8,128)}, /*index=5*/f32[2,16,1536]{2,1,0:T(8,128)S(1)}, f32[4,16,1536]{2,1,0:T(8,128)S(1)}, ...), branch_computations={%region_1.2_spmd, %region_2.3_spmd, %region_3.4_spmd, %region_4.5_... | conditional | flops 559104 | bytes 62349696 | solution.py:581
  25.5 0.0 copy-start.8
  25.6 3.2 %branch_2_fun.8 = (f32[4,8,1536]{2,1,0:T(8,128)S(1)}, f32[2,8,1536]{2,1,0:T(8,128)S(1)}, f32[2,8,128]{2,1,0:T(8,128)S(1)}, f32[103,8,128]{2,1,0:T(8,128)S(1)}) custom-call(s32[4]{0:T(128)S(1)} %get-tuple-element.176.info_ref, s32[64]{0:T(128)S(1)} %get-tuple-element.245, f32[2,512,128]{2,1,0:T(8,128)S(1)} %get-tuple-element.194.coef_in_ref, ...), custom_call_target="tpu_custom_call" | custom-call | tf_op jit(solution)/shard_map/cond/branch_2_fun/pallas_call | solution.py:442
  28.8 2.0 %collective-permute-start.20 = (f32[103,8,128]{2,1,0:T(8,128)S(1)}, f32[103,8,128]{2,1,0:T(8,128)S(1)}, u32[]{:S(2)}, u32[]{:S(2)}) collective-permute-start(f32[103,8,128]{2,1,0:T(8,128)S(1)} %get-tuple-element.196), channel_id=1, source_target_pairs={{0,8},{8,0},{16,24},{24,16},{1,9},{9,1},{17,25},{25,17},{2,10},{10... | collective-permute-start | bytes 1265672 | tf_op jit(solution)/shard_map/cond/branch_2_fun/ppermute | solution.py:455
  30.8 9.5 %branch_2_fun.6 = (f32[8,64,1536]{2,1,0:T(8,128)S(1)}, f32[4,8,1536]{2,1,0:T(8,128)S(1)}, f32[2,8,1536]{2,1,0:T(8,128)S(1)}, f32[2,8,128]{2,1,0:T(8,128)S(1)}, f32[103,8,128]{2,1,0:T(8,128)S(1)}) custom-call(s32[4]{0:T(128)S(1)} %get-tuple-element.176.info_ref, s32[64]{0:T(128)S(1)} %get-tuple-element.245, f32[16,64,1440]{2,1,0:T(8,128)} %get-tuple-element.179.s_ref, ...), custom_call_target="tpu_custom_call" | custom-call | tf_op jit(solution)/shard_map/cond/branch_2_fun/pallas_call | solution.py:442
  40.3 0.0 copy-start.3
  40.3 1.7 %copy-done.3 = f32[8,64,1536]{2,1,0:T(8,128)} copy-done((f32[8,64,1536]{2,1,0:T(8,128)}, f32[8,64,1536]{2,1,0:T(8,128)S(1)}, u32[]{:S(2)}) %copy-start.3) | copy-done | bytes 3145752 | tf_op jit(solution)/shard_map/cond
  42.0 0.0 collective-permute-start.16
  42.0 0.1 add.48.a_ref
  42.0 2.1 %collective-permute-start.21 = (f32[103,8,128]{2,1,0:T(8,128)S(1)}, f32[103,8,128]{2,1,0:T(8,128)S(1)}, u32[]{:S(2)}, u32[]{:S(2)}) collective-permute-start(f32[103,8,128]{2,1,0:T(8,128)S(1)} %add.48.a_ref), channel_id=1, source_target_pairs={{0,16},{8,24},{16,0},{24,8},{1,17},{9,25},{17,1},{25,9},{2,18},{10... | collective-permute-start | bytes 1265672 | tf_op jit(solution)/shard_map/cond/branch_2_fun/ppermute | solution.py:455
  44.1 10.5 %collective-permute-done.16 = f32[103,8,128]{2,1,0:T(8,128)S(1)} collective-permute-done((f32[103,8,128]{2,1,0:T(8,128)S(1)}, f32[103,8,128]{2,1,0:T(8,128)S(1)}, u32[]{:S(2)}, u32[]{:S(2)}) %collective-permute-start.16) | collective-permute-done | bytes 421920 | tf_op jit(solution)/shard_map/cond/branch_2_fun/ppermute | solution.py:455
  54.7 0.1 collective-permute-start.17
  54.8 7.1 %collective-permute-done.21.b_ref = f32[103,8,128]{2,1,0:T(8,128)S(1)} collective-permute-done((f32[103,8,128]{2,1,0:T(8,128)S(1)}, f32[103,8,128]{2,1,0:T(8,128)S(1)}, u32[]{:S(2)}, u32[]{:S(2)}) %collective-permute-start.21) | collective-permute-done | bytes 421920 | tf_op jit(solution)/shard_map/cond/branch_2_fun/ppermute | solution.py:455
  61.9 11.8 %branch_2_fun.9 = (f32[8,64,1536]{2,1,0:T(8,128)S(1)}, f32[98,8,128]{2,1,0:T(8,128)S(1)}) custom-call(s32[4]{0:T(128)S(1)} %get-tuple-element.176.info_ref, s32[64]{0:T(128)S(1)} %get-tuple-element.245, s32[1,64]{1,0:T(1,128)S(1)} %bitcast.14, f32[103,8,128]{2,1,0:T(8,128)S(1)} %add.48.a_ref, f32[103,8,128]{2,1,0:T(8,128)S(1)} %collective-permute-done.21.b_ref, ...), custom_call_target="tpu_custom_call" | custom-call | tf_op jit(solution)/shard_map/cond/branch_2_fun/pallas_call | solution.py:442
  73.8 0.6 collective-permute-start.22
  74.4 11.7 %branch_2_fun.7 = (f32[8,64,1536]{2,1,0:T(8,128)S(1)}, f32[98,8,128]{2,1,0:T(8,128)S(1)}) custom-call(s32[4]{0:T(128)S(1)} %get-tuple-element.176.info_ref, s32[64]{0:T(128)S(1)} %get-tuple-element.245, s32[1,64]{1,0:T(1,128)S(1)} %bitcast.15, f32[103,8,128]{2,1,0:T(8,128)S(1)} %add.46.a_ref, f32[103,8,128]{2,1,0:T(8,128)S(1)} %collective-permute-done.17.b_ref, ...), custom_call_target="tpu_custom_call" | custom-call | tf_op jit(solution)/shard_map/cond/branch_2_fun/pallas_call | solution.py:442
  86.0 1.7 %collective-permute-start.18 = (f32[98,8,128]{2,1,0:T(8,128)S(1)}, f32[98,8,128]{2,1,0:T(8,128)S(1)}, u32[]{:S(2)}, u32[]{:S(2)}) collective-permute-start(f32[98,8,128]{2,1,0:T(8,128)S(1)} %get-tuple-element.192), channel_id=1, source_target_pairs={{0,16},{8,24},{16,0},{24,8},{1,17},{9,25},{17,1},{25,9},{2,18},{10... | collective-permute-start | bytes 1204232 | tf_op jit(solution)/shard_map/cond/branch_2_fun/ppermute | solution.py:455
  87.8 0.5 collective-permute-start.23
  88.3 10.1 %collective-permute-done.18 = f32[98,8,128]{2,1,0:T(8,128)S(1)} collective-permute-done((f32[98,8,128]{2,1,0:T(8,128)S(1)}, f32[98,8,128]{2,1,0:T(8,128)S(1)}, u32[]{:S(2)}, u32[]{:S(2)}) %collective-permute-start.18) | collective-permute-done | bytes 401440 | tf_op jit(solution)/shard_map/cond/branch_2_fun/ppermute | solution.py:455
  98.4 1.6 %collective-permute-start.19 = (f32[98,8,128]{2,1,0:T(8,128)S(1)}, f32[98,8,128]{2,1,0:T(8,128)S(1)}, u32[]{:S(2)}, u32[]{:S(2)}) collective-permute-start(f32[98,8,128]{2,1,0:T(8,128)S(1)} %add.47.a_ref), channel_id=1, source_target_pairs={{0,8},{8,0},{16,24},{24,16},{1,9},{9,1},{17,25},{25,17},{2,10},{10... | collective-permute-start | bytes 1204232 | tf_op jit(solution)/shard_map/cond/branch_2_fun/ppermute | solution.py:455
  99.9 5.6 %collective-permute-done.23.b_ref = f32[98,8,128]{2,1,0:T(8,128)S(1)} collective-permute-done((f32[98,8,128]{2,1,0:T(8,128)S(1)}, f32[98,8,128]{2,1,0:T(8,128)S(1)}, u32[]{:S(2)}, u32[]{:S(2)}) %collective-permute-start.23) | collective-permute-done | bytes 401440 | tf_op jit(solution)/shard_map/cond/branch_2_fun/ppermute | solution.py:455
  105.5 5.3 %branch_2_fun.10.refs_0_ = f32[16,64,1440]{2,1,0:T(8,128)} custom-call(s32[4]{0:T(128)S(1)} %get-tuple-element.176.info_ref, s32[64]{0:T(128)S(1)} %get-tuple-element.245, s32[1,64]{1,0:T(1,128)S(1)} %bitcast.16, f32[98,8,128]{2,1,0:T(8,128)S(1)} %add.49.a_ref, f32[98,8,128]{2,1,0:T(8,128)S(1)} %collective-permute-done.23.b_ref, ...), custom_call_target="tpu_custom_call" | custom-call | tf_op jit(solution)/shard_map/cond/branch_2_fun/pallas_call | solution.py:442
  110.8 5.3 %branch_2_fun.11 = f32[16,64,1440]{2,1,0:T(8,128)} custom-call(s32[4]{0:T(128)S(1)} %get-tuple-element.176.info_ref, s32[64]{0:T(128)S(1)} %get-tuple-element.245, s32[1,64]{1,0:T(1,128)S(1)} %bitcast.17, f32[98,8,128]{2,1,0:T(8,128)S(1)} %add.47.a_ref, f32[98,8,128]{2,1,0:T(8,128)S(1)} %collective-permute-done.19.b_ref, ...), custom_call_target="tpu_custom_call", output_to_operand_aliasing={{}: (7, {})} | custom-call | tf_op jit(solution)/shard_map/cond/branch_2_fun/pallas_call | solution.py:442
  (11 shorter events, 0.1 us)
Async XLA Ops:
  0.1 0.7 copy-start.4
  0.7 0.7 copy-start.5
  4.1 14.2 %collective-permute-start.32 = (f32[4,16,1536]{2,1,0:T(8,128)S(1)}, f32[4,16,1536]{2,1,0:T(8,128)S(1)}, u32[]{:S(2)}, u32[]{:S(2)}) collective-permute-start(f32[4,16,1536]{2,1,0:T(8,128)S(1)} %get-tuple-element.237), channel_id=1, source_target_pairs={{0,1},{8,9},{16,0},{24,8},{1,2},{9,10},{17,16},{25,24},{2,3},{10,1... | collective-permute-start | bytes 1179656 | tf_op jit(solution)/shard_map/ppermute | solution.py:503
  4.6 13.7 %collective-permute-start.33 = (f32[4,16,1536]{2,1,0:T(8,128)S(1)}, f32[4,16,1536]{2,1,0:T(8,128)S(1)}, u32[]{:S(2)}, u32[]{:S(2)}) collective-permute-start(f32[4,16,1536]{2,1,0:T(8,128)S(1)} %get-tuple-element.238), channel_id=1, source_target_pairs={{0,16},{8,24},{16,17},{24,25},{1,0},{9,8},{17,18},{25,26},{2,1},{1... | collective-permute-start | bytes 1179656 | tf_op jit(solution)/shard_map/ppermute | solution.py:504
  25.5 5.2 %copy-start.8 = (bf16[4,1536,512]{2,1,0:T(8,128)(2,1)S(1)}, bf16[4,1536,512]{2,1,0:T(8,128)(2,1)}, u32[]{:S(2)}) copy-start(bf16[4,1536,512]{2,1,0:T(8,128)(2,1)} %get-tuple-element.185.tables_ref) | copy-start | bytes 18874372 | tf_op jit(solution)/shard_map/cond
  28.8 13.2 %collective-permute-start.20 = (f32[103,8,128]{2,1,0:T(8,128)S(1)}, f32[103,8,128]{2,1,0:T(8,128)S(1)}, u32[]{:S(2)}, u32[]{:S(2)}) collective-permute-start(f32[103,8,128]{2,1,0:T(8,128)S(1)} %get-tuple-element.196), channel_id=1, source_target_pairs={{0,8},{8,0},{16,24},{24,16},{1,9},{9,1},{17,25},{25,17},{2,10},{10... | collective-permute-start | bytes 1265672 | tf_op jit(solution)/shard_map/cond/branch_2_fun/ppermute | solution.py:455
  40.3 1.7 %copy-start.3 = (f32[8,64,1536]{2,1,0:T(8,128)}, f32[8,64,1536]{2,1,0:T(8,128)S(1)}, u32[]{:S(2)}) copy-start(f32[8,64,1536]{2,1,0:T(8,128)S(1)} %get-tuple-element.190.hbm_in_ref) | copy-start | bytes 9437188 | tf_op jit(solution)/shard_map/cond
  42.0 12.7 %collective-permute-start.16 = (f32[103,8,128]{2,1,0:T(8,128)S(1)}, f32[103,8,128]{2,1,0:T(8,128)S(1)}, u32[]{:S(2)}, u32[]{:S(2)}) collective-permute-start(f32[103,8,128]{2,1,0:T(8,128)S(1)} %get-tuple-element.186), channel_id=1, source_target_pairs={{0,16},{8,24},{16,0},{24,8},{1,17},{9,25},{17,1},{25,9},{2,18},{10... | collective-permute-start | bytes 1265672 | tf_op jit(solution)/shard_map/cond/branch_2_fun/ppermute | solution.py:455
  42.0 19.9 %collective-permute-start.21 = (f32[103,8,128]{2,1,0:T(8,128)S(1)}, f32[103,8,128]{2,1,0:T(8,128)S(1)}, u32[]{:S(2)}, u32[]{:S(2)}) collective-permute-start(f32[103,8,128]{2,1,0:T(8,128)S(1)} %add.48.a_ref), channel_id=1, source_target_pairs={{0,16},{8,24},{16,0},{24,8},{1,17},{9,25},{17,1},{25,9},{2,18},{10... | collective-permute-start | bytes 1265672 | tf_op jit(solution)/shard_map/cond/branch_2_fun/ppermute | solution.py:455
  54.7 19.7 %collective-permute-start.17 = (f32[103,8,128]{2,1,0:T(8,128)S(1)}, f32[103,8,128]{2,1,0:T(8,128)S(1)}, u32[]{:S(2)}, u32[]{:S(2)}) collective-permute-start(f32[103,8,128]{2,1,0:T(8,128)S(1)} %add.46.a_ref), channel_id=1, source_target_pairs={{0,8},{8,0},{16,24},{24,16},{1,9},{9,1},{17,25},{25,17},{2,10},{10... | collective-permute-start | bytes 1265672 | tf_op jit(solution)/shard_map/cond/branch_2_fun/ppermute | solution.py:455
  73.8 13.9 %collective-permute-start.22 = (f32[98,8,128]{2,1,0:T(8,128)S(1)}, f32[98,8,128]{2,1,0:T(8,128)S(1)}, u32[]{:S(2)}, u32[]{:S(2)}) collective-permute-start(f32[98,8,128]{2,1,0:T(8,128)S(1)} %get-tuple-element.201), channel_id=1, source_target_pairs={{0,8},{8,0},{16,24},{24,16},{1,9},{9,1},{17,25},{25,17},{2,10},{10... | collective-permute-start | bytes 1204232 | tf_op jit(solution)/shard_map/cond/branch_2_fun/ppermute | solution.py:455
  86.0 12.3 %collective-permute-start.18 = (f32[98,8,128]{2,1,0:T(8,128)S(1)}, f32[98,8,128]{2,1,0:T(8,128)S(1)}, u32[]{:S(2)}, u32[]{:S(2)}) collective-permute-start(f32[98,8,128]{2,1,0:T(8,128)S(1)} %get-tuple-element.192), channel_id=1, source_target_pairs={{0,16},{8,24},{16,0},{24,8},{1,17},{9,25},{17,1},{25,9},{2,18},{10... | collective-permute-start | bytes 1204232 | tf_op jit(solution)/shard_map/cond/branch_2_fun/ppermute | solution.py:455
  87.8 17.8 %collective-permute-start.23 = (f32[98,8,128]{2,1,0:T(8,128)S(1)}, f32[98,8,128]{2,1,0:T(8,128)S(1)}, u32[]{:S(2)}, u32[]{:S(2)}) collective-permute-start(f32[98,8,128]{2,1,0:T(8,128)S(1)} %add.49.a_ref), channel_id=1, source_target_pairs={{0,16},{8,24},{16,0},{24,8},{1,17},{9,25},{17,1},{25,9},{2,18},{10... | collective-permute-start | bytes 1204232 | tf_op jit(solution)/shard_map/cond/branch_2_fun/ppermute | solution.py:455
  98.4 12.4 %collective-permute-start.19 = (f32[98,8,128]{2,1,0:T(8,128)S(1)}, f32[98,8,128]{2,1,0:T(8,128)S(1)}, u32[]{:S(2)}, u32[]{:S(2)}) collective-permute-start(f32[98,8,128]{2,1,0:T(8,128)S(1)} %add.47.a_ref), channel_id=1, source_target_pairs={{0,8},{8,0},{16,24},{24,16},{1,9},{9,1},{17,25},{25,17},{2,10},{10... | collective-permute-start | bytes 1204232 | tf_op jit(solution)/shard_map/cond/branch_2_fun/ppermute | solution.py:455
where the time goes:
time: 129 us; the launch traced here: 127 us
  Pallas kernels  57.9 us (45%)
  waiting for transfers between devices  33.3 us (26%)
  loops' own time  16.6 us (13%)
  starting transfers between devices  11.6 us (9%)
  between operations  3.33 us (3%)
  local copies, waits for them, and re-layouts  2.98 us (2%)
    pallas_call x7, Pallas kernels, call(): pl.pallas_call(kernel, in_specs=[spec for _, spec in inputs], out_specs=[...  55.3 us
    ppermute x8, waiting for transfers between devices, swap(): return lax.ppermute(x, 'lon', [(i, i ^ 1 << bit) for i in range(count)])  33.3 us
    another operation x1, loops' own time, on_device(): lax.switch(choice, [functools.partial(rest, x) for x in limits], info, cu...  16.6 us
    ppermute x8, starting transfers between devices, swap(): return lax.ppermute(x, 'lon', [(i, i ^ 1 << bit) for i in range(count)])  8.53 us
    pallas_call x1, Pallas kernels, on_device(): pl.pallas_call(edge_kernel, grid=(1,), in_specs=[SMEM, SMEM, SMEM, top, t...  2.68 us
    ppermute x1, starting transfers between devices, on_device(): got1 = lax.ppermute(ring1, ring, lat_ring(bands, ways, 1))  2.59 us
  transfers between devices with their start and end apart: 10, of which 4 were waited for; matrix products, arithmetic and copies ran while one was open for 1% of the time, Pallas kernels for 37%

commit v1 on v0

v1 whole, which is shorter than its diff:
```python
import functools

import jax
import jax.numpy as jnp
import ml_dtypes
import numpy as np
from jax import lax
from jax.experimental import pallas as pl
from jax.experimental.pallas import tpu as pltpu
from jax.sharding import PartitionSpec as P

KMAX = 128
HALF = KMAX // 2
DIFFUSION = 0.1
GROUP = 4
SUB = 8
FIRST_MIB = 52
LIMITS = (92, 128)
F32 = jnp.float32
BF16 = jnp.bfloat16
MIB = 1024 * 1024


def wide(cells):
    return -(-(cells + 2) // 128) * 128


def split_np(values):
    high = values.astype(ml_dtypes.bfloat16)
    low = (values - high.astype(np.float64)).astype(ml_dtypes.bfloat16)
    return high, low


@functools.lru_cache(maxsize=None)
def wave_tables(cells, ways):
    total = cells * ways
    width = wide(cells)
    lane = np.arange(width)
    start = np.arange(ways)[:, None] * cells
    place = np.where(lane == width - 1, -1, lane)[None, :] + start
    used = (lane <= cells) | (lane == width - 1)
    column = np.arange(2 * KMAX)
    wave = column // KMAX * HALF + column % HALF
    sine = column % KMAX // HALF
    angle = (place[:, :, None] * wave[None, None, :] % total) * (2.0 * np.pi / total)
    table = np.where(sine == 1, np.sin(angle), np.cos(angle))
    project = split_np(np.where(used[None, :, None], table, 0.0))
    inside = np.where((lane < cells)[None, :, None], table, 0.0).transpose(0, 2, 1)
    rebuild = split_np(inside)
    return np.concatenate(project, axis=2), np.concatenate(rebuild, axis=1)


def split(x):
    high = x.astype(BF16)
    return high, (x - high.astype(F32)).astype(BF16)


def project(x, table):
    high, low = split(x)
    both = jnp.dot(high, table, preferred_element_type=F32)
    cross = jnp.dot(low, table[:, : 2 * KMAX], preferred_element_type=F32)
    return both[:, : 2 * KMAX] + both[:, 2 * KMAX :] + cross


def rebuild(coefficients, table):
    high, low = split(coefficients)
    both = jnp.dot(jnp.concatenate([high, high], axis=1), table, preferred_element_type=F32)
    return both + jnp.dot(low, table[: 2 * KMAX], preferred_element_type=F32)


def padded(x, width):
    return jnp.concatenate([x, jnp.zeros((x.shape[0], width - x.shape[1]), F32)], axis=1)


def along_lon(s, u):
    width = s.shape[1]
    spread = DIFFUSION * s
    carry = (0.5 * u) * s
    return (
        (1.0 - 4.0 * DIFFUSION) * s
        + pltpu.roll(spread - carry, width - 1, 1)
        + pltpu.roll(spread + carry, 1, 1)
    )


def moved_rows(s, u, v):
    rows = s.shape[0]
    spread = DIFFUSION * s
    carry = (0.5 * v) * s
    row = lax.broadcasted_iota(jnp.int32, s.shape, 0)
    from_next = jnp.where(row == rows - 1, 0.0, pltpu.roll(spread - carry, rows - 1, 0))
    from_last = jnp.where(row == 0, 0.0, pltpu.roll(spread + carry, 1, 0))
    return along_lon(s, u) + from_next + from_last


def put_halves(ref, at, value):
    for half in range(2):
        ref[half, at, :] = value[:, half * KMAX : (half + 1) * KMAX]


def both_halves(ref, at):
    return jnp.concatenate([ref[0, at, :], ref[1, at, :]], axis=1)


def southward(s, v):
    return DIFFUSION * s + (0.5 * v) * s


def northward(s, v):
    return DIFFUSION * s - (0.5 * v) * s


def edge_kernel(
    info_ref, cut_row_ref, s0_ref, u0_ref, v0_ref, s1_ref, u1_ref, v1_ref, ring0_ref, ring1_ref, own_ref,
):
    levels, width = own_ref.shape[1:]
    rows = cut_row_ref.shape[1]
    near = info_ref[0] < info_ref[1] // 2
    last = s1_ref.shape[1] - 1
    sides = []
    for refs, at, beyond, flow, row in (
        ((s0_ref, u0_ref, v0_ref), 0, 1, northward, 0),
        ((s1_ref, u1_ref, v1_ref), last, last - 1, southward, rows - 1),
    ):
        cut = cut_row_ref[:, row : row + 1]
        s, u, v = (ref[:, at, :] for ref in refs)
        tail = jnp.broadcast_to(cut.astype(F32), (levels, width - s.shape[1]))
        parts = [padded(u, width), padded(v, width), padded(flow(refs[0][:, beyond, :], refs[2][:, beyond, :]), width)]
        sides.append([jnp.concatenate([s, tail], axis=1), *parts])
    own_ref[0] = padded(northward(s0_ref[:, 0, :], v0_ref[:, 0, :]), width)
    own_ref[1] = padded(southward(s1_ref[:, last, :], v1_ref[:, last, :]), width)
    for i in range(4):
        ring0_ref[i] = jnp.where(near, sides[1][i], sides[0][i])
        ring1_ref[i] = jnp.where(near, sides[0][i], sides[1][i])


def level_copies(hbm_refs, buffers, sem, first, level):
    return [
        pltpu.make_async_copy(h.at[first + level], b.at[level], sem.at[q, level])
        for q, (h, b) in enumerate(zip(hbm_refs, buffers))
    ]


def every(copies, act):
    for copy in copies:
        getattr(copy, act)()


def group_store(buffer, hbm_ref, sem, first, i):
    return pltpu.make_async_copy(
        buffer.at[pl.ds(i * GROUP, GROUP)], hbm_ref.at[pl.ds(first + i * GROUP, GROUP)], sem.at[i]
    )


def is_diagonal(rows, lanes):
    lane = lax.broadcasted_iota(jnp.int32, (rows, lanes), 1)
    return lax.broadcasted_iota(jnp.int32, (rows, lanes), 0) == lax.rem(lane, rows)


def outflow(tile, cells, width):
    rows = tile.shape[0]
    at = cells - (width - 128)
    lane = lax.broadcasted_iota(jnp.int32, tile.shape, 1)
    both = jnp.where(lane < rows, tile[:, at : at + 1], tile[:, 127:128])
    return jnp.sum(jnp.where(is_diagonal(*tile.shape), both, 0.0), axis=0, keepdims=True)


def column(row):
    rows = row.shape[1]
    spread = jnp.broadcast_to(row, (rows, rows))
    return jnp.sum(jnp.where(is_diagonal(rows, rows), spread, 0.0), axis=1, keepdims=True)


def pack_rows(cut_ref, source_ref, first, out_ref):
    rows = cut_ref.shape[0]

    def body(r, unit):
        cut = cut_ref[r]
        for half in range(2):
            out_ref[unit + half] = source_ref[half, pl.ds(r, SUB, stride=rows), :]
        return unit + (cut >= 0).astype(jnp.int32) + (cut >= HALF).astype(jnp.int32)

    lax.fori_loop(0, rows, body, first, unroll=8)


def scaled(x, half, cut, total):
    lane = lax.broadcasted_iota(jnp.int32, (SUB, KMAX), 1)
    wave = half * HALF + lane % HALF
    scale = jnp.where(wave == 0, 1.0 / total, 2.0 / total)
    return jnp.where(wave <= cut, x * scale, 0.0)


def unpack_rows(cut_ref, a_ref, b_ref, first, total, out_ref):
    rows = cut_ref.shape[0]
    last = a_ref.shape[0] - 1

    def body(r, unit):
        cut = cut_ref[r]
        for half in range(2):
            at = jnp.minimum(unit + half, last)
            out_ref[half, pl.ds(r, SUB, stride=rows), :] = scaled(a_ref[at] + b_ref[at], half, cut, total)
        return unit + (cut >= 0).astype(jnp.int32) + (cut >= HALF).astype(jnp.int32)

    lax.fori_loop(0, rows, body, first, unroll=8)


def put_slots(out_ref, first, ways, lon, value):
    for i in range(ways):
        out_ref[first + i] = jnp.zeros(value.shape, F32)
    out_ref[first + lon] = value


def inflow(a_ref, b_ref, first, ways, lon, rows, place_ref):
    west, east = first + lax.rem(lon + ways - 1, ways), first + lax.rem(lon + 1, ways)
    lane = lax.broadcasted_iota(jnp.int32, (SUB, 2 * rows), 1)
    place_ref[...] = jnp.where(lane < rows, a_ref[west] + b_ref[west], a_ref[east] + b_ref[east])


def loop(count, body):
    def step(i, _):
        body(i)
        return 0

    lax.fori_loop(0, count, step, 0)


def project_groups(x_ref, table_ref, coef_ref):
    levels, rows, width = x_ref.shape

    def body(i):
        x = x_ref[pl.ds(i * GROUP, GROUP)].reshape(GROUP * rows, width)
        put_halves(coef_ref, pl.ds(i * GROUP * rows, GROUP * rows), project(x, table_ref[...]))

    loop(levels // GROUP, body)


def first_body(first, cells, hbm_refs, buffers, sem, moved_ref, coef_ref, edge_ref, table_ref, ready=None):
    levels, rows, width = moved_ref.shape

    def one(level):
        every(level_copies(hbm_refs, buffers, sem, first, level), "wait")
        moved_ref[level] = moved_rows(*[padded(b[level], width) for b in buffers])
        edge_ref[pl.ds(level, 1), :] = outflow(moved_ref[level, :, width - 128 :], cells, width)

    loop(levels, one)
    if ready is not None:
        ready.wait()
    project_groups(moved_ref, table_ref, coef_ref)


def first_kernel(
    first, cells, info_ref, s_ref, u_ref, v_ref, tables_ref, backs_ref,
    moved_ref, coef_ref, edge_ref, table_ref, back_ref, s_buf, u_buf, v_buf, sem, table_sem,
):
    hbm_refs, buffers = (s_ref, u_ref, v_ref), (s_buf, u_buf, v_buf)
    lon = info_ref[0]
    ready = pltpu.make_async_copy(tables_ref.at[lon], table_ref, table_sem.at[0])
    later = pltpu.make_async_copy(backs_ref.at[lon], back_ref, table_sem.at[1])
    loop(SUB, lambda level: every(level_copies(hbm_refs, buffers, sem, first, level), "start"))
    ready.start()
    later.start()
    first_body(first, cells, hbm_refs, buffers, sem, moved_ref, coef_ref, edge_ref, table_ref, ready)
    later.wait()


def join_flows(first, cells, info_ref, own_ref, ring0_ref, ring1_ref, flow_ref, edge_v_ref, edge_cut_ref):
    levels, width = flow_ref.shape[1:]
    at = slice(first, first + levels)
    near = info_ref[0] < info_ref[1] // 2
    lane = lax.broadcasted_iota(jnp.int32, (levels, width), 1)
    for side in range(2):
        got = [jnp.where(near == (side == 0), ring0_ref[i, at, :], ring1_ref[i, at, :]) for i in range(4)]
        edge_cut_ref[side] = jnp.broadcast_to(got[0][:, cells : cells + 1], (levels, KMAX))
        s = jnp.where(lane < cells, got[0], 0.0)
        pole = info_ref[2] == (0 if side == 0 else info_ref[3] - 1)
        v = jnp.where(pole, -got[2], got[2])
        edge_v_ref[side] = v
        flow_ref[side] = southward(s, v) if side == 0 else northward(s, v)
        flow_ref[2 + side] = along_lon(s, got[1]) + got[3] + own_ref[side, at, :]


def join_body(cells, info_ref, cut_ref, ways, coef_ref, edge_ref, flow_ref, table_ref, out_ref):
    rows = cut_ref.shape[0]
    levels, width = flow_ref.shape[1:]
    lon = info_ref[0]
    extra = project(flow_ref[...].reshape(4 * levels, width), table_ref[...])
    first = pl.ds(0, SUB, stride=rows)
    last = pl.ds(rows - 1, SUB, stride=rows)
    for half in range(2):
        part = extra[:, half * KMAX : (half + 1) * KMAX]
        coef_ref[half, first, :] = coef_ref[half, first, :] + part[:levels]
        coef_ref[half, last, :] = coef_ref[half, last, :] + part[levels : 2 * levels]
        out_ref[half] = part[2 * levels : 3 * levels]
        out_ref[2 + half] = part[3 * levels :]
    put_slots(out_ref, 4, ways, lon, edge_ref[...])
    lane = lax.broadcasted_iota(jnp.int32, (SUB, KMAX), 1)
    unit = jnp.zeros((SUB, KMAX), F32)
    for side in range(2):
        for way, at in enumerate((cells, width - 1)):
            unit = jnp.where(lane == 4 * lon + 2 * side + way, flow_ref[2 + side][:, at : at + 1], unit)
    out_ref[4 + ways] = unit
    pack_rows(cut_ref, coef_ref, 5 + ways, out_ref)


def join_kernel(
    first, cells, ways,
    info_ref, cut_ref, coef_in_ref, edge_ref, own_ref, ring0_ref, ring1_ref, table_ref,
    flow_ref, edge_v_ref, edge_cut_ref, out_ref, coef_ref,
):
    coef_ref[...] = coef_in_ref[...]
    join_flows(first, cells, info_ref, own_ref, ring0_ref, ring1_ref, flow_ref, edge_v_ref, edge_cut_ref)
    join_body(cells, info_ref, cut_ref, ways, coef_ref, edge_ref, flow_ref, table_ref, out_ref)


def first_join_kernel(
    first, cells, ways,
    info_ref, cut_ref, s_ref, u_ref, v_ref, own_ref, ring0_ref, ring1_ref, table_ref,
    moved_ref, flow_ref, edge_v_ref, edge_cut_ref, out_ref,
    s_buf, u_buf, v_buf, coef_ref, edge_ref, sem,
):
    hbm_refs, buffers = (s_ref, u_ref, v_ref), (s_buf, u_buf, v_buf)
    loop(SUB, lambda level: every(level_copies(hbm_refs, buffers, sem, first, level), "start"))
    join_flows(first, cells, info_ref, own_ref, ring0_ref, ring1_ref, flow_ref, edge_v_ref, edge_cut_ref)
    first_body(first, cells, hbm_refs, buffers, sem, moved_ref, coef_ref, edge_ref, table_ref)
    join_body(cells, info_ref, cut_ref, ways, coef_ref, edge_ref, flow_ref, table_ref, out_ref)


def closed(x, west, east, cells):
    end = x.shape[1] - 128
    lane = lax.broadcasted_iota(jnp.int32, (x.shape[0], 128), 1)
    head = x[:, :128] + jnp.where(lane == 0, west, 0.0)
    tail = x[:, end:] + jnp.where(lane == cells - 1 - end, east, 0.0)
    return jnp.concatenate([head, x[:, 128:end], jnp.where(lane < cells - end, tail, 0.0)], axis=1)


def closed_groups(cells, cut_row_ref, in_ref, coef_ref, back_ref, moved_ref, flow_ref, out_ref, after=None):
    levels, rows, width = moved_ref.shape
    filtered = column(cut_row_ref[...].astype(F32)) >= 0.0
    row = lax.broadcasted_iota(jnp.int32, (8, width), 0)

    def body(i):
        smooth = rebuild(both_halves(coef_ref, pl.ds(i * GROUP * rows, GROUP * rows)), back_ref[...])
        for g in range(GROUP):
            level = i * GROUP + g
            came = in_ref[pl.ds(level, 1), :]
            plain = closed(moved_ref[level], column(came[:, :rows]), column(came[:, rows:]), cells)
            s = jnp.where(filtered, smooth[g * rows : (g + 1) * rows], plain)
            out_ref[level] = s[:, : out_ref.shape[2]]
            if flow_ref is not None:
                for side, at, edge in ((0, 0, 0), (1, rows - 8, 7)):
                    plain_edge = (row == edge) & jnp.logical_not(filtered[at : at + 8])
                    out_ref[level, at : at + 8, :] = out_ref[level, at : at + 8, :] + jnp.where(
                        plain_edge, flow_ref[side, pl.ds(level, 1), :], 0.0
                    )
        if after is not None:
            after(i)

    loop(levels // GROUP, body)


def second_kernel(
    first, total, cells, ways,
    info_ref, cut_ref, cut_row_ref, a_ref, b_ref, flow_ref, edge_v_ref, edge_cut_ref,
    moved_ref, table_ref, back_ref, u_ref, v_ref,
    out_ref, pay_ref,
    coef_ref, sum_ref, step_ref, edge_ref, in_ref, place_ref, s_ref, u_buf, v_buf, sem,
):
    rows = cut_ref.shape[0]
    levels, _, width = out_ref.shape
    lon = info_ref[0]

    def copies(level):
        return level_copies((u_ref, v_ref), (u_buf, v_buf), sem, first, level)

    loop(levels, lambda level: every(copies(level), "start"))
    unpack_rows(cut_ref, a_ref, b_ref, 5 + ways, total, coef_ref)
    for side in range(2):
        for half in range(2):
            at = 2 * side + half
            cut = edge_cut_ref[side].astype(jnp.int32)
            edge_ref[side * levels : (side + 1) * levels, half * KMAX : (half + 1) * KMAX] = scaled(
                a_ref[at] + b_ref[at], half, cut, total
            )
    inflow(a_ref, b_ref, 4, ways, lon, rows, in_ref)
    unit = a_ref[4 + ways] + b_ref[4 + ways]
    lane = lax.broadcasted_iota(jnp.int32, (SUB, KMAX), 1)
    smooth = rebuild(edge_ref[...], back_ref[...])
    for side in range(2):
        came = [
            jnp.sum(jnp.where(lane == 4 * lax.rem(lon + ways + step, ways) + 2 * side + way, unit, 0.0), axis=1, keepdims=True)
            for way, step in enumerate((-1, 1))
        ]
        plain = closed(flow_ref[2 + side], came[0], came[1], cells)
        filtered = edge_cut_ref[side][:, 0:1] >= 0.0
        s = jnp.where(filtered, smooth[side * levels : (side + 1) * levels], plain)
        step_ref[side] = (southward if side == 0 else northward)(s, edge_v_ref[side])
    closed_groups(cells, cut_row_ref, in_ref, coef_ref, back_ref, moved_ref, flow_ref, s_ref)

    def one(level):
        row = pl.ds(level, 1)
        every(copies(level), "wait")
        out_ref[level] = moved_rows(s_ref[level], padded(u_buf[level], width), padded(v_buf[level], width))
        out_ref[level, 0:1, :] = out_ref[level, 0:1, :] + step_ref[0, row, :]
        out_ref[level, rows - 1 : rows, :] = out_ref[level, rows - 1 : rows, :] + step_ref[1, row, :]
        place_ref[row, :] = outflow(out_ref[level, :, width - 128 :], cells, width)

    loop(levels, one)
    project_groups(out_ref, table_ref, sum_ref)
    put_slots(pay_ref, 0, ways, lon, place_ref[...])
    pack_rows(cut_ref, sum_ref, ways, pay_ref)


def third_kernel(
    first, total, cells, ways, info_ref, cut_ref, cut_row_ref, a_ref, b_ref, moved_ref, back_ref, *refs
):
    out_ref, coef_ref, in_ref, buffer, out_sem = refs[-5:]
    rows = cut_ref.shape[0]
    levels = moved_ref.shape[0]
    unpack_rows(cut_ref, a_ref, b_ref, ways, total, coef_ref)
    inflow(a_ref, b_ref, 0, ways, info_ref[0], rows, in_ref)
    closed_groups(
        cells, cut_row_ref, in_ref, coef_ref, back_ref, moved_ref, None, buffer,
        lambda i: group_store(buffer, out_ref, out_sem, first, i).start(),
    )
    loop(levels // GROUP, lambda i: group_store(buffer, out_ref, out_sem, first, i).wait())


SMEM = pl.BlockSpec(memory_space=pltpu.SMEM)
VMEM = pl.BlockSpec(memory_space=pltpu.VMEM)
HBM = pl.BlockSpec(memory_space=pltpu.HBM)


def shape(*dims, dtype=F32):
    return jax.ShapeDtypeStruct(dims, dtype)


def call(kernel, inputs, outputs, scratch, mib, aliases=None):
    return pl.pallas_call(
        kernel,
        in_specs=[spec for _, spec in inputs],
        out_specs=[spec for _, spec in outputs],
        out_shape=[what for what, _ in outputs],
        scratch_shapes=scratch,
        input_output_aliases=aliases or {},
        compiler_params=pltpu.CompilerParams(vmem_limit_bytes=mib * MIB),
    )(*[array for array, _ in inputs])


def swap(x, bit):
    count = lax.axis_size("lon")
    return lax.ppermute(x, "lon", [(i, i ^ (1 << bit)) for i in range(count)])


def sum_over_lon(x, upward):
    bits = lax.axis_size("lon").bit_length() - 1
    for i in range(bits):
        got = swap(x, i if upward else bits - 1 - i)
        if i == bits - 1:
            return x, got
        x = x + got


def lat_ring(bands, ways, turn):
    pairs = []
    for band in range(bands):
        for l in range(ways):
            east = l < ways // 2
            other = (l + ways // 2) % ways
            step = 1 if east == (turn == 0) else -1
            to = (band + step, l) if 0 <= band + step < bands else (band, other)
            pairs.append((l * bands + band, to[1] * bands + to[0]))
    return pairs


def on_device(tracer, zonal, meridional, cutoff_wave, polar_mask):
    levels, rows, cells = tracer.shape
    ways, bands = lax.axis_size("lon"), lax.axis_size("lat")
    width = wide(cells)
    total = cells * ways
    tables, backs = (jnp.asarray(x) for x in wave_tables(cells, ways))
    lon, band = lax.axis_index("lon"), lax.axis_index("lat")
    info = jnp.stack([lon, jnp.int32(ways), band, jnp.int32(bands)]).astype(jnp.int32)
    parts = levels // SUB
    steps = SUB // GROUP
    winds = (tracer, zonal, meridional)
    cut = jnp.where(polar_mask == 1, cutoff_wave, -1)
    cut_row = cut[None, :]

    top = pl.BlockSpec((levels, SUB, cells), lambda i: (0, 0, 0))
    bottom = pl.BlockSpec((levels, SUB, cells), lambda i: (0, rows // SUB - 1, 0))
    full = pl.BlockSpec((4, levels, width), lambda i: (0, 0, 0))
    ring0, ring1, own = pl.pallas_call(
        edge_kernel,
        grid=(1,),
        in_specs=[SMEM, pl.BlockSpec((1, rows), lambda i: (0, 0)), top, top, top, bottom, bottom, bottom],
        out_specs=[full, full, pl.BlockSpec((2, levels, width), lambda i: (0, 0, 0))],
        out_shape=[shape(4, levels, width), shape(4, levels, width), shape(2, levels, width)],
        compiler_params=pltpu.CompilerParams(vmem_limit_bytes=FIRST_MIB * MIB),
    )(info, cut_row, *winds, *winds)
    later, ring0 = lax.optimization_barrier((cut_row, ring0))
    kept = jnp.sum((later >= 0).astype(jnp.int32) + (later >= HALF).astype(jnp.int32))
    ring = ("lon", "lat")
    got0 = lax.ppermute(ring0, ring, lat_ring(bands, ways, 0))
    got1 = lax.ppermute(ring1, ring, lat_ring(bands, ways, 1))

    grid = shape(SUB, rows, width)
    coef = shape(2, SUB * rows, KMAX)
    edge = shape(SUB, KMAX)
    flows = [(shape(4, SUB, width), VMEM), (shape(2, SUB, width), VMEM), (shape(2, SUB, KMAX), VMEM)]
    head = 5 + ways

    def room(what):
        return pltpu.VMEM(what.shape, what.dtype)

    buffer = pltpu.VMEM((SUB, rows, cells), F32)
    table_shape, back_shape = (shape(*x.shape[1:], dtype=BF16) for x in (tables, backs))
    sems = pltpu.SemaphoreType.DMA
    moved_a, coef_a, edge_a, table, back = call(
        functools.partial(first_kernel, 0, cells),
        [(info, SMEM), *[(x, HBM) for x in (*winds, tables, backs)]],
        [(x, VMEM) for x in (grid, coef, edge, table_shape, back_shape)],
        [buffer, buffer, buffer, sems((3, SUB)), sems((2,))],
        FIRST_MIB,
    )

    def rest(limit, info, cut, cut_row, tracer, zonal, meridional, own, got0, got1, moved_a, coef_a, edge_a, table, back):
        pay = (shape(limit + head + 2, SUB, KMAX), VMEM)
        around = [(x, VMEM) for x in (own, got0, got1, table)]
        scalars = [(info, SMEM), (cut, SMEM)]
        joined = [(moved_a, *call(
            functools.partial(join_kernel, 0, cells, ways),
            [*scalars, (coef_a, VMEM), (edge_a, VMEM), *around],
            [*flows, pay],
            [room(coef)],
            8,
        ))]
        sums = [sum_over_lon(joined[0][4], True)]
        for part in range(1, parts):
            joined.append(call(
                functools.partial(first_join_kernel, part * SUB, cells, ways),
                [*scalars, *[(x, HBM) for x in (tracer, zonal, meridional)], *around],
                [(grid, VMEM), *flows, pay],
                [buffer, buffer, buffer, room(coef), room(edge), sems((3, SUB))],
                20,
            ))
            sums.append(sum_over_lon(joined[part][4], True))
        seconds = []
        for part in range(parts):
            moved, flow, edge_v, edge_cut, _ = joined[part]
            seconds.append(call(
                functools.partial(second_kernel, part * SUB, total, cells, ways),
                [*scalars, *[(x, VMEM) for x in (cut_row, *sums[part], flow, edge_v, edge_cut, moved, table, back)],
                 (zonal, HBM), (meridional, HBM)],
                [(grid, VMEM), (shape(limit + ways + 2, SUB, KMAX), VMEM)],
                [room(coef), room(coef), pltpu.VMEM((2, SUB, width), F32),
                 pltpu.VMEM((2 * SUB, 2 * KMAX), F32), room(edge), room(edge), room(grid), buffer, buffer, sems((2, SUB))],
                20,
            ))
        sums = [sum_over_lon(x[1], True) for x in seconds]
        out = []
        for part in range(parts):
            out = call(
                functools.partial(third_kernel, part * SUB, total, cells, ways),
                [*scalars, *[(x, VMEM) for x in (cut_row, *sums[part], seconds[part][0], back)],
                 *[(x, HBM) for x in out]],
                [(shape(levels, rows, cells), HBM)],
                [room(coef), room(edge), buffer, sems((steps,))],
                12,
                {7: 0} if part else None,
            )
        return out[0]

    limits = sorted({min(-(-x * rows // 64), 2 * rows) for x in LIMITS})
    choice = sum((kept > x).astype(jnp.int32) for x in limits[:-1])
    return lax.switch(
        choice, [functools.partial(rest, x) for x in limits],
        info, cut, cut_row, tracer, zonal, meridional, own, got0, got1, moved_a, coef_a, edge_a, table, back,
    )


def solution(mesh):
    placed = (
        P(None, "lat", "lon"),
        P(None, "lat", "lon"),
        P(None, "lat", "lon"),
        P("lat"),
        P("lat"),
    )
    return jax.shard_map(
        on_device, mesh=mesh, in_specs=placed, out_specs=P(None, "lat", "lon"), check_vma=False
    )
```

time: 129 us -> 94.3 us (0.73); the launches traced: 127 us -> 94.1 us
  loops' own time: 16.6 us -> 0.36 us
  waiting for transfers between devices: 33.3 us -> 23.6 us
  local copies, waits for them, and re-layouts: 2.98 us -> 0.04 us
  between operations: 3.33 us -> 0.86 us
  Pallas kernels: 57.9 us -> 56.2 us
    another operation x1, loops' own time: 16.6 us -> 0.36 us  [on_device(): lax.switch(choice, [functools.partial(rest, x) for x in limits], info, cu...]
    ppermute x8, waiting for transfers between devices: 33.3 us -> 23.6 us  [swap(): return lax.ppermute(x, 'lon', [(i, i ^ 1 << bit) for i in range(count)])]
    pallas_call x7, Pallas kernels: 55.3 us -> 53.4 us  [call(): pl.pallas_call(kernel, in_specs=[spec for _, spec in inputs], out_specs=[...]
    cond x4 -> x16, local copies, waits for them, and re-layouts: 1.67 us -> 0.04 us
    unnamed x4 -> x0, local copies, waits for them, and re-layouts: 1.31 us -> none
  transfers between devices with their start and end apart: 10 -> 10, of which waited for: 4 -> 4; matrix products, arithmetic and copies ran while one was open for 1% -> 1% of each run, Pallas kernels for 37% -> 50%
where the time goes in v1:
time: 94.3 us; the launch traced here: 94.1 us
  Pallas kernels  56.2 us (60%)
  waiting for transfers between devices  23.6 us (25%)
  starting transfers between devices  11.4 us (12%)
  other arithmetic  1.57 us (2%)
    pallas_call x7, Pallas kernels, call(): pl.pallas_call(kernel, in_specs=[spec for _, spec in inputs], out_specs=[...  53.4 us
    ppermute x8, waiting for transfers between devices, swap(): return lax.ppermute(x, 'lon', [(i, i ^ 1 << bit) for i in range(count)])  23.6 us
    ppermute x8, starting transfers between devices, swap(): return lax.ppermute(x, 'lon', [(i, i ^ 1 << bit) for i in range(count)])  8.34 us
    pallas_call x1, Pallas kernels, on_device(): pl.pallas_call(edge_kernel, grid=(1,), in_specs=[SMEM, pl.BlockSpec((1, r...  2.79 us
    ppermute x1, starting transfers between devices, on_device(): got1 = lax.ppermute(ring1, ring, lat_ring(bands, ways, 1))  2.59 us
  transfers between devices with their start and end apart: 10, of which 4 were waited for; matrix products, arithmetic and copies ran while one was open for 1% of the time, Pallas kernels for 50%

profile of v1, /device:TPU:0, one launch (start us, length us, event | category | flops | bytes accessed | tf_op | source)
XLA Modules:
  0.0 94.1 jit_solution(9388197163728199678)
XLA Ops:
  0.0 0.7 compare_select_fusion
  0.7 0.1 pad_add_fusion.info_ref
  0.8 2.8 %shard_map.75 = (f32[4,16,1536]{2,1,0:T(8,128)S(1)}, f32[4,16,1536]{2,1,0:T(8,128)S(1)}, f32[2,16,1536]{2,1,0:T(8,128)S(1)}) custom-call(s32[4]{0:T(128)S(1)} %pad_add_fusion.info_ref, s32[1,64]{1,0:T(1,128)S(1)} %bitcast.11, f32[16,64,1440]{2,1,0:T(8,128)} %s_ref.1, f32[16,64,1440]{2,1,0:T(8,128)} %u_ref.1, f32[16,64,1440]{2,1,0:T(8,128)} %v_ref.1, ...), custom_call_target="tpu_custom_call" | custom-call | tf_op jit(solution)/shard_map/pallas_call | solution.py:492
  3.6 0.5 collective-permute-start.16
  4.1 2.6 %collective-permute-start.17 = (f32[4,16,1536]{2,1,0:T(8,128)S(1)}, f32[4,16,1536]{2,1,0:T(8,128)S(1)}, u32[]{:S(2)}, u32[]{:S(2)}) collective-permute-start(f32[4,16,1536]{2,1,0:T(8,128)S(1)} %get-tuple-element.132), channel_id=1, source_target_pairs={{0,16},{8,24},{16,17},{24,25},{1,0},{9,8},{17,18},{25,26},{2,1},{1... | collective-permute-start | bytes 1179656 | tf_op jit(solution)/shard_map/ppermute | solution.py:504
  6.6 0.6 fusion.1
  7.9 9.0 %shard_map.76 = (f32[8,64,1536]{2,1,0:T(8,128)}, f32[2,512,128]{2,1,0:T(8,128)}, f32[8,128]{1,0:T(8,128)S(1)}, bf16[1536,512]{1,0:T(8,128)(2,1)}, bf16[512,1536]{1,0:T(8,128)(2,1)S(1)}) custom-call(s32[4]{0:T(128)S(1)} %pad_add_fusion.info_ref, f32[16,64,1440]{2,1,0:T(8,128)} %s_ref.1, f32[16,64,1440]{2,1,0:T(8,128)} %u_ref.1, f32[16,64,1440]{2,1,0:T(8,128)} %v_ref.1, ...), custom_call_target="tpu_custom_call" | custom-call | tf_op jit(solution)/shard_map/pallas_call | solution.py:438
  17.0 0.0 collective-permute-done.17
  17.0 77.0 %conditional.1 = (f32[16,64,1440]{2,1,0:T(8,128)}) conditional(s32[]{:T(128)} %clamp.3, (s32[4]{0:T(128)S(1)}, s32[64]{0:T(128)S(1)}, f32[16,64,1440]{2,1,0:T(8,128)}, f32[16,64,1440]{2,1,0:T(8,128)}, f32[16,64,1440]{2,1,0:T(8,128)}, /*index=5*/f32[2,16,1536]{2,1,0:T(8,128)S(1)}, f32[4,16,1536]{2,1,0:T(8,128)S(1)}, f32[4,16,1536]{2,1,0:T(8,128)S(1)}, ...), branch_computations={%region_1.2_spmd, %region_2.3_spmd} | conditional | flops 559104 | bytes 83583512 | solution.py:575
  17.0 0.0 copy-start.4
  17.0 2.8 %branch_0_fun.8 = (f32[4,8,1536]{2,1,0:T(8,128)S(1)}, f32[2,8,1536]{2,1,0:T(8,128)S(1)}, f32[2,8,128]{2,1,0:T(8,128)S(1)}, f32[103,8,128]{2,1,0:T(8,128)S(1)}) custom-call(s32[4]{0:T(128)S(1)} %get-tuple-element.64.info_ref, s32[64]{0:T(128)S(1)} %bitcast.15, f32[2,512,128]{2,1,0:T(8,128)} %get-tuple-element.82.coef_in_ref, ...), custom_call_target="tpu_custom_call" | custom-call | tf_op jit(solution)/shard_map/cond/branch_0_fun/pallas_call | solution.py:438
  19.8 2.0 %collective-permute-start.4 = (f32[103,8,128]{2,1,0:T(8,128)S(1)}, f32[103,8,128]{2,1,0:T(8,128)S(1)}, u32[]{:S(2)}, u32[]{:S(2)}) collective-permute-start(f32[103,8,128]{2,1,0:T(8,128)S(1)} %get-tuple-element.84), channel_id=1, source_target_pairs={{0,8},{8,0},{16,24},{24,16},{1,9},{9,1},{17,25},{25,17},{2,10},{10... | collective-permute-start | bytes 1265672 | tf_op jit(solution)/shard_map/cond/branch_0_fun/ppermute | solution.py:451
  21.8 0.0 slice-start.1
  21.8 0.0 slice-start.5
  21.8 9.6 %branch_0_fun.6 = (f32[8,64,1536]{2,1,0:T(8,128)S(1)}, f32[4,8,1536]{2,1,0:T(8,128)S(1)}, f32[2,8,1536]{2,1,0:T(8,128)S(1)}, f32[2,8,128]{2,1,0:T(8,128)S(1)}, f32[103,8,128]{2,1,0:T(8,128)S(1)}) custom-call(s32[4]{0:T(128)S(1)} %get-tuple-element.64.info_ref, s32[64]{0:T(128)S(1)} %bitcast.16, f32[16,64,1440]{2,1,0:T(8,128)} %get-tuple-element.67.s_ref, ...), custom_call_target="tpu_custom_call" | custom-call | tf_op jit(solution)/shard_map/cond/branch_0_fun/pallas_call | solution.py:438
  31.4 0.2 collective-permute-start
  31.6 0.0 collective-permute-done.4
  31.6 1.1 %collective-permute-start.5 = (f32[103,8,128]{2,1,0:T(8,128)S(1)}, f32[103,8,128]{2,1,0:T(8,128)S(1)}, u32[]{:S(2)}, u32[]{:S(2)}) collective-permute-start(f32[103,8,128]{2,1,0:T(8,128)S(1)} %add.20.a_ref), channel_id=1, source_target_pairs={{0,16},{8,24},{16,0},{24,8},{1,17},{9,25},{17,1},{25,9},{2,18},{10... | collective-permute-start | bytes 1265672 | tf_op jit(solution)/shard_map/cond/branch_0_fun/ppermute | solution.py:451
  32.7 9.8 %collective-permute-done = f32[103,8,128]{2,1,0:T(8,128)S(1)} collective-permute-done((f32[103,8,128]{2,1,0:T(8,128)S(1)}, f32[103,8,128]{2,1,0:T(8,128)S(1)}, u32[]{:S(2)}, u32[]{:S(2)}) %collective-permute-start) | collective-permute-done | bytes 421920 | tf_op jit(solution)/shard_map/cond/branch_0_fun/ppermute | solution.py:451
  42.5 1.7 %collective-permute-start.1 = (f32[103,8,128]{2,1,0:T(8,128)S(1)}, f32[103,8,128]{2,1,0:T(8,128)S(1)}, u32[]{:S(2)}, u32[]{:S(2)}) collective-permute-start(f32[103,8,128]{2,1,0:T(8,128)S(1)} %add.18.a_ref), channel_id=1, source_target_pairs={{0,16},{8,24},{16,0},{24,8},{1,17},{9,25},{17,1},{25,9},{2,18},{10... | collective-permute-start | bytes 1265672 | tf_op jit(solution)/shard_map/cond/branch_0_fun/ppermute | solution.py:451
  44.3 12.0 %branch_0_fun.9 = (f32[8,64,1536]{2,1,0:T(8,128)S(1)}, f32[98,8,128]{2,1,0:T(8,128)S(1)}) custom-call(s32[4]{0:T(128)S(1)} %get-tuple-element.64.info_ref, s32[64]{0:T(128)S(1)} %bitcast.17, s32[1,64]{1,0:T(1,128)S(1)} %get-tuple-element.66.cut_row_ref, f32[103,8,128]{2,1,0:T(8,128)S(1)} %add.20.a_ref, f32[103,8,128]{2,1,0:T(8,128)S(1)} %collective-permute-done.5.b_ref, ...), custom_call_target="tpu_custom_call" | custom-call | tf_op jit(solution)/shard_map/cond/branch_0_fun/pallas_call | solution.py:438
  56.3 0.6 collective-permute-start.6
  56.8 12.1 %branch_0_fun.7 = (f32[8,64,1536]{2,1,0:T(8,128)S(1)}, f32[98,8,128]{2,1,0:T(8,128)S(1)}) custom-call(s32[4]{0:T(128)S(1)} %get-tuple-element.64.info_ref, s32[64]{0:T(128)S(1)} %bitcast.18, s32[1,64]{1,0:T(1,128)S(1)} %get-tuple-element.66.cut_row_ref, f32[103,8,128]{2,1,0:T(8,128)S(1)} %add.18.a_ref, f32[103,8,128]{2,1,0:T(8,128)S(1)} %collective-permute-done.1.b_ref, ...), custom_call_target="tpu_custom_call" | custom-call | tf_op jit(solution)/shard_map/cond/branch_0_fun/pallas_call | solution.py:438
  68.9 1.6 %collective-permute-start.2 = (f32[98,8,128]{2,1,0:T(8,128)S(1)}, f32[98,8,128]{2,1,0:T(8,128)S(1)}, u32[]{:S(2)}, u32[]{:S(2)}) collective-permute-start(f32[98,8,128]{2,1,0:T(8,128)S(1)} %get-tuple-element.80), channel_id=1, source_target_pairs={{0,8},{8,0},{16,24},{24,16},{1,9},{9,1},{17,25},{25,17},{2,10},{10... | collective-permute-start | bytes 1204232 | tf_op jit(solution)/shard_map/cond/branch_0_fun/ppermute | solution.py:451
  70.5 0.5 collective-permute-start.7
  71.1 8.7 %collective-permute-done.2 = f32[98,8,128]{2,1,0:T(8,128)S(1)} collective-permute-done((f32[98,8,128]{2,1,0:T(8,128)S(1)}, f32[98,8,128]{2,1,0:T(8,128)S(1)}, u32[]{:S(2)}, u32[]{:S(2)}) %collective-permute-start.2) | collective-permute-done | bytes 401440 | tf_op jit(solution)/shard_map/cond/branch_0_fun/ppermute | solution.py:451
  79.7 0.1 add.19.a_ref
  79.8 0.8 collective-permute-start.3
  80.6 0.5 collective-permute-done.7.b_ref
  81.1 4.0 %branch_0_fun.10.refs_0_ = f32[16,64,1440]{2,1,0:T(8,128)} custom-call(s32[4]{0:T(128)S(1)} %get-tuple-element.64.info_ref, s32[64]{0:T(128)S(1)} %bitcast.19, s32[1,64]{1,0:T(1,128)S(1)} %get-tuple-element.66.cut_row_ref, f32[98,8,128]{2,1,0:T(8,128)S(1)} %add.21.a_ref, f32[98,8,128]{2,1,0:T(8,128)S(1)} %collective-permute-done.7.b_ref, ...), custom_call_target="tpu_custom_call" | custom-call | tf_op jit(solution)/shard_map/cond/branch_0_fun/pallas_call | solution.py:438
  85.1 4.6 %collective-permute-done.3.b_ref = f32[98,8,128]{2,1,0:T(8,128)S(1)} collective-permute-done((f32[98,8,128]{2,1,0:T(8,128)S(1)}, f32[98,8,128]{2,1,0:T(8,128)S(1)}, u32[]{:S(2)}, u32[]{:S(2)}) %collective-permute-start.3) | collective-permute-done | bytes 401440 | tf_op jit(solution)/shard_map/cond/branch_0_fun/ppermute | solution.py:451
  89.7 4.0 %branch_0_fun.11 = f32[16,64,1440]{2,1,0:T(8,128)} custom-call(s32[4]{0:T(128)S(1)} %get-tuple-element.64.info_ref, s32[64]{0:T(128)S(1)} %bitcast.20, s32[1,64]{1,0:T(1,128)S(1)} %get-tuple-element.66.cut_row_ref, f32[98,8,128]{2,1,0:T(8,128)S(1)} %add.19.a_ref, f32[98,8,128]{2,1,0:T(8,128)S(1)} %collective-permute-done.3.b_ref, ...), custom_call_target="tpu_custom_call", output_to_operand_aliasing={{}: (7, {})} | custom-call | tf_op jit(solution)/shard_map/cond/branch_0_fun/pallas_call | solution.py:438
  (22 shorter events, 0.2 us)
Async XLA Ops:
  3.6 13.4 %collective-permute-start.16 = (f32[4,16,1536]{2,1,0:T(8,128)S(1)}, f32[4,16,1536]{2,1,0:T(8,128)S(1)}, u32[]{:S(2)}, u32[]{:S(2)}) collective-permute-start(f32[4,16,1536]{2,1,0:T(8,128)S(1)} %get-tuple-element.131), channel_id=1, source_target_pairs={{0,1},{8,9},{16,0},{24,8},{1,2},{9,10},{17,16},{25,24},{2,3},{10,1... | collective-permute-start | bytes 1179656 | tf_op jit(solution)/shard_map/ppermute | solution.py:503
  4.1 12.9 %collective-permute-start.17 = (f32[4,16,1536]{2,1,0:T(8,128)S(1)}, f32[4,16,1536]{2,1,0:T(8,128)S(1)}, u32[]{:S(2)}, u32[]{:S(2)}) collective-permute-start(f32[4,16,1536]{2,1,0:T(8,128)S(1)} %get-tuple-element.132), channel_id=1, source_target_pairs={{0,16},{8,24},{16,17},{24,25},{1,0},{9,8},{17,18},{25,26},{2,1},{1... | collective-permute-start | bytes 1179656 | tf_op jit(solution)/shard_map/ppermute | solution.py:504
  17.0 4.8 %copy-start.4 = (f32[4,16,1536]{2,1,0:T(8,128)}, f32[4,16,1536]{2,1,0:T(8,128)S(1)}, u32[]{:S(2)}) copy-start(f32[4,16,1536]{2,1,0:T(8,128)S(1)} %get-tuple-element.72.ring1_ref) | copy-start | bytes 1179652 | tf_op jit(solution)/shard_map/cond
  17.0 4.8 %copy-start.6 = (f32[2,16,1536]{2,1,0:T(8,128)}, f32[2,16,1536]{2,1,0:T(8,128)S(1)}, u32[]{:S(2)}) copy-start(f32[2,16,1536]{2,1,0:T(8,128)S(1)} %get-tuple-element.70.own_ref) | copy-start | bytes 589828 | tf_op jit(solution)/shard_map/cond
  19.8 11.8 %collective-permute-start.4 = (f32[103,8,128]{2,1,0:T(8,128)S(1)}, f32[103,8,128]{2,1,0:T(8,128)S(1)}, u32[]{:S(2)}, u32[]{:S(2)}) collective-permute-start(f32[103,8,128]{2,1,0:T(8,128)S(1)} %get-tuple-element.84), channel_id=1, source_target_pairs={{0,8},{8,0},{16,24},{24,16},{1,9},{9,1},{17,25},{25,17},{2,10},{10... | collective-permute-start | bytes 1265672 | tf_op jit(solution)/shard_map/cond/branch_0_fun/ppermute | solution.py:451
  21.8 22.4 %slice-start = ((s8[6291456]{0:T(1024)(128)(4,1)}), s8[4194304]{0:T(1024)(128)(4,1)S(1)}, s32[]{:S(2)}) async-start(s8[6291456]{0:T(1024)(128)(4,1)} %bitcast.3), calls=%async_computation | async-start | bytes 8388608 | tf_op jit(solution)/shard_map/cond
  21.8 22.4 %slice-start.4 = ((s8[6291456]{0:T(1024)(128)(4,1)}), s8[4194304]{0:T(1024)(128)(4,1)S(1)}, s32[]{:S(2)}) async-start(s8[6291456]{0:T(1024)(128)(4,1)} %bitcast.7), calls=%async_computation.4 | async-start | bytes 8388608 | tf_op jit(solution)/shard_map/cond
  21.8 22.4 %slice-start.1 = ((s8[6291456]{0:T(1024)(128)(4,1)}), s8[2097152]{0:T(1024)(128)(4,1)S(1)}, s32[]{:S(2)}) async-start(s8[6291456]{0:T(1024)(128)(4,1)} %bitcast.3), calls=%async_computation.1 | async-start | bytes 4194304 | tf_op jit(solution)/shard_map/cond
  21.8 22.4 %slice-start.5 = ((s8[6291456]{0:T(1024)(128)(4,1)}), s8[2097152]{0:T(1024)(128)(4,1)S(1)}, s32[]{:S(2)}) async-start(s8[6291456]{0:T(1024)(128)(4,1)} %bitcast.7), calls=%async_computation.5 | async-start | bytes 4194304 | tf_op jit(solution)/shard_map/cond
  21.8 22.4 %copy-start = (bf16[1536,512]{1,0:T(8,128)(2,1)S(1)}, bf16[1536,512]{1,0:T(8,128)(2,1)}, u32[]{:S(2)}) copy-start(bf16[1536,512]{1,0:T(8,128)(2,1)} %get-tuple-element.73.table_ref) | copy-start | bytes 4718596 | tf_op jit(solution)/shard_map/cond
  21.8 22.4 %copy-start.2 = (f32[8,64,1536]{2,1,0:T(8,128)S(1)}, f32[8,64,1536]{2,1,0:T(8,128)}, u32[]{:S(2)}) copy-start(f32[8,64,1536]{2,1,0:T(8,128)} %get-tuple-element.88.moved_ref) | copy-start | bytes 9437188 | tf_op jit(solution)/shard_map/cond
  31.4 11.1 %collective-permute-start = (f32[103,8,128]{2,1,0:T(8,128)S(1)}, f32[103,8,128]{2,1,0:T(8,128)S(1)}, u32[]{:S(2)}, u32[]{:S(2)}) collective-permute-start(f32[103,8,128]{2,1,0:T(8,128)S(1)} %get-tuple-element.74), channel_id=1, source_target_pairs={{0,8},{8,0},{16,24},{24,16},{1,9},{9,1},{17,25},{25,17},{2,10},{10... | collective-permute-start | bytes 1265672 | tf_op jit(solution)/shard_map/cond/branch_0_fun/ppermute | solution.py:451
  31.6 12.6 %collective-permute-start.5 = (f32[103,8,128]{2,1,0:T(8,128)S(1)}, f32[103,8,128]{2,1,0:T(8,128)S(1)}, u32[]{:S(2)}, u32[]{:S(2)}) collective-permute-start(f32[103,8,128]{2,1,0:T(8,128)S(1)} %add.20.a_ref), channel_id=1, source_target_pairs={{0,16},{8,24},{16,0},{24,8},{1,17},{9,25},{17,1},{25,9},{2,18},{10... | collective-permute-start | bytes 1265672 | tf_op jit(solution)/shard_map/cond/branch_0_fun/ppermute | solution.py:451
  42.5 14.3 %collective-permute-start.1 = (f32[103,8,128]{2,1,0:T(8,128)S(1)}, f32[103,8,128]{2,1,0:T(8,128)S(1)}, u32[]{:S(2)}, u32[]{:S(2)}) collective-permute-start(f32[103,8,128]{2,1,0:T(8,128)S(1)} %add.18.a_ref), channel_id=1, source_target_pairs={{0,16},{8,24},{16,0},{24,8},{1,17},{9,25},{17,1},{25,9},{2,18},{10... | collective-permute-start | bytes 1265672 | tf_op jit(solution)/shard_map/cond/branch_0_fun/ppermute | solution.py:451
  56.3 14.2 %collective-permute-start.6 = (f32[98,8,128]{2,1,0:T(8,128)S(1)}, f32[98,8,128]{2,1,0:T(8,128)S(1)}, u32[]{:S(2)}, u32[]{:S(2)}) collective-permute-start(f32[98,8,128]{2,1,0:T(8,128)S(1)} %get-tuple-element.89), channel_id=1, source_target_pairs={{0,8},{8,0},{16,24},{24,16},{1,9},{9,1},{17,25},{25,17},{2,10},{10... | collective-permute-start | bytes 1204232 | tf_op jit(solution)/shard_map/cond/branch_0_fun/ppermute | solution.py:451
  68.9 10.8 %collective-permute-start.2 = (f32[98,8,128]{2,1,0:T(8,128)S(1)}, f32[98,8,128]{2,1,0:T(8,128)S(1)}, u32[]{:S(2)}, u32[]{:S(2)}) collective-permute-start(f32[98,8,128]{2,1,0:T(8,128)S(1)} %get-tuple-element.80), channel_id=1, source_target_pairs={{0,8},{8,0},{16,24},{24,16},{1,9},{9,1},{17,25},{25,17},{2,10},{10... | collective-permute-start | bytes 1204232 | tf_op jit(solution)/shard_map/cond/branch_0_fun/ppermute | solution.py:451
  70.5 10.5 %collective-permute-start.7 = (f32[98,8,128]{2,1,0:T(8,128)S(1)}, f32[98,8,128]{2,1,0:T(8,128)S(1)}, u32[]{:S(2)}, u32[]{:S(2)}) collective-permute-start(f32[98,8,128]{2,1,0:T(8,128)S(1)} %add.21.a_ref), channel_id=1, source_target_pairs={{0,16},{8,24},{16,0},{24,8},{1,17},{9,25},{17,1},{25,9},{2,18},{10... | collective-permute-start | bytes 1204232 | tf_op jit(solution)/shard_map/cond/branch_0_fun/ppermute | solution.py:451
  79.8 9.9 %collective-permute-start.3 = (f32[98,8,128]{2,1,0:T(8,128)S(1)}, f32[98,8,128]{2,1,0:T(8,128)S(1)}, u32[]{:S(2)}, u32[]{:S(2)}) collective-permute-start(f32[98,8,128]{2,1,0:T(8,128)S(1)} %add.19.a_ref), channel_id=1, source_target_pairs={{0,16},{8,24},{16,0},{24,8},{1,17},{9,25},{17,1},{25,9},{2,18},{10... | collective-permute-start | bytes 1204232 | tf_op jit(solution)/shard_map/cond/branch_0_fun/ppermute | solution.py:451

commit v2 on v1

--- a/solution.py
+++ b/solution.py
@@ -15,7 +15,7 @@
 GROUP = 4
 SUB = 8
 FIRST_MIB = 52
-LIMITS = (92, 128)
+LIMITS = (88, 128)
 F32 = jnp.float32
 BF16 = jnp.bfloat16
 MIB = 1024 * 1024
@@ -111,24 +111,30 @@
 
 
 def edge_kernel(
-    info_ref, cut_row_ref, s0_ref, u0_ref, v0_ref, s1_ref, u1_ref, v1_ref, ring0_ref, ring1_ref, own_ref,
+    info_ref, cutoff_ref, mask_ref, s_ref, u_ref, v_ref,
+    ring0_ref, ring1_ref, own_ref, cut_ref, rows_ref, cuts_ref, sem,
 ):
     levels, width = own_ref.shape[1:]
-    rows = cut_row_ref.shape[1]
+    rows = cut_ref.shape[1]
     near = info_ref[0] < info_ref[1] // 2
-    last = s1_ref.shape[1] - 1
+    wanted = [(h, at) for at in (0, rows - 1) for h in (s_ref, u_ref, v_ref)]
+    wanted += [(h, at) for at in (1, rows - 2) for h in (s_ref, v_ref)]
+    copies = [
+        pltpu.make_async_copy(h.at[:, at, :], rows_ref.at[i], sem.at[i]) for i, (h, at) in enumerate(wanted)
+    ]
+    for i, h in enumerate((cutoff_ref, mask_ref)):
+        copies.append(pltpu.make_async_copy(h, cuts_ref.at[i], sem.at[len(wanted) + i]))
+    every(copies, "start")
+    every(copies, "wait")
+    cut = jnp.where(cuts_ref[1] == 1, cuts_ref[0], -1)
+    cut_ref[...] = cut
     sides = []
-    for refs, at, beyond, flow, row in (
-        ((s0_ref, u0_ref, v0_ref), 0, 1, northward, 0),
-        ((s1_ref, u1_ref, v1_ref), last, last - 1, southward, rows - 1),
-    ):
-        cut = cut_row_ref[:, row : row + 1]
-        s, u, v = (ref[:, at, :] for ref in refs)
-        tail = jnp.broadcast_to(cut.astype(F32), (levels, width - s.shape[1]))
-        parts = [padded(u, width), padded(v, width), padded(flow(refs[0][:, beyond, :], refs[2][:, beyond, :]), width)]
-        sides.append([jnp.concatenate([s, tail], axis=1), *parts])
-    own_ref[0] = padded(northward(s0_ref[:, 0, :], v0_ref[:, 0, :]), width)
-    own_ref[1] = padded(southward(s1_ref[:, last, :], v1_ref[:, last, :]), width)
+    for side, (flow, row) in enumerate(((northward, 0), (southward, rows - 1))):
+        s, u, v = (rows_ref[3 * side + i] for i in range(3))
+        tail = jnp.broadcast_to(cut[:, row : row + 1].astype(F32), (levels, width - s.shape[1]))
+        beyond = flow(rows_ref[6 + 2 * side], rows_ref[7 + 2 * side])
+        sides.append([jnp.concatenate([s, tail], axis=1), padded(u, width), padded(v, width), padded(beyond, width)])
+        own_ref[side] = padded(flow(s, v), width)
     for i in range(4):
         ring0_ref[i] = jnp.where(near, sides[1][i], sides[0][i])
         ring1_ref[i] = jnp.where(near, sides[0][i], sides[1][i])
@@ -249,8 +255,8 @@
 
 
 def first_kernel(
-    first, cells, info_ref, s_ref, u_ref, v_ref, tables_ref, backs_ref,
-    moved_ref, coef_ref, edge_ref, table_ref, back_ref, s_buf, u_buf, v_buf, sem, table_sem,
+    first, cells, info_ref, cut_row_ref, s_ref, u_ref, v_ref, tables_ref, backs_ref,
+    moved_ref, coef_ref, edge_ref, table_ref, back_ref, kept_ref, s_buf, u_buf, v_buf, sem, table_sem,
 ):
     hbm_refs, buffers = (s_ref, u_ref, v_ref), (s_buf, u_buf, v_buf)
     lon = info_ref[0]
@@ -259,6 +265,8 @@
     loop(SUB, lambda level: every(level_copies(hbm_refs, buffers, sem, first, level), "start"))
     ready.start()
     later.start()
+    cut = cut_row_ref[...]
+    kept_ref[0] = jnp.sum((cut >= 0).astype(jnp.int32) + (cut >= HALF).astype(jnp.int32))
     first_body(first, cells, hbm_refs, buffers, sem, moved_ref, coef_ref, edge_ref, table_ref, ready)
     later.wait()
 
@@ -483,22 +491,15 @@
     parts = levels // SUB
     steps = SUB // GROUP
     winds = (tracer, zonal, meridional)
-    cut = jnp.where(polar_mask == 1, cutoff_wave, -1)
-    cut_row = cut[None, :]
-
-    top = pl.BlockSpec((levels, SUB, cells), lambda i: (0, 0, 0))
-    bottom = pl.BlockSpec((levels, SUB, cells), lambda i: (0, rows // SUB - 1, 0))
-    full = pl.BlockSpec((4, levels, width), lambda i: (0, 0, 0))
-    ring0, ring1, own = pl.pallas_call(
+    ring0, ring1, own, cut_row = call(
         edge_kernel,
-        grid=(1,),
-        in_specs=[SMEM, pl.BlockSpec((1, rows), lambda i: (0, 0)), top, top, top, bottom, bottom, bottom],
-        out_specs=[full, full, pl.BlockSpec((2, levels, width), lambda i: (0, 0, 0))],
-        out_shape=[shape(4, levels, width), shape(4, levels, width), shape(2, levels, width)],
-        compiler_params=pltpu.CompilerParams(vmem_limit_bytes=FIRST_MIB * MIB),
-    )(info, cut_row, *winds, *winds)
-    later, ring0 = lax.optimization_barrier((cut_row, ring0))
-    kept = jnp.sum((later >= 0).astype(jnp.int32) + (later >= HALF).astype(jnp.int32))
+        [(info, SMEM), (cutoff_wave[None, :], HBM), (polar_mask[None, :], HBM), *[(x, HBM) for x in winds]],
+        [(shape(4, levels, width), VMEM), (shape(4, levels, width), VMEM), (shape(2, levels, width), VMEM),
+         (shape(1, rows, dtype=jnp.int32), VMEM)],
+        [pltpu.VMEM((10, levels, cells), F32), pltpu.VMEM((2, 1, rows), jnp.int32), pltpu.SemaphoreType.DMA((12,))],
+        FIRST_MIB,
+    )
+    cut = cut_row[0]
     ring = ("lon", "lat")
     got0 = lax.ppermute(ring0, ring, lat_ring(bands, ways, 0))
     got1 = lax.ppermute(ring1, ring, lat_ring(bands, ways, 1))
@@ -515,10 +516,10 @@
     buffer = pltpu.VMEM((SUB, rows, cells), F32)
     table_shape, back_shape = (shape(*x.shape[1:], dtype=BF16) for x in (tables, backs))
     sems = pltpu.SemaphoreType.DMA
-    moved_a, coef_a, edge_a, table, back = call(
+    moved_a, coef_a, edge_a, table, back, kept = call(
         functools.partial(first_kernel, 0, cells),
-        [(info, SMEM), *[(x, HBM) for x in (*winds, tables, backs)]],
-        [(x, VMEM) for x in (grid, coef, edge, table_shape, back_shape)],
+        [(info, SMEM), (cut_row, VMEM), *[(x, HBM) for x in (*winds, tables, backs)]],
+        [*[(x, VMEM) for x in (grid, coef, edge, table_shape, back_shape)], (shape(1, dtype=jnp.int32), SMEM)],
         [buffer, buffer, buffer, sems((3, SUB)), sems((2,))],
         FIRST_MIB,
     )
@@ -571,7 +572,7 @@
         return out[0]
 
     limits = sorted({min(-(-x * rows // 64), 2 * rows) for x in LIMITS})
-    choice = sum((kept > x).astype(jnp.int32) for x in limits[:-1])
+    choice = sum((kept[0] > x).astype(jnp.int32) for x in limits[:-1])
     return lax.switch(
         choice, [functools.partial(rest, x) for x in limits],
         info, cut, cut_row, tracer, zonal, meridional, own, got0, got1, moved_a, coef_a, edge_a, table, back,

time: 94.3 us -> 89.7 us (0.951)
  waiting for transfers between devices: 23.6 us -> 19.1 us
  starting transfers between devices: 11.4 us -> 14.5 us
  Pallas kernels: 56.2 us -> 53.2 us
  other arithmetic: 1.57 us -> 0.27 us
  local copies, waits for them, and re-layouts: 0.04 us -> 1.33 us
    ppermute x8, waiting for transfers between devices: 23.6 us -> 19.1 us  [swap(): return lax.ppermute(x, 'lon', [(i, i ^ 1 << bit) for i in range(count)])]
    ppermute x8, starting transfers between devices: 8.34 us -> 11.4 us  [swap(): return lax.ppermute(x, 'lon', [(i, i ^ 1 << bit) for i in range(count)])]
    pallas_call x1 -> x0, Pallas kernels: 2.79 us -> none  [on_device(): pl.pallas_call(edge_kernel, grid=(1,), in_specs=[SMEM, pl.BlockSpec((1, r...]
    unnamed x0 -> x6, local copies, waits for them, and re-layouts: none -> 1.31 us
    pallas_call x7 -> x8, Pallas kernels: 53.4 us -> 53.2 us  [call(): pl.pallas_call(kernel, in_specs=[spec for _, spec in inputs], out_specs=[...]
  transfers between devices with their start and end apart: 10 -> 10, of which waited for: 4 -> 5; matrix products, arithmetic and copies ran while one was open for 1% -> 0% of each run, Pallas kernels for 50% -> 50%
where the time goes in v2:
time: 89.7 us; the launch traced here: 89.6 us
  Pallas kernels  53.2 us (59%)
  waiting for transfers between devices  19.1 us (21%)
  starting transfers between devices  14.5 us (16%)
  local copies, waits for them, and re-layouts  1.33 us (1%)
    pallas_call x8, Pallas kernels, call(): pl.pallas_call(kernel, in_specs=[spec for _, spec in inputs], out_specs=[...  53.2 us
    ppermute x8, waiting for transfers between devices, swap(): return lax.ppermute(x, 'lon', [(i, i ^ 1 << bit) for i in range(count)])  19.1 us
    ppermute x8, starting transfers between devices, swap(): return lax.ppermute(x, 'lon', [(i, i ^ 1 << bit) for i in range(count)])  11.4 us
    ppermute x1, starting transfers between devices, on_device(): got1 = lax.ppermute(ring1, ring, lat_ring(bands, ways, 1))  2.59 us
  transfers between devices with their start and end apart: 10, of which 5 were waited for; matrix products, arithmetic and copies ran while one was open for 0% of the time, Pallas kernels for 50%

profile of v2, /device:TPU:0, one launch (start us, length us, event | category | flops | bytes accessed | tf_op | source)
XLA Modules:
  0.0 89.6 jit_solution(2967174564179958035)
XLA Ops:
  0.0 0.1 pad_add_fusion.info_ref
  0.1 0.7 copy-done
  0.7 0.7 copy-done.1
  1.4 2.4 %shard_map.75 = (f32[4,16,1536]{2,1,0:T(8,128)S(1)}, f32[4,16,1536]{2,1,0:T(8,128)S(1)}, f32[2,16,1536]{2,1,0:T(8,128)S(1)}, s32[1,64]{1,0:T(1,128)S(1)}) custom-call(s32[4]{0:T(128)S(1)} %pad_add_fusion.info_ref, s32[1,64]{1,0:T(1,128)S(1)} %bitcast.6, s32[1,64]{1,0:T(1,128)S(1)} %bitcast.7, f32[16,64,1440]{2,1,0:T(8,128)} %s_ref.3, f32[16,64,1440]{2,1,0:T(8,128)} %u_ref.3, ...), custom_call_target="tpu_custom_call" | custom-call | tf_op jit(solution)/shard_map/pallas_call | solution.py:446
  3.8 0.5 collective-permute-start.16
  4.3 2.6 %collective-permute-start.17 = (f32[4,16,1536]{2,1,0:T(8,128)S(1)}, f32[4,16,1536]{2,1,0:T(8,128)S(1)}, u32[]{:S(2)}, u32[]{:S(2)}) collective-permute-start(f32[4,16,1536]{2,1,0:T(8,128)S(1)} %get-tuple-element.132), channel_id=1, source_target_pairs={{0,16},{8,24},{16,17},{24,25},{1,0},{9,8},{17,18},{25,26},{2,1},{1... | collective-permute-start | bytes 1179656 | tf_op jit(solution)/shard_map/ppermute | solution.py:505
  6.9 8.9 %shard_map.76 = (f32[8,64,1536]{2,1,0:T(8,128)}, f32[2,512,128]{2,1,0:T(8,128)S(1)}, f32[8,128]{1,0:T(8,128)S(1)}, bf16[1536,512]{1,0:T(8,128)(2,1)S(1)}, bf16[512,1536]{1,0:T(8,128)(2,1)S(1)}, /*index=5*/s32[1]{0:T(128)}) custom-call(s32[4]{0:T(128)S(1)} %pad_add_fusion.info_ref, s32[1,64]{1,0:T(1,128)S(1)} %get-tuple-element.128.cut_row_ref, ...), custom_call_target="tpu_custom_call" | custom-call | tf_op jit(solution)/shard_map/pallas_call | solution.py:446
  16.5 0.0 collective-permute-done.16
  16.5 0.0 collective-permute-done.17
  16.5 72.9 %conditional.1 = (f32[16,64,1440]{2,1,0:T(8,128)}) conditional(s32[]{:T(128)} %bitcast.4, (s32[4]{0:T(128)S(1)}, s32[64]{0:T(128)S(1)}, f32[16,64,1440]{2,1,0:T(8,128)}, f32[16,64,1440]{2,1,0:T(8,128)S(1)}, f32[16,64,1440]{2,1,0:T(8,128)}, /*index=5*/f32[2,16,1536]{2,1,0:T(8,128)S(1)}, f32[4,16,1536]{2,1,0:T(8,128)S(1)}, ...), branch_computations={%region_0.0_spmd, %region_1.0_spmd} | conditional | flops 559104 | bytes 56058260 | solution.py:576
  16.5 1.5 %branch_0_fun.8 = (f32[4,8,1536]{2,1,0:T(8,128)S(1)}, f32[2,8,1536]{2,1,0:T(8,128)S(1)}, f32[2,8,128]{2,1,0:T(8,128)S(1)}, f32[99,8,128]{2,1,0:T(8,128)S(1)}) custom-call(s32[4]{0:T(128)S(1)} %get-tuple-element.64.info_ref, s32[64]{0:T(128)S(1)} %bitcast.14, f32[2,512,128]{2,1,0:T(8,128)S(1)} %get-tuple-element.82.coef_in_ref, ...), custom_call_target="tpu_custom_call" | custom-call | tf_op jit(solution)/shard_map/cond/branch_0_fun/pallas_call | solution.py:446
  18.1 2.0 %collective-permute-start.4 = (f32[99,8,128]{2,1,0:T(8,128)S(1)}, f32[99,8,128]{2,1,0:T(8,128)S(1)}, u32[]{:S(2)}, u32[]{:S(2)}) collective-permute-start(f32[99,8,128]{2,1,0:T(8,128)S(1)} %get-tuple-element.84), channel_id=1, source_target_pairs={{0,8},{8,0},{16,24},{24,16},{1,9},{9,1},{17,25},{25,17},{2,10},{10... | collective-permute-start | bytes 1216520 | tf_op jit(solution)/shard_map/cond/branch_0_fun/ppermute | solution.py:459
  20.1 8.2 %branch_0_fun.6 = (f32[8,64,1536]{2,1,0:T(8,128)S(1)}, f32[4,8,1536]{2,1,0:T(8,128)S(1)}, f32[2,8,1536]{2,1,0:T(8,128)S(1)}, f32[2,8,128]{2,1,0:T(8,128)S(1)}, f32[99,8,128]{2,1,0:T(8,128)S(1)}) custom-call(s32[4]{0:T(128)S(1)} %get-tuple-element.64.info_ref, s32[64]{0:T(128)S(1)} %bitcast.15, f32[16,64,1440]{2,1,0:T(8,128)} %get-tuple-element.67.s_ref, ...), custom_call_target="tpu_custom_call" | custom-call | tf_op jit(solution)/shard_map/cond/branch_0_fun/pallas_call | solution.py:446
  28.3 0.2 collective-permute-start
  28.4 1.1 %collective-permute-done.4 = f32[99,8,128]{2,1,0:T(8,128)S(1)} collective-permute-done((f32[99,8,128]{2,1,0:T(8,128)S(1)}, f32[99,8,128]{2,1,0:T(8,128)S(1)}, u32[]{:S(2)}, u32[]{:S(2)}) %collective-permute-start.4) | collective-permute-done | bytes 405536 | tf_op jit(solution)/shard_map/cond/branch_0_fun/ppermute | solution.py:459
  29.5 0.1 add.18.a_ref
  29.6 1.6 %collective-permute-start.5 = (f32[99,8,128]{2,1,0:T(8,128)S(1)}, f32[99,8,128]{2,1,0:T(8,128)S(1)}, u32[]{:S(2)}, u32[]{:S(2)}) collective-permute-start(f32[99,8,128]{2,1,0:T(8,128)S(1)} %add.18.a_ref), channel_id=1, source_target_pairs={{0,16},{8,24},{16,0},{24,8},{1,17},{9,25},{17,1},{25,9},{2,18},{10... | collective-permute-start | bytes 1216520 | tf_op jit(solution)/shard_map/cond/branch_0_fun/ppermute | solution.py:459
  31.2 7.8 %collective-permute-done = f32[99,8,128]{2,1,0:T(8,128)S(1)} collective-permute-done((f32[99,8,128]{2,1,0:T(8,128)S(1)}, f32[99,8,128]{2,1,0:T(8,128)S(1)}, u32[]{:S(2)}, u32[]{:S(2)}) %collective-permute-start) | collective-permute-done | bytes 405536 | tf_op jit(solution)/shard_map/cond/branch_0_fun/ppermute | solution.py:459
  39.1 1.7 %collective-permute-start.1 = (f32[99,8,128]{2,1,0:T(8,128)S(1)}, f32[99,8,128]{2,1,0:T(8,128)S(1)}, u32[]{:S(2)}, u32[]{:S(2)}) collective-permute-start(f32[99,8,128]{2,1,0:T(8,128)S(1)} %add.16.a_ref), channel_id=1, source_target_pairs={{0,16},{8,24},{16,0},{24,8},{1,17},{9,25},{17,1},{25,9},{2,18},{10... | collective-permute-start | bytes 1216520 | tf_op jit(solution)/shard_map/cond/branch_0_fun/ppermute | solution.py:459
  40.7 0.2 collective-permute-done.5.b_ref
  40.9 12.0 %branch_0_fun.9 = (f32[8,64,1536]{2,1,0:T(8,128)S(1)}, f32[94,8,128]{2,1,0:T(8,128)S(1)}) custom-call(s32[4]{0:T(128)S(1)} %get-tuple-element.64.info_ref, s32[64]{0:T(128)S(1)} %bitcast.16, s32[1,64]{1,0:T(1,128)S(1)} %get-tuple-element.66.cut_row_ref, f32[99,8,128]{2,1,0:T(8,128)S(1)} %add.18.a_ref, f32[99,8,128]{2,1,0:T(8,128)S(1)} %collective-permute-done.5.b_ref, ...), custom_call_target="tpu_custom_call" | custom-call | tf_op jit(solution)/shard_map/cond/branch_0_fun/pallas_call | solution.py:446
  52.9 1.6 %collective-permute-start.6 = (f32[94,8,128]{2,1,0:T(8,128)S(1)}, f32[94,8,128]{2,1,0:T(8,128)S(1)}, u32[]{:S(2)}, u32[]{:S(2)}) collective-permute-start(f32[94,8,128]{2,1,0:T(8,128)S(1)} %get-tuple-element.89), channel_id=1, source_target_pairs={{0,8},{8,0},{16,24},{24,16},{1,9},{9,1},{17,25},{25,17},{2,10},{10... | collective-permute-start | bytes 1155080 | tf_op jit(solution)/shard_map/cond/branch_0_fun/ppermute | solution.py:459
  54.6 0.0 collective-permute-done.1.b_ref
  54.6 12.1 %branch_0_fun.7 = (f32[8,64,1536]{2,1,0:T(8,128)S(1)}, f32[94,8,128]{2,1,0:T(8,128)S(1)}) custom-call(s32[4]{0:T(128)S(1)} %get-tuple-element.64.info_ref, s32[64]{0:T(128)S(1)} %bitcast.17, s32[1,64]{1,0:T(1,128)S(1)} %get-tuple-element.66.cut_row_ref, f32[99,8,128]{2,1,0:T(8,128)S(1)} %add.16.a_ref, f32[99,8,128]{2,1,0:T(8,128)S(1)} %collective-permute-done.1.b_ref, ...), custom_call_target="tpu_custom_call" | custom-call | tf_op jit(solution)/shard_map/cond/branch_0_fun/pallas_call | solution.py:446
  66.6 0.5 collective-permute-start.2
  67.2 1.8 %collective-permute-start.7 = (f32[94,8,128]{2,1,0:T(8,128)S(1)}, f32[94,8,128]{2,1,0:T(8,128)S(1)}, u32[]{:S(2)}, u32[]{:S(2)}) collective-permute-start(f32[94,8,128]{2,1,0:T(8,128)S(1)} %add.19.a_ref), channel_id=1, source_target_pairs={{0,16},{8,24},{16,0},{24,8},{1,17},{9,25},{17,1},{25,9},{2,18},{10... | collective-permute-start | bytes 1155080 | tf_op jit(solution)/shard_map/cond/branch_0_fun/ppermute | solution.py:459
  69.0 7.2 %collective-permute-done.2 = f32[94,8,128]{2,1,0:T(8,128)S(1)} collective-permute-done((f32[94,8,128]{2,1,0:T(8,128)S(1)}, f32[94,8,128]{2,1,0:T(8,128)S(1)}, u32[]{:S(2)}, u32[]{:S(2)}) %collective-permute-start.2) | collective-permute-done | bytes 385056 | tf_op jit(solution)/shard_map/cond/branch_0_fun/ppermute | solution.py:459
  76.1 0.1 add.17.a_ref
  76.2 2.0 %collective-permute-start.3 = (f32[94,8,128]{2,1,0:T(8,128)S(1)}, f32[94,8,128]{2,1,0:T(8,128)S(1)}, u32[]{:S(2)}, u32[]{:S(2)}) collective-permute-start(f32[94,8,128]{2,1,0:T(8,128)S(1)} %add.17.a_ref), channel_id=1, source_target_pairs={{0,16},{8,24},{16,0},{24,8},{1,17},{9,25},{17,1},{25,9},{2,18},{10... | collective-permute-start | bytes 1155080 | tf_op jit(solution)/shard_map/cond/branch_0_fun/ppermute | solution.py:459
  78.2 4.0 %branch_0_fun.10.refs_0_ = f32[16,64,1440]{2,1,0:T(8,128)} custom-call(s32[4]{0:T(128)S(1)} %get-tuple-element.64.info_ref, s32[64]{0:T(128)S(1)} %bitcast.18, s32[1,64]{1,0:T(1,128)S(1)} %get-tuple-element.66.cut_row_ref, f32[94,8,128]{2,1,0:T(8,128)S(1)} %add.19.a_ref, f32[94,8,128]{2,1,0:T(8,128)S(1)} %collective-permute-done.7.b_ref, ...), custom_call_target="tpu_custom_call" | custom-call | tf_op jit(solution)/shard_map/cond/branch_0_fun/pallas_call | solution.py:446
  82.2 2.9 %collective-permute-done.3.b_ref = f32[94,8,128]{2,1,0:T(8,128)S(1)} collective-permute-done((f32[94,8,128]{2,1,0:T(8,128)S(1)}, f32[94,8,128]{2,1,0:T(8,128)S(1)}, u32[]{:S(2)}, u32[]{:S(2)}) %collective-permute-start.3) | collective-permute-done | bytes 385056 | tf_op jit(solution)/shard_map/cond/branch_0_fun/ppermute | solution.py:459
  85.2 4.0 %branch_0_fun.11 = f32[16,64,1440]{2,1,0:T(8,128)} custom-call(s32[4]{0:T(128)S(1)} %get-tuple-element.64.info_ref, s32[64]{0:T(128)S(1)} %bitcast.19, s32[1,64]{1,0:T(1,128)S(1)} %get-tuple-element.66.cut_row_ref, f32[94,8,128]{2,1,0:T(8,128)S(1)} %add.17.a_ref, f32[94,8,128]{2,1,0:T(8,128)S(1)} %collective-permute-done.3.b_ref, ...), custom_call_target="tpu_custom_call", output_to_operand_aliasing={{}: (7, {})} | custom-call | tf_op jit(solution)/shard_map/cond/branch_0_fun/pallas_call | solution.py:446
  (15 shorter events, 0.1 us)
Async XLA Ops:
  0.1 0.7 copy-start
  0.7 0.7 copy-start.1
  1.4 5.5 %copy-start.2 = (f32[16,64,1440]{2,1,0:T(8,128)S(1)}, f32[16,64,1440]{2,1,0:T(8,128)}, u32[]{:S(2)}) copy-start(f32[16,64,1440]{2,1,0:T(8,128)} %u_ref.3) | copy-start | bytes 17694724
  3.8 12.7 %collective-permute-start.16 = (f32[4,16,1536]{2,1,0:T(8,128)S(1)}, f32[4,16,1536]{2,1,0:T(8,128)S(1)}, u32[]{:S(2)}, u32[]{:S(2)}) collective-permute-start(f32[4,16,1536]{2,1,0:T(8,128)S(1)} %get-tuple-element.131), channel_id=1, source_target_pairs={{0,1},{8,9},{16,0},{24,8},{1,2},{9,10},{17,16},{25,24},{2,3},{10,1... | collective-permute-start | bytes 1179656 | tf_op jit(solution)/shard_map/ppermute | solution.py:504
  4.3 12.2 %collective-permute-start.17 = (f32[4,16,1536]{2,1,0:T(8,128)S(1)}, f32[4,16,1536]{2,1,0:T(8,128)S(1)}, u32[]{:S(2)}, u32[]{:S(2)}) collective-permute-start(f32[4,16,1536]{2,1,0:T(8,128)S(1)} %get-tuple-element.132), channel_id=1, source_target_pairs={{0,16},{8,24},{16,17},{24,25},{1,0},{9,8},{17,18},{25,26},{2,1},{1... | collective-permute-start | bytes 1179656 | tf_op jit(solution)/shard_map/ppermute | solution.py:505
  18.1 11.5 %collective-permute-start.4 = (f32[99,8,128]{2,1,0:T(8,128)S(1)}, f32[99,8,128]{2,1,0:T(8,128)S(1)}, u32[]{:S(2)}, u32[]{:S(2)}) collective-permute-start(f32[99,8,128]{2,1,0:T(8,128)S(1)} %get-tuple-element.84), channel_id=1, source_target_pairs={{0,8},{8,0},{16,24},{24,16},{1,9},{9,1},{17,25},{25,17},{2,10},{10... | collective-permute-start | bytes 1216520 | tf_op jit(solution)/shard_map/cond/branch_0_fun/ppermute | solution.py:459
  20.1 20.8 %slice-start = ((s8[6291456]{0:T(1024)(128)(4,1)}), s8[4194304]{0:T(1024)(128)(4,1)S(1)}, s32[]{:S(2)}) async-start(s8[6291456]{0:T(1024)(128)(4,1)} %bitcast.8), calls=%async_computation | async-start | bytes 8388608 | tf_op jit(solution)/shard_map/cond
  20.1 20.8 %slice-start.1 = ((s8[6291456]{0:T(1024)(128)(4,1)}), s8[2097152]{0:T(1024)(128)(4,1)S(1)}, s32[]{:S(2)}) async-start(s8[6291456]{0:T(1024)(128)(4,1)} %bitcast.8), calls=%async_computation.1 | async-start | bytes 4194304 | tf_op jit(solution)/shard_map/cond
  20.1 20.8 %copy-start.3 = (f32[8,64,1536]{2,1,0:T(8,128)S(1)}, f32[8,64,1536]{2,1,0:T(8,128)}, u32[]{:S(2)}) copy-start(f32[8,64,1536]{2,1,0:T(8,128)} %get-tuple-element.88.moved_ref) | copy-start | bytes 9437188 | tf_op jit(solution)/shard_map/cond
  28.3 10.7 %collective-permute-start = (f32[99,8,128]{2,1,0:T(8,128)S(1)}, f32[99,8,128]{2,1,0:T(8,128)S(1)}, u32[]{:S(2)}, u32[]{:S(2)}) collective-permute-start(f32[99,8,128]{2,1,0:T(8,128)S(1)} %get-tuple-element.74), channel_id=1, source_target_pairs={{0,8},{8,0},{16,24},{24,16},{1,9},{9,1},{17,25},{25,17},{2,10},{10... | collective-permute-start | bytes 1216520 | tf_op jit(solution)/shard_map/cond/branch_0_fun/ppermute | solution.py:459
  29.6 11.3 %collective-permute-start.5 = (f32[99,8,128]{2,1,0:T(8,128)S(1)}, f32[99,8,128]{2,1,0:T(8,128)S(1)}, u32[]{:S(2)}, u32[]{:S(2)}) collective-permute-start(f32[99,8,128]{2,1,0:T(8,128)S(1)} %add.18.a_ref), channel_id=1, source_target_pairs={{0,16},{8,24},{16,0},{24,8},{1,17},{9,25},{17,1},{25,9},{2,18},{10... | collective-permute-start | bytes 1216520 | tf_op jit(solution)/shard_map/cond/branch_0_fun/ppermute | solution.py:459
  39.1 15.5 %collective-permute-start.1 = (f32[99,8,128]{2,1,0:T(8,128)S(1)}, f32[99,8,128]{2,1,0:T(8,128)S(1)}, u32[]{:S(2)}, u32[]{:S(2)}) collective-permute-start(f32[99,8,128]{2,1,0:T(8,128)S(1)} %add.16.a_ref), channel_id=1, source_target_pairs={{0,16},{8,24},{16,0},{24,8},{1,17},{9,25},{17,1},{25,9},{2,18},{10... | collective-permute-start | bytes 1216520 | tf_op jit(solution)/shard_map/cond/branch_0_fun/ppermute | solution.py:459
  52.9 14.2 %collective-permute-start.6 = (f32[94,8,128]{2,1,0:T(8,128)S(1)}, f32[94,8,128]{2,1,0:T(8,128)S(1)}, u32[]{:S(2)}, u32[]{:S(2)}) collective-permute-start(f32[94,8,128]{2,1,0:T(8,128)S(1)} %get-tuple-element.89), channel_id=1, source_target_pairs={{0,8},{8,0},{16,24},{24,16},{1,9},{9,1},{17,25},{25,17},{2,10},{10... | collective-permute-start | bytes 1155080 | tf_op jit(solution)/shard_map/cond/branch_0_fun/ppermute | solution.py:459
  66.6 9.5 %collective-permute-start.2 = (f32[94,8,128]{2,1,0:T(8,128)S(1)}, f32[94,8,128]{2,1,0:T(8,128)S(1)}, u32[]{:S(2)}, u32[]{:S(2)}) collective-permute-start(f32[94,8,128]{2,1,0:T(8,128)S(1)} %get-tuple-element.80), channel_id=1, source_target_pairs={{0,8},{8,0},{16,24},{24,16},{1,9},{9,1},{17,25},{25,17},{2,10},{10... | collective-permute-start | bytes 1155080 | tf_op jit(solution)/shard_map/cond/branch_0_fun/ppermute | solution.py:459
  67.2 11.0 %collective-permute-start.7 = (f32[94,8,128]{2,1,0:T(8,128)S(1)}, f32[94,8,128]{2,1,0:T(8,128)S(1)}, u32[]{:S(2)}, u32[]{:S(2)}) collective-permute-start(f32[94,8,128]{2,1,0:T(8,128)S(1)} %add.19.a_ref), channel_id=1, source_target_pairs={{0,16},{8,24},{16,0},{24,8},{1,17},{9,25},{17,1},{25,9},{2,18},{10... | collective-permute-start | bytes 1155080 | tf_op jit(solution)/shard_map/cond/branch_0_fun/ppermute | solution.py:459
  76.2 9.0 %collective-permute-start.3 = (f32[94,8,128]{2,1,0:T(8,128)S(1)}, f32[94,8,128]{2,1,0:T(8,128)S(1)}, u32[]{:S(2)}, u32[]{:S(2)}) collective-permute-start(f32[94,8,128]{2,1,0:T(8,128)S(1)} %add.17.a_ref), channel_id=1, source_target_pairs={{0,16},{8,24},{16,0},{24,8},{1,17},{9,25},{17,1},{25,9},{2,18},{10... | collective-permute-start | bytes 1155080 | tf_op jit(solution)/shard_map/cond/branch_0_fun/ppermute | solution.py:459

commit v3 on v2

--- a/solution.py
+++ b/solution.py
@@ -111,8 +111,7 @@
 
 
 def edge_kernel(
-    info_ref, cutoff_ref, mask_ref, s_ref, u_ref, v_ref,
-    ring0_ref, ring1_ref, own_ref, cut_ref, rows_ref, cuts_ref, sem,
+    info_ref, cut_ref, s_ref, u_ref, v_ref, ring0_ref, ring1_ref, own_ref, rows_ref, sem,
 ):
     levels, width = own_ref.shape[1:]
     rows = cut_ref.shape[1]
@@ -122,12 +121,9 @@
     copies = [
         pltpu.make_async_copy(h.at[:, at, :], rows_ref.at[i], sem.at[i]) for i, (h, at) in enumerate(wanted)
     ]
-    for i, h in enumerate((cutoff_ref, mask_ref)):
-        copies.append(pltpu.make_async_copy(h, cuts_ref.at[i], sem.at[len(wanted) + i]))
     every(copies, "start")
     every(copies, "wait")
-    cut = jnp.where(cuts_ref[1] == 1, cuts_ref[0], -1)
-    cut_ref[...] = cut
+    cut = cut_ref[...]
     sides = []
     for side, (flow, row) in enumerate(((northward, 0), (southward, rows - 1))):
         s, u, v = (rows_ref[3 * side + i] for i in range(3))
@@ -371,16 +367,12 @@
     info_ref, cut_ref, cut_row_ref, a_ref, b_ref, flow_ref, edge_v_ref, edge_cut_ref,
     moved_ref, table_ref, back_ref, u_ref, v_ref,
     out_ref, pay_ref,
-    coef_ref, sum_ref, step_ref, edge_ref, in_ref, place_ref, s_ref, u_buf, v_buf, sem,
+    coef_ref, sum_ref, step_ref, edge_ref, in_ref, place_ref, s_ref,
 ):
     rows = cut_ref.shape[0]
     levels, _, width = out_ref.shape
     lon = info_ref[0]
 
-    def copies(level):
-        return level_copies((u_ref, v_ref), (u_buf, v_buf), sem, first, level)
-
-    loop(levels, lambda level: every(copies(level), "start"))
     unpack_rows(cut_ref, a_ref, b_ref, 5 + ways, total, coef_ref)
     for side in range(2):
         for half in range(2):
@@ -406,8 +398,7 @@
 
     def one(level):
         row = pl.ds(level, 1)
-        every(copies(level), "wait")
-        out_ref[level] = moved_rows(s_ref[level], padded(u_buf[level], width), padded(v_buf[level], width))
+        out_ref[level] = moved_rows(s_ref[level], padded(u_ref[first + level], width), padded(v_ref[first + level], width))
         out_ref[level, 0:1, :] = out_ref[level, 0:1, :] + step_ref[0, row, :]
         out_ref[level, rows - 1 : rows, :] = out_ref[level, rows - 1 : rows, :] + step_ref[1, row, :]
         place_ref[row, :] = outflow(out_ref[level, :, width - 128 :], cells, width)
@@ -491,15 +482,15 @@
     parts = levels // SUB
     steps = SUB // GROUP
     winds = (tracer, zonal, meridional)
-    ring0, ring1, own, cut_row = call(
+    cut = jnp.where(polar_mask == 1, cutoff_wave, -1)
+    cut_row = cut[None, :]
+    ring0, ring1, own = call(
         edge_kernel,
-        [(info, SMEM), (cutoff_wave[None, :], HBM), (polar_mask[None, :], HBM), *[(x, HBM) for x in winds]],
-        [(shape(4, levels, width), VMEM), (shape(4, levels, width), VMEM), (shape(2, levels, width), VMEM),
-         (shape(1, rows, dtype=jnp.int32), VMEM)],
-        [pltpu.VMEM((10, levels, cells), F32), pltpu.VMEM((2, 1, rows), jnp.int32), pltpu.SemaphoreType.DMA((12,))],
+        [(info, SMEM), (cut_row, VMEM), *[(x, HBM) for x in winds]],
+        [(shape(4, levels, width), VMEM), (shape(4, levels, width), VMEM), (shape(2, levels, width), VMEM)],
+        [pltpu.VMEM((10, levels, cells), F32), pltpu.SemaphoreType.DMA((10,))],
         FIRST_MIB,
     )
-    cut = cut_row[0]
     ring = ("lon", "lat")
     got0 = lax.ppermute(ring0, ring, lat_ring(bands, ways, 0))
     got1 = lax.ppermute(ring1, ring, lat_ring(bands, ways, 1))
@@ -551,10 +542,10 @@
             seconds.append(call(
                 functools.partial(second_kernel, part * SUB, total, cells, ways),
                 [*scalars, *[(x, VMEM) for x in (cut_row, *sums[part], flow, edge_v, edge_cut, moved, table, back)],
-                 (zonal, HBM), (meridional, HBM)],
+                 (zonal, VMEM), (meridional, VMEM)],
                 [(grid, VMEM), (shape(limit + ways + 2, SUB, KMAX), VMEM)],
                 [room(coef), room(coef), pltpu.VMEM((2, SUB, width), F32),
-                 pltpu.VMEM((2 * SUB, 2 * KMAX), F32), room(edge), room(edge), room(grid), buffer, buffer, sems((2, SUB))],
+                 pltpu.VMEM((2 * SUB, 2 * KMAX), F32), room(edge), room(edge), room(grid)],
                 20,
             ))
         sums = [sum_over_lon(x[1], True) for x in seconds]

time: 89.7 us -> 82.5 us (0.920)
  Pallas kernels: 53.2 us -> 46.7 us
  local copies, waits for them, and re-layouts: 1.33 us -> 0.01 us
    pallas_call x8, Pallas kernels: 53.2 us -> 46.7 us  [call(): pl.pallas_call(kernel, in_specs=[spec for _, spec in inputs], out_specs=[...]
    unnamed x6 -> x2, local copies, waits for them, and re-layouts: 1.31 us -> 0.01 us
  transfers between devices with their start and end apart: 10 -> 10, of which waited for: 5 -> 5; matrix products, arithmetic and copies ran while one was open for 0% -> 0% of each run, Pallas kernels for 50% -> 47%
where the time goes in v3:
time: 82.5 us; the launch traced here: 82.4 us
  Pallas kernels  46.7 us (57%)
  waiting for transfers between devices  19 us (23%)
  starting transfers between devices  14.6 us (18%)
  other arithmetic  0.96 us (1%)
  between operations  0.85 us (1%)
    pallas_call x8, Pallas kernels, call(): pl.pallas_call(kernel, in_specs=[spec for _, spec in inputs], out_specs=[...  46.7 us
    ppermute x8, waiting for transfers between devices, swap(): return lax.ppermute(x, 'lon', [(i, i ^ 1 << bit) for i in range(count)])  19 us
    ppermute x8, starting transfers between devices, swap(): return lax.ppermute(x, 'lon', [(i, i ^ 1 << bit) for i in range(count)])  11.5 us
    ppermute x1, starting transfers between devices, on_device(): got1 = lax.ppermute(ring1, ring, lat_ring(bands, ways, 1))  2.59 us
  transfers between devices with their start and end apart: 10, of which 5 were waited for; matrix products, arithmetic and copies ran while one was open for 0% of the time, Pallas kernels for 47%

profile of v3, /device:TPU:0, one launch (start us, length us, event | category | flops | bytes accessed | tf_op | source)
XLA Modules:
  0.0 82.4 jit_solution(17686540800521519276)
XLA Ops:
  0.0 0.7 compare_select_fusion
  0.7 0.1 pad_add_fusion.info_ref
  0.8 2.4 %shard_map.76 = (f32[4,16,1536]{2,1,0:T(8,128)S(1)}, f32[4,16,1536]{2,1,0:T(8,128)S(1)}, f32[2,16,1536]{2,1,0:T(8,128)S(1)}) custom-call(s32[4]{0:T(128)S(1)} %pad_add_fusion.info_ref, s32[1,64]{1,0:T(1,128)S(1)} %bitcast.8, f32[16,64,1440]{2,1,0:T(8,128)} %s_ref.3, f32[16,64,1440]{2,1,0:T(8,128)} %u_ref.3, f32[16,64,1440]{2,1,0:T(8,128)} %v_ref.3), custom_call_target="tpu_custom_call" | custom-call | tf_op jit(solution)/shard_map/pallas_call | solution.py:437
  3.2 0.5 collective-permute-start.16
  3.7 2.6 %collective-permute-start.17 = (f32[4,16,1536]{2,1,0:T(8,128)S(1)}, f32[4,16,1536]{2,1,0:T(8,128)S(1)}, u32[]{:S(2)}, u32[]{:S(2)}) collective-permute-start(f32[4,16,1536]{2,1,0:T(8,128)S(1)} %get-tuple-element.130), channel_id=1, source_target_pairs={{0,16},{8,24},{16,17},{24,25},{1,0},{9,8},{17,18},{25,26},{2,1},{1... | collective-permute-start | bytes 1179656 | tf_op jit(solution)/shard_map/ppermute | solution.py:496
  6.3 8.9 %shard_map.75 = (f32[8,64,1536]{2,1,0:T(8,128)}, f32[2,512,128]{2,1,0:T(8,128)S(1)}, f32[8,128]{1,0:T(8,128)S(1)}, bf16[1536,512]{1,0:T(8,128)(2,1)S(1)}, bf16[512,1536]{1,0:T(8,128)(2,1)S(1)}, /*index=5*/s32[1]{0:T(128)}) custom-call(s32[4]{0:T(128)S(1)} %pad_add_fusion.info_ref, s32[1,64]{1,0:T(1,128)S(1)} %bitcast.9, f32[16,64,1440]{2,1,0:T(8,128)} %s_ref.3, ...), custom_call_target="tpu_custom_call" | custom-call | tf_op jit(solution)/shard_map/pallas_call | solution.py:437
  15.8 0.0 collective-permute-done.16
  15.9 0.0 collective-permute-done.17
  15.9 66.3 %conditional.1 = (f32[16,64,1440]{2,1,0:T(8,128)}) conditional(s32[]{:T(128)} %bitcast.3, (s32[4]{0:T(128)S(1)}, s32[64]{0:T(128)S(1)}, f32[16,64,1440]{2,1,0:T(8,128)}, f32[16,64,1440]{2,1,0:T(8,128)S(1)}, f32[16,64,1440]{2,1,0:T(8,128)}, /*index=5*/f32[2,16,1536]{2,1,0:T(8,128)S(1)}, f32[4,16,1536]{2,1,0:T(8,128)S(1)}, ...), branch_computations={%region_0.1_spmd, %region_1.2_spmd} | conditional | flops 559104 | bytes 56058260 | solution.py:567
  15.9 1.5 %branch_0_fun.8 = (f32[4,8,1536]{2,1,0:T(8,128)S(1)}, f32[2,8,1536]{2,1,0:T(8,128)S(1)}, f32[2,8,128]{2,1,0:T(8,128)S(1)}, f32[99,8,128]{2,1,0:T(8,128)S(1)}) custom-call(s32[4]{0:T(128)S(1)} %get-tuple-element.64.info_ref, s32[64]{0:T(128)S(1)} %bitcast.12, f32[2,512,128]{2,1,0:T(8,128)S(1)} %get-tuple-element.82.coef_in_ref, ...), custom_call_target="tpu_custom_call" | custom-call | tf_op jit(solution)/shard_map/cond/branch_0_fun/pallas_call | solution.py:437
  17.4 2.0 %collective-permute-start.4 = (f32[99,8,128]{2,1,0:T(8,128)S(1)}, f32[99,8,128]{2,1,0:T(8,128)S(1)}, u32[]{:S(2)}, u32[]{:S(2)}) collective-permute-start(f32[99,8,128]{2,1,0:T(8,128)S(1)} %get-tuple-element.84), channel_id=1, source_target_pairs={{0,8},{8,0},{16,24},{24,16},{1,9},{9,1},{17,25},{25,17},{2,10},{10... | collective-permute-start | bytes 1216520 | tf_op jit(solution)/shard_map/cond/branch_0_fun/ppermute | solution.py:450
  19.4 8.2 %branch_0_fun.6 = (f32[8,64,1536]{2,1,0:T(8,128)S(1)}, f32[4,8,1536]{2,1,0:T(8,128)S(1)}, f32[2,8,1536]{2,1,0:T(8,128)S(1)}, f32[2,8,128]{2,1,0:T(8,128)S(1)}, f32[99,8,128]{2,1,0:T(8,128)S(1)}) custom-call(s32[4]{0:T(128)S(1)} %get-tuple-element.64.info_ref, s32[64]{0:T(128)S(1)} %bitcast.13, f32[16,64,1440]{2,1,0:T(8,128)} %get-tuple-element.67.s_ref, ...), custom_call_target="tpu_custom_call" | custom-call | tf_op jit(solution)/shard_map/cond/branch_0_fun/pallas_call | solution.py:437
  27.6 0.2 collective-permute-start
  27.8 1.1 %collective-permute-done.4 = f32[99,8,128]{2,1,0:T(8,128)S(1)} collective-permute-done((f32[99,8,128]{2,1,0:T(8,128)S(1)}, f32[99,8,128]{2,1,0:T(8,128)S(1)}, u32[]{:S(2)}, u32[]{:S(2)}) %collective-permute-start.4) | collective-permute-done | bytes 405536 | tf_op jit(solution)/shard_map/cond/branch_0_fun/ppermute | solution.py:450
  28.9 0.1 add.18.a_ref
  28.9 1.7 %collective-permute-start.5 = (f32[99,8,128]{2,1,0:T(8,128)S(1)}, f32[99,8,128]{2,1,0:T(8,128)S(1)}, u32[]{:S(2)}, u32[]{:S(2)}) collective-permute-start(f32[99,8,128]{2,1,0:T(8,128)S(1)} %add.18.a_ref), channel_id=1, source_target_pairs={{0,16},{8,24},{16,0},{24,8},{1,17},{9,25},{17,1},{25,9},{2,18},{10... | collective-permute-start | bytes 1216520 | tf_op jit(solution)/shard_map/cond/branch_0_fun/ppermute | solution.py:450
  30.6 7.8 %collective-permute-done = f32[99,8,128]{2,1,0:T(8,128)S(1)} collective-permute-done((f32[99,8,128]{2,1,0:T(8,128)S(1)}, f32[99,8,128]{2,1,0:T(8,128)S(1)}, u32[]{:S(2)}, u32[]{:S(2)}) %collective-permute-start) | collective-permute-done | bytes 405536 | tf_op jit(solution)/shard_map/cond/branch_0_fun/ppermute | solution.py:450
  38.4 0.1 add.16.a_ref
  38.4 1.6 %collective-permute-start.1 = (f32[99,8,128]{2,1,0:T(8,128)S(1)}, f32[99,8,128]{2,1,0:T(8,128)S(1)}, u32[]{:S(2)}, u32[]{:S(2)}) collective-permute-start(f32[99,8,128]{2,1,0:T(8,128)S(1)} %add.16.a_ref), channel_id=1, source_target_pairs={{0,16},{8,24},{16,0},{24,8},{1,17},{9,25},{17,1},{25,9},{2,18},{10... | collective-permute-start | bytes 1216520 | tf_op jit(solution)/shard_map/cond/branch_0_fun/ppermute | solution.py:450
  40.1 0.1 collective-permute-done.5.b_ref
  40.2 8.8 %branch_0_fun.9 = (f32[8,64,1536]{2,1,0:T(8,128)S(1)}, f32[94,8,128]{2,1,0:T(8,128)S(1)}) custom-call(s32[4]{0:T(128)S(1)} %get-tuple-element.64.info_ref, s32[64]{0:T(128)S(1)} %bitcast.14, s32[1,64]{1,0:T(1,128)S(1)} %get-tuple-element.66.cut_row_ref, f32[99,8,128]{2,1,0:T(8,128)S(1)} %add.18.a_ref, f32[99,8,128]{2,1,0:T(8,128)S(1)} %collective-permute-done.5.b_ref, ...), custom_call_target="tpu_custom_call" | custom-call | tf_op jit(solution)/shard_map/cond/branch_0_fun/pallas_call | solution.py:437
  49.0 1.7 %collective-permute-start.6 = (f32[94,8,128]{2,1,0:T(8,128)S(1)}, f32[94,8,128]{2,1,0:T(8,128)S(1)}, u32[]{:S(2)}, u32[]{:S(2)}) collective-permute-start(f32[94,8,128]{2,1,0:T(8,128)S(1)} %get-tuple-element.89), channel_id=1, source_target_pairs={{0,8},{8,0},{16,24},{24,16},{1,9},{9,1},{17,25},{25,17},{2,10},{10... | collective-permute-start | bytes 1155080 | tf_op jit(solution)/shard_map/cond/branch_0_fun/ppermute | solution.py:450
  50.7 0.0 collective-permute-done.1.b_ref
  50.7 8.8 %branch_0_fun.7 = (f32[8,64,1536]{2,1,0:T(8,128)S(1)}, f32[94,8,128]{2,1,0:T(8,128)S(1)}) custom-call(s32[4]{0:T(128)S(1)} %get-tuple-element.64.info_ref, s32[64]{0:T(128)S(1)} %bitcast.15, s32[1,64]{1,0:T(1,128)S(1)} %get-tuple-element.66.cut_row_ref, f32[99,8,128]{2,1,0:T(8,128)S(1)} %add.16.a_ref, f32[99,8,128]{2,1,0:T(8,128)S(1)} %collective-permute-done.1.b_ref, ...), custom_call_target="tpu_custom_call" | custom-call | tf_op jit(solution)/shard_map/cond/branch_0_fun/pallas_call | solution.py:437
  59.5 0.5 collective-permute-start.2
  60.0 1.8 %collective-permute-start.7 = (f32[94,8,128]{2,1,0:T(8,128)S(1)}, f32[94,8,128]{2,1,0:T(8,128)S(1)}, u32[]{:S(2)}, u32[]{:S(2)}) collective-permute-start(f32[94,8,128]{2,1,0:T(8,128)S(1)} %add.19.a_ref), channel_id=1, source_target_pairs={{0,16},{8,24},{16,0},{24,8},{1,17},{9,25},{17,1},{25,9},{2,18},{10... | collective-permute-start | bytes 1155080 | tf_op jit(solution)/shard_map/cond/branch_0_fun/ppermute | solution.py:450
  61.8 7.1 %collective-permute-done.2 = f32[94,8,128]{2,1,0:T(8,128)S(1)} collective-permute-done((f32[94,8,128]{2,1,0:T(8,128)S(1)}, f32[94,8,128]{2,1,0:T(8,128)S(1)}, u32[]{:S(2)}, u32[]{:S(2)}) %collective-permute-start.2) | collective-permute-done | bytes 385056 | tf_op jit(solution)/shard_map/cond/branch_0_fun/ppermute | solution.py:450
  68.9 0.1 add.17.a_ref
  69.0 2.0 %collective-permute-start.3 = (f32[94,8,128]{2,1,0:T(8,128)S(1)}, f32[94,8,128]{2,1,0:T(8,128)S(1)}, u32[]{:S(2)}, u32[]{:S(2)}) collective-permute-start(f32[94,8,128]{2,1,0:T(8,128)S(1)} %add.17.a_ref), channel_id=1, source_target_pairs={{0,16},{8,24},{16,0},{24,8},{1,17},{9,25},{17,1},{25,9},{2,18},{10... | collective-permute-start | bytes 1155080 | tf_op jit(solution)/shard_map/cond/branch_0_fun/ppermute | solution.py:450
  71.0 4.0 %branch_0_fun.10.refs_0_ = f32[16,64,1440]{2,1,0:T(8,128)} custom-call(s32[4]{0:T(128)S(1)} %get-tuple-element.64.info_ref, s32[64]{0:T(128)S(1)} %bitcast.16, s32[1,64]{1,0:T(1,128)S(1)} %get-tuple-element.66.cut_row_ref, f32[94,8,128]{2,1,0:T(8,128)S(1)} %add.19.a_ref, f32[94,8,128]{2,1,0:T(8,128)S(1)} %collective-permute-done.7.b_ref, ...), custom_call_target="tpu_custom_call" | custom-call | tf_op jit(solution)/shard_map/cond/branch_0_fun/pallas_call | solution.py:437
  75.0 2.9 %collective-permute-done.3.b_ref = f32[94,8,128]{2,1,0:T(8,128)S(1)} collective-permute-done((f32[94,8,128]{2,1,0:T(8,128)S(1)}, f32[94,8,128]{2,1,0:T(8,128)S(1)}, u32[]{:S(2)}, u32[]{:S(2)}) %collective-permute-start.3) | collective-permute-done | bytes 385056 | tf_op jit(solution)/shard_map/cond/branch_0_fun/ppermute | solution.py:450
  78.0 4.0 %branch_0_fun.11 = f32[16,64,1440]{2,1,0:T(8,128)} custom-call(s32[4]{0:T(128)S(1)} %get-tuple-element.64.info_ref, s32[64]{0:T(128)S(1)} %bitcast.17, s32[1,64]{1,0:T(1,128)S(1)} %get-tuple-element.66.cut_row_ref, f32[94,8,128]{2,1,0:T(8,128)S(1)} %add.17.a_ref, f32[94,8,128]{2,1,0:T(8,128)S(1)} %collective-permute-done.3.b_ref, ...), custom_call_target="tpu_custom_call", output_to_operand_aliasing={{}: (7, {})} | custom-call | tf_op jit(solution)/shard_map/cond/branch_0_fun/pallas_call | solution.py:437
  (12 shorter events, 0.1 us)
Async XLA Ops:
  0.8 5.5 %copy-start = (f32[16,64,1440]{2,1,0:T(8,128)S(1)}, f32[16,64,1440]{2,1,0:T(8,128)}, u32[]{:S(2)}) copy-start(f32[16,64,1440]{2,1,0:T(8,128)} %u_ref.3) | copy-start | bytes 17694724
  3.2 12.7 %collective-permute-start.16 = (f32[4,16,1536]{2,1,0:T(8,128)S(1)}, f32[4,16,1536]{2,1,0:T(8,128)S(1)}, u32[]{:S(2)}, u32[]{:S(2)}) collective-permute-start(f32[4,16,1536]{2,1,0:T(8,128)S(1)} %get-tuple-element.129), channel_id=1, source_target_pairs={{0,1},{8,9},{16,0},{24,8},{1,2},{9,10},{17,16},{25,24},{2,3},{10,1... | collective-permute-start | bytes 1179656 | tf_op jit(solution)/shard_map/ppermute | solution.py:495
  3.7 12.2 %collective-permute-start.17 = (f32[4,16,1536]{2,1,0:T(8,128)S(1)}, f32[4,16,1536]{2,1,0:T(8,128)S(1)}, u32[]{:S(2)}, u32[]{:S(2)}) collective-permute-start(f32[4,16,1536]{2,1,0:T(8,128)S(1)} %get-tuple-element.130), channel_id=1, source_target_pairs={{0,16},{8,24},{16,17},{24,25},{1,0},{9,8},{17,18},{25,26},{2,1},{1... | collective-permute-start | bytes 1179656 | tf_op jit(solution)/shard_map/ppermute | solution.py:496
  17.4 11.4 %collective-permute-start.4 = (f32[99,8,128]{2,1,0:T(8,128)S(1)}, f32[99,8,128]{2,1,0:T(8,128)S(1)}, u32[]{:S(2)}, u32[]{:S(2)}) collective-permute-start(f32[99,8,128]{2,1,0:T(8,128)S(1)} %get-tuple-element.84), channel_id=1, source_target_pairs={{0,8},{8,0},{16,24},{24,16},{1,9},{9,1},{17,25},{25,17},{2,10},{10... | collective-permute-start | bytes 1216520 | tf_op jit(solution)/shard_map/cond/branch_0_fun/ppermute | solution.py:450
  19.4 20.8 %slice-start = ((s8[6291456]{0:T(1024)(128)(4,1)}), s8[4194304]{0:T(1024)(128)(4,1)S(1)}, s32[]{:S(2)}) async-start(s8[6291456]{0:T(1024)(128)(4,1)} %bitcast.4), calls=%async_computation | async-start | bytes 8388608 | tf_op jit(solution)/shard_map/cond
  19.4 20.8 %slice-start.1 = ((s8[6291456]{0:T(1024)(128)(4,1)}), s8[2097152]{0:T(1024)(128)(4,1)S(1)}, s32[]{:S(2)}) async-start(s8[6291456]{0:T(1024)(128)(4,1)} %bitcast.4), calls=%async_computation.1 | async-start | bytes 4194304 | tf_op jit(solution)/shard_map/cond
  19.4 20.8 %copy-start.1 = (f32[8,64,1536]{2,1,0:T(8,128)S(1)}, f32[8,64,1536]{2,1,0:T(8,128)}, u32[]{:S(2)}) copy-start(f32[8,64,1536]{2,1,0:T(8,128)} %get-tuple-element.88.moved_ref) | copy-start | bytes 9437188 | tf_op jit(solution)/shard_map/cond
  27.6 10.7 %collective-permute-start = (f32[99,8,128]{2,1,0:T(8,128)S(1)}, f32[99,8,128]{2,1,0:T(8,128)S(1)}, u32[]{:S(2)}, u32[]{:S(2)}) collective-permute-start(f32[99,8,128]{2,1,0:T(8,128)S(1)} %get-tuple-element.74), channel_id=1, source_target_pairs={{0,8},{8,0},{16,24},{24,16},{1,9},{9,1},{17,25},{25,17},{2,10},{10... | collective-permute-start | bytes 1216520 | tf_op jit(solution)/shard_map/cond/branch_0_fun/ppermute | solution.py:450
  28.9 11.3 %collective-permute-start.5 = (f32[99,8,128]{2,1,0:T(8,128)S(1)}, f32[99,8,128]{2,1,0:T(8,128)S(1)}, u32[]{:S(2)}, u32[]{:S(2)}) collective-permute-start(f32[99,8,128]{2,1,0:T(8,128)S(1)} %add.18.a_ref), channel_id=1, source_target_pairs={{0,16},{8,24},{16,0},{24,8},{1,17},{9,25},{17,1},{25,9},{2,18},{10... | collective-permute-start | bytes 1216520 | tf_op jit(solution)/shard_map/cond/branch_0_fun/ppermute | solution.py:450
  38.4 12.3 %collective-permute-start.1 = (f32[99,8,128]{2,1,0:T(8,128)S(1)}, f32[99,8,128]{2,1,0:T(8,128)S(1)}, u32[]{:S(2)}, u32[]{:S(2)}) collective-permute-start(f32[99,8,128]{2,1,0:T(8,128)S(1)} %add.16.a_ref), channel_id=1, source_target_pairs={{0,16},{8,24},{16,0},{24,8},{1,17},{9,25},{17,1},{25,9},{2,18},{10... | collective-permute-start | bytes 1216520 | tf_op jit(solution)/shard_map/cond/branch_0_fun/ppermute | solution.py:450
  49.0 11.0 %collective-permute-start.6 = (f32[94,8,128]{2,1,0:T(8,128)S(1)}, f32[94,8,128]{2,1,0:T(8,128)S(1)}, u32[]{:S(2)}, u32[]{:S(2)}) collective-permute-start(f32[94,8,128]{2,1,0:T(8,128)S(1)} %get-tuple-element.89), channel_id=1, source_target_pairs={{0,8},{8,0},{16,24},{24,16},{1,9},{9,1},{17,25},{25,17},{2,10},{10... | collective-permute-start | bytes 1155080 | tf_op jit(solution)/shard_map/cond/branch_0_fun/ppermute | solution.py:450
  59.5 9.4 %collective-permute-start.2 = (f32[94,8,128]{2,1,0:T(8,128)S(1)}, f32[94,8,128]{2,1,0:T(8,128)S(1)}, u32[]{:S(2)}, u32[]{:S(2)}) collective-permute-start(f32[94,8,128]{2,1,0:T(8,128)S(1)} %get-tuple-element.80), channel_id=1, source_target_pairs={{0,8},{8,0},{16,24},{24,16},{1,9},{9,1},{17,25},{25,17},{2,10},{10... | collective-permute-start | bytes 1155080 | tf_op jit(solution)/shard_map/cond/branch_0_fun/ppermute | solution.py:450
  60.0 11.0 %collective-permute-start.7 = (f32[94,8,128]{2,1,0:T(8,128)S(1)}, f32[94,8,128]{2,1,0:T(8,128)S(1)}, u32[]{:S(2)}, u32[]{:S(2)}) collective-permute-start(f32[94,8,128]{2,1,0:T(8,128)S(1)} %add.19.a_ref), channel_id=1, source_target_pairs={{0,16},{8,24},{16,0},{24,8},{1,17},{9,25},{17,1},{25,9},{2,18},{10... | collective-permute-start | bytes 1155080 | tf_op jit(solution)/shard_map/cond/branch_0_fun/ppermute | solution.py:450
  69.0 9.0 %collective-permute-start.3 = (f32[94,8,128]{2,1,0:T(8,128)S(1)}, f32[94,8,128]{2,1,0:T(8,128)S(1)}, u32[]{:S(2)}, u32[]{:S(2)}) collective-permute-start(f32[94,8,128]{2,1,0:T(8,128)S(1)} %add.17.a_ref), channel_id=1, source_target_pairs={{0,16},{8,24},{16,0},{24,8},{1,17},{9,25},{17,1},{25,9},{2,18},{10... | collective-permute-start | bytes 1155080 | tf_op jit(solution)/shard_map/cond/branch_0_fun/ppermute | solution.py:450

commit v4 on v3

--- a/solution.py
+++ b/solution.py
@@ -258,8 +258,10 @@
     lon = info_ref[0]
     ready = pltpu.make_async_copy(tables_ref.at[lon], table_ref, table_sem.at[0])
     later = pltpu.make_async_copy(backs_ref.at[lon], back_ref, table_sem.at[1])
-    loop(SUB, lambda level: every(level_copies(hbm_refs, buffers, sem, first, level), "start"))
+    half = SUB // 2
+    loop(half, lambda level: every(level_copies(hbm_refs, buffers, sem, first, level), "start"))
     ready.start()
+    loop(half, lambda level: every(level_copies(hbm_refs, buffers, sem, first, level + half), "start"))
     later.start()
     cut = cut_row_ref[...]
     kept_ref[0] = jnp.sum((cut >= 0).astype(jnp.int32) + (cut >= HALF).astype(jnp.int32))
@@ -403,7 +405,7 @@
         out_ref[level, rows - 1 : rows, :] = out_ref[level, rows - 1 : rows, :] + step_ref[1, row, :]
         place_ref[row, :] = outflow(out_ref[level, :, width - 128 :], cells, width)
 
-    loop(levels, one)
+    lax.fori_loop(0, levels, lambda i, _: (one(i), 0)[1], 0, unroll=2)
     project_groups(out_ref, table_ref, sum_ref)
     put_slots(pay_ref, 0, ways, lon, place_ref[...])
     pack_rows(cut_ref, sum_ref, ways, pay_ref)

time: 82.5 us -> 82.3 us (level)
  no operation moved by 1% of the time
where the time goes in v4:
time: 82.3 us; the launch traced here: 82.1 us
  Pallas kernels  46.4 us (56%)
  waiting for transfers between devices  19 us (23%)
  starting transfers between devices  14.5 us (18%)
  other arithmetic  0.96 us (1%)
  between operations  0.85 us (1%)
    pallas_call x8, Pallas kernels, call(): pl.pallas_call(kernel, in_specs=[spec for _, spec in inputs], out_specs=[...  46.4 us
    ppermute x8, waiting for transfers between devices, swap(): return lax.ppermute(x, 'lon', [(i, i ^ 1 << bit) for i in range(count)])  19 us
    ppermute x8, starting transfers between devices, swap(): return lax.ppermute(x, 'lon', [(i, i ^ 1 << bit) for i in range(count)])  11.4 us
    ppermute x1, starting transfers between devices, on_device(): got1 = lax.ppermute(ring1, ring, lat_ring(bands, ways, 1))  2.59 us
  transfers between devices with their start and end apart: 10, of which 5 were waited for; matrix products, arithmetic and copies ran while one was open for 0% of the time, Pallas kernels for 47%

profile of v4, /device:TPU:0, one launch (start us, length us, event | category | flops | bytes accessed | tf_op | source)
XLA Modules:
  0.0 82.1 jit_solution(16249382674789989013)
XLA Ops:
  0.0 0.7 compare_select_fusion
  0.7 0.1 pad_add_fusion.info_ref
  0.8 2.4 %shard_map.76 = (f32[4,16,1536]{2,1,0:T(8,128)S(1)}, f32[4,16,1536]{2,1,0:T(8,128)S(1)}, f32[2,16,1536]{2,1,0:T(8,128)S(1)}) custom-call(s32[4]{0:T(128)S(1)} %pad_add_fusion.info_ref, s32[1,64]{1,0:T(1,128)S(1)} %bitcast.8, f32[16,64,1440]{2,1,0:T(8,128)} %s_ref.3, f32[16,64,1440]{2,1,0:T(8,128)} %u_ref.3, f32[16,64,1440]{2,1,0:T(8,128)} %v_ref.3), custom_call_target="tpu_custom_call" | custom-call | tf_op jit(solution)/shard_map/pallas_call | solution.py:439
  3.2 0.5 collective-permute-start.16
  3.7 2.6 %collective-permute-start.17 = (f32[4,16,1536]{2,1,0:T(8,128)S(1)}, f32[4,16,1536]{2,1,0:T(8,128)S(1)}, u32[]{:S(2)}, u32[]{:S(2)}) collective-permute-start(f32[4,16,1536]{2,1,0:T(8,128)S(1)} %get-tuple-element.130), channel_id=1, source_target_pairs={{0,16},{8,24},{16,17},{24,25},{1,0},{9,8},{17,18},{25,26},{2,1},{1... | collective-permute-start | bytes 1179656 | tf_op jit(solution)/shard_map/ppermute | solution.py:498
  6.3 8.9 %shard_map.75 = (f32[8,64,1536]{2,1,0:T(8,128)}, f32[2,512,128]{2,1,0:T(8,128)S(1)}, f32[8,128]{1,0:T(8,128)S(1)}, bf16[1536,512]{1,0:T(8,128)(2,1)S(1)}, bf16[512,1536]{1,0:T(8,128)(2,1)S(1)}, /*index=5*/s32[1]{0:T(128)}) custom-call(s32[4]{0:T(128)S(1)} %pad_add_fusion.info_ref, s32[1,64]{1,0:T(1,128)S(1)} %bitcast.9, f32[16,64,1440]{2,1,0:T(8,128)} %s_ref.3, ...), custom_call_target="tpu_custom_call" | custom-call | tf_op jit(solution)/shard_map/pallas_call | solution.py:439
  15.8 0.0 collective-permute-done.16
  15.8 0.0 collective-permute-done.17
  15.9 66.1 %conditional.1 = (f32[16,64,1440]{2,1,0:T(8,128)}) conditional(s32[]{:T(128)} %bitcast.3, (s32[4]{0:T(128)S(1)}, s32[64]{0:T(128)S(1)}, f32[16,64,1440]{2,1,0:T(8,128)}, f32[16,64,1440]{2,1,0:T(8,128)S(1)}, f32[16,64,1440]{2,1,0:T(8,128)}, /*index=5*/f32[2,16,1536]{2,1,0:T(8,128)S(1)}, f32[4,16,1536]{2,1,0:T(8,128)S(1)}, ...), branch_computations={%region_0.1_spmd, %region_1.2_spmd} | conditional | flops 559104 | bytes 56058260 | solution.py:569
  15.9 1.5 %branch_0_fun.8 = (f32[4,8,1536]{2,1,0:T(8,128)S(1)}, f32[2,8,1536]{2,1,0:T(8,128)S(1)}, f32[2,8,128]{2,1,0:T(8,128)S(1)}, f32[99,8,128]{2,1,0:T(8,128)S(1)}) custom-call(s32[4]{0:T(128)S(1)} %get-tuple-element.64.info_ref, s32[64]{0:T(128)S(1)} %bitcast.12, f32[2,512,128]{2,1,0:T(8,128)S(1)} %get-tuple-element.82.coef_in_ref, ...), custom_call_target="tpu_custom_call" | custom-call | tf_op jit(solution)/shard_map/cond/branch_0_fun/pallas_call | solution.py:439
  17.4 2.0 %collective-permute-start.4 = (f32[99,8,128]{2,1,0:T(8,128)S(1)}, f32[99,8,128]{2,1,0:T(8,128)S(1)}, u32[]{:S(2)}, u32[]{:S(2)}) collective-permute-start(f32[99,8,128]{2,1,0:T(8,128)S(1)} %get-tuple-element.84), channel_id=1, source_target_pairs={{0,8},{8,0},{16,24},{24,16},{1,9},{9,1},{17,25},{25,17},{2,10},{10... | collective-permute-start | bytes 1216520 | tf_op jit(solution)/shard_map/cond/branch_0_fun/ppermute | solution.py:452
  19.4 8.2 %branch_0_fun.6 = (f32[8,64,1536]{2,1,0:T(8,128)S(1)}, f32[4,8,1536]{2,1,0:T(8,128)S(1)}, f32[2,8,1536]{2,1,0:T(8,128)S(1)}, f32[2,8,128]{2,1,0:T(8,128)S(1)}, f32[99,8,128]{2,1,0:T(8,128)S(1)}) custom-call(s32[4]{0:T(128)S(1)} %get-tuple-element.64.info_ref, s32[64]{0:T(128)S(1)} %bitcast.13, f32[16,64,1440]{2,1,0:T(8,128)} %get-tuple-element.67.s_ref, ...), custom_call_target="tpu_custom_call" | custom-call | tf_op jit(solution)/shard_map/cond/branch_0_fun/pallas_call | solution.py:439
  27.6 0.2 collective-permute-start
  27.8 1.1 %collective-permute-done.4 = f32[99,8,128]{2,1,0:T(8,128)S(1)} collective-permute-done((f32[99,8,128]{2,1,0:T(8,128)S(1)}, f32[99,8,128]{2,1,0:T(8,128)S(1)}, u32[]{:S(2)}, u32[]{:S(2)}) %collective-permute-start.4) | collective-permute-done | bytes 405536 | tf_op jit(solution)/shard_map/cond/branch_0_fun/ppermute | solution.py:452
  28.9 0.1 add.18.a_ref
  28.9 1.6 %collective-permute-start.5 = (f32[99,8,128]{2,1,0:T(8,128)S(1)}, f32[99,8,128]{2,1,0:T(8,128)S(1)}, u32[]{:S(2)}, u32[]{:S(2)}) collective-permute-start(f32[99,8,128]{2,1,0:T(8,128)S(1)} %add.18.a_ref), channel_id=1, source_target_pairs={{0,16},{8,24},{16,0},{24,8},{1,17},{9,25},{17,1},{25,9},{2,18},{10... | collective-permute-start | bytes 1216520 | tf_op jit(solution)/shard_map/cond/branch_0_fun/ppermute | solution.py:452
  30.6 7.8 %collective-permute-done = f32[99,8,128]{2,1,0:T(8,128)S(1)} collective-permute-done((f32[99,8,128]{2,1,0:T(8,128)S(1)}, f32[99,8,128]{2,1,0:T(8,128)S(1)}, u32[]{:S(2)}, u32[]{:S(2)}) %collective-permute-start) | collective-permute-done | bytes 405536 | tf_op jit(solution)/shard_map/cond/branch_0_fun/ppermute | solution.py:452
  38.4 0.1 add.16.a_ref
  38.4 1.6 %collective-permute-start.1 = (f32[99,8,128]{2,1,0:T(8,128)S(1)}, f32[99,8,128]{2,1,0:T(8,128)S(1)}, u32[]{:S(2)}, u32[]{:S(2)}) collective-permute-start(f32[99,8,128]{2,1,0:T(8,128)S(1)} %add.16.a_ref), channel_id=1, source_target_pairs={{0,16},{8,24},{16,0},{24,8},{1,17},{9,25},{17,1},{25,9},{2,18},{10... | collective-permute-start | bytes 1216520 | tf_op jit(solution)/shard_map/cond/branch_0_fun/ppermute | solution.py:452
  40.1 0.1 collective-permute-done.5.b_ref
  40.2 8.6 %branch_0_fun.9 = (f32[8,64,1536]{2,1,0:T(8,128)S(1)}, f32[94,8,128]{2,1,0:T(8,128)S(1)}) custom-call(s32[4]{0:T(128)S(1)} %get-tuple-element.64.info_ref, s32[64]{0:T(128)S(1)} %bitcast.14, s32[1,64]{1,0:T(1,128)S(1)} %get-tuple-element.66.cut_row_ref, f32[99,8,128]{2,1,0:T(8,128)S(1)} %add.18.a_ref, f32[99,8,128]{2,1,0:T(8,128)S(1)} %collective-permute-done.5.b_ref, ...), custom_call_target="tpu_custom_call" | custom-call | tf_op jit(solution)/shard_map/cond/branch_0_fun/pallas_call | solution.py:439
  48.9 1.7 %collective-permute-start.6 = (f32[94,8,128]{2,1,0:T(8,128)S(1)}, f32[94,8,128]{2,1,0:T(8,128)S(1)}, u32[]{:S(2)}, u32[]{:S(2)}) collective-permute-start(f32[94,8,128]{2,1,0:T(8,128)S(1)} %get-tuple-element.89), channel_id=1, source_target_pairs={{0,8},{8,0},{16,24},{24,16},{1,9},{9,1},{17,25},{25,17},{2,10},{10... | collective-permute-start | bytes 1155080 | tf_op jit(solution)/shard_map/cond/branch_0_fun/ppermute | solution.py:452
  50.5 8.7 %branch_0_fun.7 = (f32[8,64,1536]{2,1,0:T(8,128)S(1)}, f32[94,8,128]{2,1,0:T(8,128)S(1)}) custom-call(s32[4]{0:T(128)S(1)} %get-tuple-element.64.info_ref, s32[64]{0:T(128)S(1)} %bitcast.15, s32[1,64]{1,0:T(1,128)S(1)} %get-tuple-element.66.cut_row_ref, f32[99,8,128]{2,1,0:T(8,128)S(1)} %add.16.a_ref, f32[99,8,128]{2,1,0:T(8,128)S(1)} %collective-permute-done.1.b_ref, ...), custom_call_target="tpu_custom_call" | custom-call | tf_op jit(solution)/shard_map/cond/branch_0_fun/pallas_call | solution.py:439
  59.2 0.5 collective-permute-start.2
  59.7 0.0 collective-permute-done.6
  59.7 1.8 %collective-permute-start.7 = (f32[94,8,128]{2,1,0:T(8,128)S(1)}, f32[94,8,128]{2,1,0:T(8,128)S(1)}, u32[]{:S(2)}, u32[]{:S(2)}) collective-permute-start(f32[94,8,128]{2,1,0:T(8,128)S(1)} %add.19.a_ref), channel_id=1, source_target_pairs={{0,16},{8,24},{16,0},{24,8},{1,17},{9,25},{17,1},{25,9},{2,18},{10... | collective-permute-start | bytes 1155080 | tf_op jit(solution)/shard_map/cond/branch_0_fun/ppermute | solution.py:452
  61.5 7.1 %collective-permute-done.2 = f32[94,8,128]{2,1,0:T(8,128)S(1)} collective-permute-done((f32[94,8,128]{2,1,0:T(8,128)S(1)}, f32[94,8,128]{2,1,0:T(8,128)S(1)}, u32[]{:S(2)}, u32[]{:S(2)}) %collective-permute-start.2) | collective-permute-done | bytes 385056 | tf_op jit(solution)/shard_map/cond/branch_0_fun/ppermute | solution.py:452
  68.6 0.1 add.17.a_ref
  68.7 2.0 %collective-permute-start.3 = (f32[94,8,128]{2,1,0:T(8,128)S(1)}, f32[94,8,128]{2,1,0:T(8,128)S(1)}, u32[]{:S(2)}, u32[]{:S(2)}) collective-permute-start(f32[94,8,128]{2,1,0:T(8,128)S(1)} %add.17.a_ref), channel_id=1, source_target_pairs={{0,16},{8,24},{16,0},{24,8},{1,17},{9,25},{17,1},{25,9},{2,18},{10... | collective-permute-start | bytes 1155080 | tf_op jit(solution)/shard_map/cond/branch_0_fun/ppermute | solution.py:452
  70.7 4.0 %branch_0_fun.10.refs_0_ = f32[16,64,1440]{2,1,0:T(8,128)} custom-call(s32[4]{0:T(128)S(1)} %get-tuple-element.64.info_ref, s32[64]{0:T(128)S(1)} %bitcast.16, s32[1,64]{1,0:T(1,128)S(1)} %get-tuple-element.66.cut_row_ref, f32[94,8,128]{2,1,0:T(8,128)S(1)} %add.19.a_ref, f32[94,8,128]{2,1,0:T(8,128)S(1)} %collective-permute-done.7.b_ref, ...), custom_call_target="tpu_custom_call" | custom-call | tf_op jit(solution)/shard_map/cond/branch_0_fun/pallas_call | solution.py:439
  74.8 2.9 %collective-permute-done.3.b_ref = f32[94,8,128]{2,1,0:T(8,128)S(1)} collective-permute-done((f32[94,8,128]{2,1,0:T(8,128)S(1)}, f32[94,8,128]{2,1,0:T(8,128)S(1)}, u32[]{:S(2)}, u32[]{:S(2)}) %collective-permute-start.3) | collective-permute-done | bytes 385056 | tf_op jit(solution)/shard_map/cond/branch_0_fun/ppermute | solution.py:452
  77.7 4.0 %branch_0_fun.11 = f32[16,64,1440]{2,1,0:T(8,128)} custom-call(s32[4]{0:T(128)S(1)} %get-tuple-element.64.info_ref, s32[64]{0:T(128)S(1)} %bitcast.17, s32[1,64]{1,0:T(1,128)S(1)} %get-tuple-element.66.cut_row_ref, f32[94,8,128]{2,1,0:T(8,128)S(1)} %add.17.a_ref, f32[94,8,128]{2,1,0:T(8,128)S(1)} %collective-permute-done.3.b_ref, ...), custom_call_target="tpu_custom_call", output_to_operand_aliasing={{}: (7, {})} | custom-call | tf_op jit(solution)/shard_map/cond/branch_0_fun/pallas_call | solution.py:439
  (12 shorter events, 0.1 us)
Async XLA Ops:
  0.8 5.5 %copy-start = (f32[16,64,1440]{2,1,0:T(8,128)S(1)}, f32[16,64,1440]{2,1,0:T(8,128)}, u32[]{:S(2)}) copy-start(f32[16,64,1440]{2,1,0:T(8,128)} %u_ref.3) | copy-start | bytes 17694724
  3.2 12.7 %collective-permute-start.16 = (f32[4,16,1536]{2,1,0:T(8,128)S(1)}, f32[4,16,1536]{2,1,0:T(8,128)S(1)}, u32[]{:S(2)}, u32[]{:S(2)}) collective-permute-start(f32[4,16,1536]{2,1,0:T(8,128)S(1)} %get-tuple-element.129), channel_id=1, source_target_pairs={{0,1},{8,9},{16,0},{24,8},{1,2},{9,10},{17,16},{25,24},{2,3},{10,1... | collective-permute-start | bytes 1179656 | tf_op jit(solution)/shard_map/ppermute | solution.py:497
  3.7 12.2 %collective-permute-start.17 = (f32[4,16,1536]{2,1,0:T(8,128)S(1)}, f32[4,16,1536]{2,1,0:T(8,128)S(1)}, u32[]{:S(2)}, u32[]{:S(2)}) collective-permute-start(f32[4,16,1536]{2,1,0:T(8,128)S(1)} %get-tuple-element.130), channel_id=1, source_target_pairs={{0,16},{8,24},{16,17},{24,25},{1,0},{9,8},{17,18},{25,26},{2,1},{1... | collective-permute-start | bytes 1179656 | tf_op jit(solution)/shard_map/ppermute | solution.py:498
  17.4 11.5 %collective-permute-start.4 = (f32[99,8,128]{2,1,0:T(8,128)S(1)}, f32[99,8,128]{2,1,0:T(8,128)S(1)}, u32[]{:S(2)}, u32[]{:S(2)}) collective-permute-start(f32[99,8,128]{2,1,0:T(8,128)S(1)} %get-tuple-element.84), channel_id=1, source_target_pairs={{0,8},{8,0},{16,24},{24,16},{1,9},{9,1},{17,25},{25,17},{2,10},{10... | collective-permute-start | bytes 1216520 | tf_op jit(solution)/shard_map/cond/branch_0_fun/ppermute | solution.py:452
  19.4 20.8 %slice-start = ((s8[6291456]{0:T(1024)(128)(4,1)}), s8[4194304]{0:T(1024)(128)(4,1)S(1)}, s32[]{:S(2)}) async-start(s8[6291456]{0:T(1024)(128)(4,1)} %bitcast.4), calls=%async_computation | async-start | bytes 8388608 | tf_op jit(solution)/shard_map/cond
  19.4 20.8 %slice-start.1 = ((s8[6291456]{0:T(1024)(128)(4,1)}), s8[2097152]{0:T(1024)(128)(4,1)S(1)}, s32[]{:S(2)}) async-start(s8[6291456]{0:T(1024)(128)(4,1)} %bitcast.4), calls=%async_computation.1 | async-start | bytes 4194304 | tf_op jit(solution)/shard_map/cond
  19.4 20.8 %copy-start.1 = (f32[8,64,1536]{2,1,0:T(8,128)S(1)}, f32[8,64,1536]{2,1,0:T(8,128)}, u32[]{:S(2)}) copy-start(f32[8,64,1536]{2,1,0:T(8,128)} %get-tuple-element.88.moved_ref) | copy-start | bytes 9437188 | tf_op jit(solution)/shard_map/cond
  27.6 10.7 %collective-permute-start = (f32[99,8,128]{2,1,0:T(8,128)S(1)}, f32[99,8,128]{2,1,0:T(8,128)S(1)}, u32[]{:S(2)}, u32[]{:S(2)}) collective-permute-start(f32[99,8,128]{2,1,0:T(8,128)S(1)} %get-tuple-element.74), channel_id=1, source_target_pairs={{0,8},{8,0},{16,24},{24,16},{1,9},{9,1},{17,25},{25,17},{2,10},{10... | collective-permute-start | bytes 1216520 | tf_op jit(solution)/shard_map/cond/branch_0_fun/ppermute | solution.py:452
  28.9 11.2 %collective-permute-start.5 = (f32[99,8,128]{2,1,0:T(8,128)S(1)}, f32[99,8,128]{2,1,0:T(8,128)S(1)}, u32[]{:S(2)}, u32[]{:S(2)}) collective-permute-start(f32[99,8,128]{2,1,0:T(8,128)S(1)} %add.18.a_ref), channel_id=1, source_target_pairs={{0,16},{8,24},{16,0},{24,8},{1,17},{9,25},{17,1},{25,9},{2,18},{10... | collective-permute-start | bytes 1216520 | tf_op jit(solution)/shard_map/cond/branch_0_fun/ppermute | solution.py:452
  38.4 12.1 %collective-permute-start.1 = (f32[99,8,128]{2,1,0:T(8,128)S(1)}, f32[99,8,128]{2,1,0:T(8,128)S(1)}, u32[]{:S(2)}, u32[]{:S(2)}) collective-permute-start(f32[99,8,128]{2,1,0:T(8,128)S(1)} %add.16.a_ref), channel_id=1, source_target_pairs={{0,16},{8,24},{16,0},{24,8},{1,17},{9,25},{17,1},{25,9},{2,18},{10... | collective-permute-start | bytes 1216520 | tf_op jit(solution)/shard_map/cond/branch_0_fun/ppermute | solution.py:452
  48.9 10.8 %collective-permute-start.6 = (f32[94,8,128]{2,1,0:T(8,128)S(1)}, f32[94,8,128]{2,1,0:T(8,128)S(1)}, u32[]{:S(2)}, u32[]{:S(2)}) collective-permute-start(f32[94,8,128]{2,1,0:T(8,128)S(1)} %get-tuple-element.89), channel_id=1, source_target_pairs={{0,8},{8,0},{16,24},{24,16},{1,9},{9,1},{17,25},{25,17},{2,10},{10... | collective-permute-start | bytes 1155080 | tf_op jit(solution)/shard_map/cond/branch_0_fun/ppermute | solution.py:452
  59.2 9.4 %collective-permute-start.2 = (f32[94,8,128]{2,1,0:T(8,128)S(1)}, f32[94,8,128]{2,1,0:T(8,128)S(1)}, u32[]{:S(2)}, u32[]{:S(2)}) collective-permute-start(f32[94,8,128]{2,1,0:T(8,128)S(1)} %get-tuple-element.80), channel_id=1, source_target_pairs={{0,8},{8,0},{16,24},{24,16},{1,9},{9,1},{17,25},{25,17},{2,10},{10... | collective-permute-start | bytes 1155080 | tf_op jit(solution)/shard_map/cond/branch_0_fun/ppermute | solution.py:452
  59.7 11.0 %collective-permute-start.7 = (f32[94,8,128]{2,1,0:T(8,128)S(1)}, f32[94,8,128]{2,1,0:T(8,128)S(1)}, u32[]{:S(2)}, u32[]{:S(2)}) collective-permute-start(f32[94,8,128]{2,1,0:T(8,128)S(1)} %add.19.a_ref), channel_id=1, source_target_pairs={{0,16},{8,24},{16,0},{24,8},{1,17},{9,25},{17,1},{25,9},{2,18},{10... | collective-permute-start | bytes 1155080 | tf_op jit(solution)/shard_map/cond/branch_0_fun/ppermute | solution.py:452
  68.7 9.0 %collective-permute-start.3 = (f32[94,8,128]{2,1,0:T(8,128)S(1)}, f32[94,8,128]{2,1,0:T(8,128)S(1)}, u32[]{:S(2)}, u32[]{:S(2)}) collective-permute-start(f32[94,8,128]{2,1,0:T(8,128)S(1)} %add.17.a_ref), channel_id=1, source_target_pairs={{0,16},{8,24},{16,0},{24,8},{1,17},{9,25},{17,1},{25,9},{2,18},{10... | collective-permute-start | bytes 1155080 | tf_op jit(solution)/shard_map/cond/branch_0_fun/ppermute | solution.py:452

commit v5 on v3

--- a/solution.py
+++ b/solution.py
@@ -15,7 +15,7 @@
 GROUP = 4
 SUB = 8
 FIRST_MIB = 52
-LIMITS = (88, 128)
+LIMITS = (86, 128)
 F32 = jnp.float32
 BF16 = jnp.bfloat16
 MIB = 1024 * 1024

time: 82.5 us -> 82 us (level)
  transfers between devices with their start and end apart: 10 -> 10, of which waited for: 5 -> 4; matrix products, arithmetic and copies ran while one was open for 0% -> 0% of each run, Pallas kernels for 47% -> 47%
where the time goes in v5:
time: 82 us; the launch traced here: 81.9 us
  Pallas kernels  46.7 us (57%)
  waiting for transfers between devices  18.6 us (23%)
  starting transfers between devices  14.5 us (18%)
  other arithmetic  0.93 us (1%)
  between operations  0.85 us (1%)
    pallas_call x8, Pallas kernels, call(): pl.pallas_call(kernel, in_specs=[spec for _, spec in inputs], out_specs=[...  46.7 us
    ppermute x8, waiting for transfers between devices, swap(): return lax.ppermute(x, 'lon', [(i, i ^ 1 << bit) for i in range(count)])  18.6 us
    ppermute x8, starting transfers between devices, swap(): return lax.ppermute(x, 'lon', [(i, i ^ 1 << bit) for i in range(count)])  11.4 us
    ppermute x1, starting transfers between devices, on_device(): got1 = lax.ppermute(ring1, ring, lat_ring(bands, ways, 1))  2.59 us
  transfers between devices with their start and end apart: 10, of which 4 were waited for; matrix products, arithmetic and copies ran while one was open for 0% of the time, Pallas kernels for 47%

profile of v5, /device:TPU:0, one launch (start us, length us, event | category | flops | bytes accessed | tf_op | source)
XLA Modules:
  0.0 81.9 jit_solution(5641268527243921404)
XLA Ops:
  0.0 0.7 compare_select_fusion
  0.7 0.1 pad_add_fusion.info_ref
  0.8 2.4 %shard_map.76 = (f32[4,16,1536]{2,1,0:T(8,128)S(1)}, f32[4,16,1536]{2,1,0:T(8,128)S(1)}, f32[2,16,1536]{2,1,0:T(8,128)S(1)}) custom-call(s32[4]{0:T(128)S(1)} %pad_add_fusion.info_ref, s32[1,64]{1,0:T(1,128)S(1)} %bitcast.8, f32[16,64,1440]{2,1,0:T(8,128)} %s_ref.3, f32[16,64,1440]{2,1,0:T(8,128)} %u_ref.3, f32[16,64,1440]{2,1,0:T(8,128)} %v_ref.3), custom_call_target="tpu_custom_call" | custom-call | tf_op jit(solution)/shard_map/pallas_call | solution.py:437
  3.2 0.5 collective-permute-start.16
  3.7 2.6 %collective-permute-start.17 = (f32[4,16,1536]{2,1,0:T(8,128)S(1)}, f32[4,16,1536]{2,1,0:T(8,128)S(1)}, u32[]{:S(2)}, u32[]{:S(2)}) collective-permute-start(f32[4,16,1536]{2,1,0:T(8,128)S(1)} %get-tuple-element.130), channel_id=1, source_target_pairs={{0,16},{8,24},{16,17},{24,25},{1,0},{9,8},{17,18},{25,26},{2,1},{1... | collective-permute-start | bytes 1179656 | tf_op jit(solution)/shard_map/ppermute | solution.py:496
  6.3 8.9 %shard_map.75 = (f32[8,64,1536]{2,1,0:T(8,128)}, f32[2,512,128]{2,1,0:T(8,128)S(1)}, f32[8,128]{1,0:T(8,128)S(1)}, bf16[1536,512]{1,0:T(8,128)(2,1)S(1)}, bf16[512,1536]{1,0:T(8,128)(2,1)S(1)}, /*index=5*/s32[1]{0:T(128)}) custom-call(s32[4]{0:T(128)S(1)} %pad_add_fusion.info_ref, s32[1,64]{1,0:T(1,128)S(1)} %bitcast.9, f32[16,64,1440]{2,1,0:T(8,128)} %s_ref.3, ...), custom_call_target="tpu_custom_call" | custom-call | tf_op jit(solution)/shard_map/pallas_call | solution.py:437
  15.8 0.0 collective-permute-done.16
  15.9 0.0 collective-permute-done.17
  15.9 65.8 %conditional.1 = (f32[16,64,1440]{2,1,0:T(8,128)}) conditional(s32[]{:T(128)} %bitcast.3, (s32[4]{0:T(128)S(1)}, s32[64]{0:T(128)S(1)}, f32[16,64,1440]{2,1,0:T(8,128)}, f32[16,64,1440]{2,1,0:T(8,128)S(1)}, f32[16,64,1440]{2,1,0:T(8,128)}, /*index=5*/f32[2,16,1536]{2,1,0:T(8,128)S(1)}, f32[4,16,1536]{2,1,0:T(8,128)S(1)}, ...), branch_computations={%region_0.1_spmd, %region_1.2_spmd} | conditional | flops 559104 | bytes 56058260 | solution.py:567
  15.9 1.5 %branch_0_fun.8 = (f32[4,8,1536]{2,1,0:T(8,128)S(1)}, f32[2,8,1536]{2,1,0:T(8,128)S(1)}, f32[2,8,128]{2,1,0:T(8,128)S(1)}, f32[97,8,128]{2,1,0:T(8,128)S(1)}) custom-call(s32[4]{0:T(128)S(1)} %get-tuple-element.64.info_ref, s32[64]{0:T(128)S(1)} %bitcast.12, f32[2,512,128]{2,1,0:T(8,128)S(1)} %get-tuple-element.82.coef_in_ref, ...), custom_call_target="tpu_custom_call" | custom-call | tf_op jit(solution)/shard_map/cond/branch_0_fun/pallas_call | solution.py:437
  17.4 2.0 %collective-permute-start.4 = (f32[97,8,128]{2,1,0:T(8,128)S(1)}, f32[97,8,128]{2,1,0:T(8,128)S(1)}, u32[]{:S(2)}, u32[]{:S(2)}) collective-permute-start(f32[97,8,128]{2,1,0:T(8,128)S(1)} %get-tuple-element.84), channel_id=1, source_target_pairs={{0,8},{8,0},{16,24},{24,16},{1,9},{9,1},{17,25},{25,17},{2,10},{10... | collective-permute-start | bytes 1191944 | tf_op jit(solution)/shard_map/cond/branch_0_fun/ppermute | solution.py:450
  19.4 8.2 %branch_0_fun.6 = (f32[8,64,1536]{2,1,0:T(8,128)S(1)}, f32[4,8,1536]{2,1,0:T(8,128)S(1)}, f32[2,8,1536]{2,1,0:T(8,128)S(1)}, f32[2,8,128]{2,1,0:T(8,128)S(1)}, f32[97,8,128]{2,1,0:T(8,128)S(1)}) custom-call(s32[4]{0:T(128)S(1)} %get-tuple-element.64.info_ref, s32[64]{0:T(128)S(1)} %bitcast.13, f32[16,64,1440]{2,1,0:T(8,128)} %get-tuple-element.67.s_ref, ...), custom_call_target="tpu_custom_call" | custom-call | tf_op jit(solution)/shard_map/cond/branch_0_fun/pallas_call | solution.py:437
  27.6 0.2 collective-permute-start
  27.8 0.9 %collective-permute-done.4 = f32[97,8,128]{2,1,0:T(8,128)S(1)} collective-permute-done((f32[97,8,128]{2,1,0:T(8,128)S(1)}, f32[97,8,128]{2,1,0:T(8,128)S(1)}, u32[]{:S(2)}, u32[]{:S(2)}) %collective-permute-start.4) | collective-permute-done | bytes 397344 | tf_op jit(solution)/shard_map/cond/branch_0_fun/ppermute | solution.py:450
  28.7 0.1 add.18.a_ref
  28.8 1.7 %collective-permute-start.5 = (f32[97,8,128]{2,1,0:T(8,128)S(1)}, f32[97,8,128]{2,1,0:T(8,128)S(1)}, u32[]{:S(2)}, u32[]{:S(2)}) collective-permute-start(f32[97,8,128]{2,1,0:T(8,128)S(1)} %add.18.a_ref), channel_id=1, source_target_pairs={{0,16},{8,24},{16,0},{24,8},{1,17},{9,25},{17,1},{25,9},{2,18},{10... | collective-permute-start | bytes 1191944 | tf_op jit(solution)/shard_map/cond/branch_0_fun/ppermute | solution.py:450
  30.4 7.8 %collective-permute-done = f32[97,8,128]{2,1,0:T(8,128)S(1)} collective-permute-done((f32[97,8,128]{2,1,0:T(8,128)S(1)}, f32[97,8,128]{2,1,0:T(8,128)S(1)}, u32[]{:S(2)}, u32[]{:S(2)}) %collective-permute-start) | collective-permute-done | bytes 397344 | tf_op jit(solution)/shard_map/cond/branch_0_fun/ppermute | solution.py:450
  38.2 1.6 %collective-permute-start.1 = (f32[97,8,128]{2,1,0:T(8,128)S(1)}, f32[97,8,128]{2,1,0:T(8,128)S(1)}, u32[]{:S(2)}, u32[]{:S(2)}) collective-permute-start(f32[97,8,128]{2,1,0:T(8,128)S(1)} %add.16.a_ref), channel_id=1, source_target_pairs={{0,16},{8,24},{16,0},{24,8},{1,17},{9,25},{17,1},{25,9},{2,18},{10... | collective-permute-start | bytes 1191944 | tf_op jit(solution)/shard_map/cond/branch_0_fun/ppermute | solution.py:450
  39.9 0.0 collective-permute-done.5.b_ref
  39.9 8.8 %branch_0_fun.9 = (f32[8,64,1536]{2,1,0:T(8,128)S(1)}, f32[92,8,128]{2,1,0:T(8,128)S(1)}) custom-call(s32[4]{0:T(128)S(1)} %get-tuple-element.64.info_ref, s32[64]{0:T(128)S(1)} %bitcast.14, s32[1,64]{1,0:T(1,128)S(1)} %get-tuple-element.66.cut_row_ref, f32[97,8,128]{2,1,0:T(8,128)S(1)} %add.18.a_ref, f32[97,8,128]{2,1,0:T(8,128)S(1)} %collective-permute-done.5.b_ref, ...), custom_call_target="tpu_custom_call" | custom-call | tf_op jit(solution)/shard_map/cond/branch_0_fun/pallas_call | solution.py:437
  48.7 1.7 %collective-permute-start.6 = (f32[92,8,128]{2,1,0:T(8,128)S(1)}, f32[92,8,128]{2,1,0:T(8,128)S(1)}, u32[]{:S(2)}, u32[]{:S(2)}) collective-permute-start(f32[92,8,128]{2,1,0:T(8,128)S(1)} %get-tuple-element.89), channel_id=1, source_target_pairs={{0,8},{8,0},{16,24},{24,16},{1,9},{9,1},{17,25},{25,17},{2,10},{10... | collective-permute-start | bytes 1130504 | tf_op jit(solution)/shard_map/cond/branch_0_fun/ppermute | solution.py:450
  50.4 0.0 collective-permute-done.1.b_ref
  50.4 8.8 %branch_0_fun.7 = (f32[8,64,1536]{2,1,0:T(8,128)S(1)}, f32[92,8,128]{2,1,0:T(8,128)S(1)}) custom-call(s32[4]{0:T(128)S(1)} %get-tuple-element.64.info_ref, s32[64]{0:T(128)S(1)} %bitcast.15, s32[1,64]{1,0:T(1,128)S(1)} %get-tuple-element.66.cut_row_ref, f32[97,8,128]{2,1,0:T(8,128)S(1)} %add.16.a_ref, f32[97,8,128]{2,1,0:T(8,128)S(1)} %collective-permute-done.1.b_ref, ...), custom_call_target="tpu_custom_call" | custom-call | tf_op jit(solution)/shard_map/cond/branch_0_fun/pallas_call | solution.py:437
  59.2 0.5 collective-permute-start.2
  59.7 0.0 collective-permute-done.6
  59.7 1.8 %collective-permute-start.7 = (f32[92,8,128]{2,1,0:T(8,128)S(1)}, f32[92,8,128]{2,1,0:T(8,128)S(1)}, u32[]{:S(2)}, u32[]{:S(2)}) collective-permute-start(f32[92,8,128]{2,1,0:T(8,128)S(1)} %add.19.a_ref), channel_id=1, source_target_pairs={{0,16},{8,24},{16,0},{24,8},{1,17},{9,25},{17,1},{25,9},{2,18},{10... | collective-permute-start | bytes 1130504 | tf_op jit(solution)/shard_map/cond/branch_0_fun/ppermute | solution.py:450
  61.5 7.0 %collective-permute-done.2 = f32[92,8,128]{2,1,0:T(8,128)S(1)} collective-permute-done((f32[92,8,128]{2,1,0:T(8,128)S(1)}, f32[92,8,128]{2,1,0:T(8,128)S(1)}, u32[]{:S(2)}, u32[]{:S(2)}) %collective-permute-start.2) | collective-permute-done | bytes 376864 | tf_op jit(solution)/shard_map/cond/branch_0_fun/ppermute | solution.py:450
  68.5 2.0 %collective-permute-start.3 = (f32[92,8,128]{2,1,0:T(8,128)S(1)}, f32[92,8,128]{2,1,0:T(8,128)S(1)}, u32[]{:S(2)}, u32[]{:S(2)}) collective-permute-start(f32[92,8,128]{2,1,0:T(8,128)S(1)} %add.17.a_ref), channel_id=1, source_target_pairs={{0,16},{8,24},{16,0},{24,8},{1,17},{9,25},{17,1},{25,9},{2,18},{10... | collective-permute-start | bytes 1130504 | tf_op jit(solution)/shard_map/cond/branch_0_fun/ppermute | solution.py:450
  70.6 0.0 collective-permute-done.7.b_ref
  70.6 4.0 %branch_0_fun.10.refs_0_ = f32[16,64,1440]{2,1,0:T(8,128)} custom-call(s32[4]{0:T(128)S(1)} %get-tuple-element.64.info_ref, s32[64]{0:T(128)S(1)} %bitcast.16, s32[1,64]{1,0:T(1,128)S(1)} %get-tuple-element.66.cut_row_ref, f32[92,8,128]{2,1,0:T(8,128)S(1)} %add.19.a_ref, f32[92,8,128]{2,1,0:T(8,128)S(1)} %collective-permute-done.7.b_ref, ...), custom_call_target="tpu_custom_call" | custom-call | tf_op jit(solution)/shard_map/cond/branch_0_fun/pallas_call | solution.py:437
  74.6 2.9 %collective-permute-done.3.b_ref = f32[92,8,128]{2,1,0:T(8,128)S(1)} collective-permute-done((f32[92,8,128]{2,1,0:T(8,128)S(1)}, f32[92,8,128]{2,1,0:T(8,128)S(1)}, u32[]{:S(2)}, u32[]{:S(2)}) %collective-permute-start.3) | collective-permute-done | bytes 376864 | tf_op jit(solution)/shard_map/cond/branch_0_fun/ppermute | solution.py:450
  77.5 4.0 %branch_0_fun.11 = f32[16,64,1440]{2,1,0:T(8,128)} custom-call(s32[4]{0:T(128)S(1)} %get-tuple-element.64.info_ref, s32[64]{0:T(128)S(1)} %bitcast.17, s32[1,64]{1,0:T(1,128)S(1)} %get-tuple-element.66.cut_row_ref, f32[92,8,128]{2,1,0:T(8,128)S(1)} %add.17.a_ref, f32[92,8,128]{2,1,0:T(8,128)S(1)} %collective-permute-done.3.b_ref, ...), custom_call_target="tpu_custom_call", output_to_operand_aliasing={{}: (7, {})} | custom-call | tf_op jit(solution)/shard_map/cond/branch_0_fun/pallas_call | solution.py:437
  (12 shorter events, 0.1 us)
Async XLA Ops:
  0.8 5.5 %copy-start = (f32[16,64,1440]{2,1,0:T(8,128)S(1)}, f32[16,64,1440]{2,1,0:T(8,128)}, u32[]{:S(2)}) copy-start(f32[16,64,1440]{2,1,0:T(8,128)} %u_ref.3) | copy-start | bytes 17694724
  3.2 12.7 %collective-permute-start.16 = (f32[4,16,1536]{2,1,0:T(8,128)S(1)}, f32[4,16,1536]{2,1,0:T(8,128)S(1)}, u32[]{:S(2)}, u32[]{:S(2)}) collective-permute-start(f32[4,16,1536]{2,1,0:T(8,128)S(1)} %get-tuple-element.129), channel_id=1, source_target_pairs={{0,1},{8,9},{16,0},{24,8},{1,2},{9,10},{17,16},{25,24},{2,3},{10,1... | collective-permute-start | bytes 1179656 | tf_op jit(solution)/shard_map/ppermute | solution.py:495
  3.7 12.2 %collective-permute-start.17 = (f32[4,16,1536]{2,1,0:T(8,128)S(1)}, f32[4,16,1536]{2,1,0:T(8,128)S(1)}, u32[]{:S(2)}, u32[]{:S(2)}) collective-permute-start(f32[4,16,1536]{2,1,0:T(8,128)S(1)} %get-tuple-element.130), channel_id=1, source_target_pairs={{0,16},{8,24},{16,17},{24,25},{1,0},{9,8},{17,18},{25,26},{2,1},{1... | collective-permute-start | bytes 1179656 | tf_op jit(solution)/shard_map/ppermute | solution.py:496
  17.4 11.3 %collective-permute-start.4 = (f32[97,8,128]{2,1,0:T(8,128)S(1)}, f32[97,8,128]{2,1,0:T(8,128)S(1)}, u32[]{:S(2)}, u32[]{:S(2)}) collective-permute-start(f32[97,8,128]{2,1,0:T(8,128)S(1)} %get-tuple-element.84), channel_id=1, source_target_pairs={{0,8},{8,0},{16,24},{24,16},{1,9},{9,1},{17,25},{25,17},{2,10},{10... | collective-permute-start | bytes 1191944 | tf_op jit(solution)/shard_map/cond/branch_0_fun/ppermute | solution.py:450
  19.4 20.5 %slice-start = ((s8[6291456]{0:T(1024)(128)(4,1)}), s8[4194304]{0:T(1024)(128)(4,1)S(1)}, s32[]{:S(2)}) async-start(s8[6291456]{0:T(1024)(128)(4,1)} %bitcast.4), calls=%async_computation | async-start | bytes 8388608 | tf_op jit(solution)/shard_map/cond
  19.4 20.5 %slice-start.1 = ((s8[6291456]{0:T(1024)(128)(4,1)}), s8[2097152]{0:T(1024)(128)(4,1)S(1)}, s32[]{:S(2)}) async-start(s8[6291456]{0:T(1024)(128)(4,1)} %bitcast.4), calls=%async_computation.1 | async-start | bytes 4194304 | tf_op jit(solution)/shard_map/cond
  19.4 20.5 %copy-start.1 = (f32[8,64,1536]{2,1,0:T(8,128)S(1)}, f32[8,64,1536]{2,1,0:T(8,128)}, u32[]{:S(2)}) copy-start(f32[8,64,1536]{2,1,0:T(8,128)} %get-tuple-element.88.moved_ref) | copy-start | bytes 9437188 | tf_op jit(solution)/shard_map/cond
  27.6 10.6 %collective-permute-start = (f32[97,8,128]{2,1,0:T(8,128)S(1)}, f32[97,8,128]{2,1,0:T(8,128)S(1)}, u32[]{:S(2)}, u32[]{:S(2)}) collective-permute-start(f32[97,8,128]{2,1,0:T(8,128)S(1)} %get-tuple-element.74), channel_id=1, source_target_pairs={{0,8},{8,0},{16,24},{24,16},{1,9},{9,1},{17,25},{25,17},{2,10},{10... | collective-permute-start | bytes 1191944 | tf_op jit(solution)/shard_map/cond/branch_0_fun/ppermute | solution.py:450
  28.8 11.1 %collective-permute-start.5 = (f32[97,8,128]{2,1,0:T(8,128)S(1)}, f32[97,8,128]{2,1,0:T(8,128)S(1)}, u32[]{:S(2)}, u32[]{:S(2)}) collective-permute-start(f32[97,8,128]{2,1,0:T(8,128)S(1)} %add.18.a_ref), channel_id=1, source_target_pairs={{0,16},{8,24},{16,0},{24,8},{1,17},{9,25},{17,1},{25,9},{2,18},{10... | collective-permute-start | bytes 1191944 | tf_op jit(solution)/shard_map/cond/branch_0_fun/ppermute | solution.py:450
  38.2 12.2 %collective-permute-start.1 = (f32[97,8,128]{2,1,0:T(8,128)S(1)}, f32[97,8,128]{2,1,0:T(8,128)S(1)}, u32[]{:S(2)}, u32[]{:S(2)}) collective-permute-start(f32[97,8,128]{2,1,0:T(8,128)S(1)} %add.16.a_ref), channel_id=1, source_target_pairs={{0,16},{8,24},{16,0},{24,8},{1,17},{9,25},{17,1},{25,9},{2,18},{10... | collective-permute-start | bytes 1191944 | tf_op jit(solution)/shard_map/cond/branch_0_fun/ppermute | solution.py:450
  48.7 11.0 %collective-permute-start.6 = (f32[92,8,128]{2,1,0:T(8,128)S(1)}, f32[92,8,128]{2,1,0:T(8,128)S(1)}, u32[]{:S(2)}, u32[]{:S(2)}) collective-permute-start(f32[92,8,128]{2,1,0:T(8,128)S(1)} %get-tuple-element.89), channel_id=1, source_target_pairs={{0,8},{8,0},{16,24},{24,16},{1,9},{9,1},{17,25},{25,17},{2,10},{10... | collective-permute-start | bytes 1130504 | tf_op jit(solution)/shard_map/cond/branch_0_fun/ppermute | solution.py:450
  59.2 9.3 %collective-permute-start.2 = (f32[92,8,128]{2,1,0:T(8,128)S(1)}, f32[92,8,128]{2,1,0:T(8,128)S(1)}, u32[]{:S(2)}, u32[]{:S(2)}) collective-permute-start(f32[92,8,128]{2,1,0:T(8,128)S(1)} %get-tuple-element.80), channel_id=1, source_target_pairs={{0,8},{8,0},{16,24},{24,16},{1,9},{9,1},{17,25},{25,17},{2,10},{10... | collective-permute-start | bytes 1130504 | tf_op jit(solution)/shard_map/cond/branch_0_fun/ppermute | solution.py:450
  59.7 10.8 %collective-permute-start.7 = (f32[92,8,128]{2,1,0:T(8,128)S(1)}, f32[92,8,128]{2,1,0:T(8,128)S(1)}, u32[]{:S(2)}, u32[]{:S(2)}) collective-permute-start(f32[92,8,128]{2,1,0:T(8,128)S(1)} %add.19.a_ref), channel_id=1, source_target_pairs={{0,16},{8,24},{16,0},{24,8},{1,17},{9,25},{17,1},{25,9},{2,18},{10... | collective-permute-start | bytes 1130504 | tf_op jit(solution)/shard_map/cond/branch_0_fun/ppermute | solution.py:450
  68.5 8.9 %collective-permute-start.3 = (f32[92,8,128]{2,1,0:T(8,128)S(1)}, f32[92,8,128]{2,1,0:T(8,128)S(1)}, u32[]{:S(2)}, u32[]{:S(2)}) collective-permute-start(f32[92,8,128]{2,1,0:T(8,128)S(1)} %add.17.a_ref), channel_id=1, source_target_pairs={{0,16},{8,24},{16,0},{24,8},{1,17},{9,25},{17,1},{25,9},{2,18},{10... | collective-permute-start | bytes 1130504 | tf_op jit(solution)/shard_map/cond/branch_0_fun/ppermute | solution.py:450
